TPU v7x, 32 devices: a whole 2x2x4 slice. The times are simulated.
32 devices in a mesh: dp: 16 (over z, y, x), tensor: 2 (over core).
Axes of the slice: x: 2, y: 2, z: 4, core: 2. Of those that a mesh axis runs over, the one named last changes fastest.
Arguments:
- layer_input: bfloat16 [16, 1024, 768], P('dp', 'tensor'), may hold values from -6 to 6
- seq_lengths: int32 [16], P('dp'), may hold values from 576 to 1024, as said below
- expert_routes: int32 [16, 1024, 2], P('dp'), may hold values from 0 to 7, all different within a row; in each aligned block of 1024 rows (0 to 1023, 1024 to 2047, ..., all dimensions but the last counted through in order) at most 512 rows name the same one
- w_query: float32 [768, 768], P('dp', 'tensor'), may hold values from -0.21875 to 0.21875
- w_key: float32 [768, 768], P('dp', 'tensor'), may hold values from -0.21875 to 0.21875
- w_value: float32 [768, 768], P('dp', 'tensor'), may hold values from -0.21875 to 0.21875
- w_output: float32 [768, 768], P('dp', 'tensor'), may hold values from -3.5 to 3.5
- gain_attn: float32 [768], P('dp'), may hold values from 0.1 to 1.9
- gain_ffn: float32 [768], P('dp'), may hold values from 0.1 to 1.9
- router_weight: float32 [768, 8], P('dp'), may hold values from -0.15625 to 0.15625
- expert_gate: float32 [768, 8, 2048], P('dp', None, 'tensor'), may hold values from -0.21875 to 0.21875
- expert_up: float32 [768, 8, 2048], P('dp', None, 'tensor'), may hold values from -0.21875 to 0.21875
- expert_down: float32 [768, 8, 2048], P('dp', None, 'tensor'), may hold values from -0.125 to 0.125
- shared_gate: float32 [768, 2048], P('dp', 'tensor'), may hold values from -0.21875 to 0.21875
- shared_up: float32 [768, 2048], P('dp', 'tensor'), may hold values from -0.21875 to 0.21875
- shared_down: float32 [768, 2048], P('dp', 'tensor'), may hold values from -0.125 to 0.125
- out_cotangent: bfloat16 [16, 1024, 768], P('dp', 'tensor'), may hold values from -6 to 6
Outputs:
- layer_output: bfloat16 [16, 1024, 768], P('dp', 'tensor')
- grad_input: bfloat16 [16, 1024, 768], P('dp', 'tensor')
- grad_query: float32 [768, 768], P('dp', 'tensor')
- grad_key: float32 [768, 768], P('dp', 'tensor')
- grad_value: float32 [768, 768], P('dp', 'tensor')
- grad_output_proj: float32 [768, 768], P('dp', 'tensor')
- grad_gain_attn: float32 [768], P('dp')
- grad_gain_ffn: float32 [768], P('dp')
- grad_router: float32 [768, 8], P('dp')
- grad_expert_gate: float32 [768, 8, 2048], P('dp', None, 'tensor')
- grad_expert_up: float32 [768, 8, 2048], P('dp', None, 'tensor')
- grad_expert_down: float32 [768, 8, 2048], P('dp', None, 'tensor')
- grad_shared_gate: float32 [768, 2048], P('dp', 'tensor')
- grad_shared_up: float32 [768, 2048], P('dp', 'tensor')
- grad_shared_down: float32 [768, 2048], P('dp', 'tensor')
Inputs may be any that keep to these rules, and one draw needn't show every extreme that they name: `seq_lengths`: every sequence has more than half of its 1024 slots valid, and in every draw some sequence fills all 1024. `expert_routes`: A token's two experts differ. Among the 1024 tokens of one dp group no expert is named more than 512 times, and in some group an expert is named exactly 512 times.
All inputs are finite; a program needn't handle non-finite values.
Results may differ from a plain program's by a relative error of at most 0.017.
The roundings to bfloat16 on the way count: a program that leaves them out, or rounds other values in their place, can miss the bound.
Values may be sent and summed in bfloat16 or wider, within the bound.
A program may use at most 320 MiB of HBM per device.

v0:
```python
import math

import jax
import jax.numpy as jnp
from jax import lax
from jax.sharding import PartitionSpec as P

HD = 64


epsilon = 1e-06
highest = lax.Precision.HIGHEST


def apply_rms_norm(values, gain_row):
    factor = lax.rsqrt(jnp.mean(values * values, axis=-1, keepdims=True) + epsilon)
    normed = values * factor
    return (normed * gain_row, normed, factor)


def norm_backward_pass(grad_rows, normed, factor, gain_row):
    grad_hat = grad_rows * gain_row
    grad_vals = factor * (grad_hat - normed * jnp.mean(grad_hat * normed, axis=-1, keepdims=True))
    return (grad_vals, jnp.sum(grad_rows * normed, axis=(0, 1)))


def rope_tables(length, half_size):
    places = jnp.arange(length, dtype=jnp.float32)[:, None]
    inverse = jnp.exp(jnp.arange(half_size, dtype=jnp.float32) * (-math.log(10000.0) / half_size))
    angles = places * inverse[None, :]
    return (jnp.cos(angles), jnp.sin(angles))


def rotate(values, cosine, sine_table):
    half_size = values.shape[-1] // 2
    first_half = values[..., :half_size]
    second = values[..., half_size:]
    cos_b = cosine[:, None, :]
    sin_b = sine_table[:, None, :]
    return jnp.concatenate(
        [first_half * cos_b - second * sin_b, second * cos_b + first_half * sin_b], axis=-1
    )


def unrotate(grad_rows, cosine, sine_table):
    half_size = grad_rows.shape[-1] // 2
    first_half = grad_rows[..., :half_size]
    second = grad_rows[..., half_size:]
    cos_b = cosine[:, None, :]
    sin_b = sine_table[:, None, :]
    return jnp.concatenate(
        [first_half * cos_b + second * sin_b, second * cos_b - first_half * sin_b], axis=-1
    )


def block_scores(query_block, key_rot, row_start, length, score_scale):
    seq_span = key_rot.shape[0]
    block_rows = query_block.shape[0]
    scores = (
        jnp.einsum("qhd,khd->hqk", query_block, key_rot, preferred_element_type=jnp.float32)
        * score_scale
    )
    row_pos = row_start + jnp.arange(block_rows)[:, None]
    column = jnp.arange(seq_span)[None, :]
    allowed = (column <= row_pos) & (column < length)
    return jnp.where(allowed[None], scores, -1e30)


def attend_forward(query_rot, key_rot, value_rows, length, score_scale):
    seq_span = query_rot.shape[0]
    block_rows = min(seq_span, 512)
    block_count = seq_span // block_rows

    def one_block(block_index):
        row_start = block_index * block_rows
        query_block = lax.dynamic_slice_in_dim(query_rot, row_start, block_rows, 0)
        masked = block_scores(query_block, key_rot, row_start, length, score_scale)
        row_peak = jnp.max(masked, axis=-1, keepdims=True)
        exp_rows = jnp.exp(masked - row_peak)
        exp_total = jnp.sum(exp_rows, axis=-1, keepdims=True)
        prob_rows = (exp_rows / exp_total).astype(jnp.bfloat16)
        context = jnp.einsum(
            "hqk,khd->qhd", prob_rows, value_rows, preferred_element_type=jnp.float32
        )
        return (context.astype(jnp.bfloat16), (row_peak + jnp.log(exp_total))[..., 0])

    contexts, log_total = lax.map(one_block, jnp.arange(block_count))
    return (contexts.reshape(seq_span, query_rot.shape[1], query_rot.shape[2]), log_total)


def attend_backward(query_rot, key_rot, value_rows, length, log_total, grad_context, score_scale):
    seq_span = query_rot.shape[0]
    block_rows = min(seq_span, 512)
    block_count = seq_span // block_rows

    def one_block(running, block_index):
        key_grad, value_grad = running
        row_start = block_index * block_rows
        query_block = lax.dynamic_slice_in_dim(query_rot, row_start, block_rows, 0)
        grad_block = lax.dynamic_slice_in_dim(grad_context, row_start, block_rows, 0)
        masked = block_scores(query_block, key_rot, row_start, length, score_scale)
        prob_rows = jnp.exp(masked - log_total[block_index][..., None])
        grad_probs = jnp.einsum(
            "qhd,khd->hqk", grad_block, value_rows, preferred_element_type=jnp.float32
        )
        row_inner = jnp.sum(grad_probs * prob_rows, axis=-1, keepdims=True)
        grad_scores = (prob_rows * (grad_probs - row_inner)).astype(jnp.bfloat16)
        query_grad = (
            jnp.einsum("hqk,khd->qhd", grad_scores, key_rot, preferred_element_type=jnp.float32)
            * score_scale
        )
        key_grad = (
            key_grad
            + jnp.einsum(
                "hqk,qhd->khd", grad_scores, query_block, preferred_element_type=jnp.float32
            )
            * score_scale
        )
        value_grad = value_grad + jnp.einsum(
            "hqk,qhd->khd",
            prob_rows.astype(jnp.bfloat16),
            grad_block,
            preferred_element_type=jnp.float32,
        )
        return ((key_grad, value_grad), query_grad)

    zeros_rows = jnp.zeros(key_rot.shape, jnp.float32)
    (key_grad, value_grad), query_grads = lax.scan(
        one_block, (zeros_rows, zeros_rows), jnp.arange(block_count)
    )
    return (query_grads.reshape(key_rot.shape), key_grad, value_grad)


def fetch_weights(masters):
    (
        w_query,
        w_key,
        w_value,
        w_output,
        gain_attn,
        gain_ffn,
        router_weight,
        expert_gate,
        expert_up,
        expert_down,
        shared_gate,
        shared_up,
        shared_down,
    ) = masters
    small_set = (
        lax.all_gather(w_query.astype(jnp.bfloat16), "dp", axis=0, tiled=True),
        lax.all_gather(w_key.astype(jnp.bfloat16), "dp", axis=0, tiled=True),
        lax.all_gather(w_value.astype(jnp.bfloat16), "dp", axis=0, tiled=True),
        lax.all_gather(w_output.astype(jnp.bfloat16), "dp", axis=0, tiled=True),
        lax.all_gather(gain_attn.astype(jnp.bfloat16), "dp", axis=0, tiled=True),
        lax.all_gather(gain_ffn.astype(jnp.bfloat16), "dp", axis=0, tiled=True),
        lax.all_gather(router_weight.astype(jnp.bfloat16), "dp", axis=0, tiled=True),
    )
    large_set = (
        lax.all_gather(expert_gate.astype(jnp.bfloat16), "dp", axis=0, tiled=True),
        lax.all_gather(expert_up.astype(jnp.bfloat16), "dp", axis=0, tiled=True),
        lax.all_gather(expert_down.astype(jnp.bfloat16), "dp", axis=0, tiled=True),
        lax.all_gather(shared_gate.astype(jnp.bfloat16), "dp", axis=0, tiled=True),
        lax.all_gather(shared_up.astype(jnp.bfloat16), "dp", axis=0, tiled=True),
        lax.all_gather(shared_down.astype(jnp.bfloat16), "dp", axis=0, tiled=True),
    )
    return (small_set, large_set)


def per_device(
    layer_input,
    seq_lengths,
    expert_routes,
    w_query,
    w_key,
    w_value,
    w_output,
    gain_attn,
    gain_ffn,
    router_weight,
    expert_gate,
    expert_up,
    expert_down,
    shared_gate,
    shared_up,
    shared_down,
    out_cotangent,
):
    masters = (
        w_query,
        w_key,
        w_value,
        w_output,
        gain_attn,
        gain_ffn,
        router_weight,
        expert_gate,
        expert_up,
        expert_down,
        shared_gate,
        shared_up,
        shared_down,
    )
    small_set, large_set = fetch_weights(masters)
    query_w, key_w, value_w, out_w, gain_one, gain_two, router_w = small_set
    gate_w, up_w, down_w, sgate_w, sup_w, sdown_w = large_set
    seq_count, own_len, model_width = layer_input.shape
    part_count = lax.axis_size("tensor")
    seq_span = own_len * part_count
    row_count = seq_count * seq_span
    local_width = query_w.shape[1]
    heads_here = local_width // HD
    experts = gate_w.shape[1]
    capacity = 4 * row_count // experts
    score_scale = 1.0 / math.sqrt(HD)
    cosine, sine_table = rope_tables(seq_span, HD // 2)
    first_gain_float = gain_one.astype(jnp.float32)
    second_gain_float = gain_two.astype(jnp.float32)
    input_rows = layer_input.astype(jnp.float32)
    first_normed_output, first_unit_input, first_norm_factor = apply_rms_norm(
        input_rows, first_gain_float
    )
    attn_in = lax.all_gather(first_normed_output.astype(jnp.bfloat16), "tensor", axis=1, tiled=True)
    attn_flat = attn_in.reshape(row_count, model_width)
    query_raw = jnp.dot(attn_flat, query_w, preferred_element_type=jnp.float32)
    key_raw = jnp.dot(attn_flat, key_w, preferred_element_type=jnp.float32)
    value_raw = jnp.dot(attn_flat, value_w, preferred_element_type=jnp.float32)
    head_shape = (seq_count, seq_span, heads_here, HD)
    query_rot = rotate(query_raw.reshape(head_shape), cosine, sine_table).astype(jnp.bfloat16)
    key_rot = rotate(key_raw.reshape(head_shape), cosine, sine_table).astype(jnp.bfloat16)
    value_rows = value_raw.astype(jnp.bfloat16).reshape(head_shape)
    contexts, log_total = lax.map(
        lambda seq_item: attend_forward(
            seq_item[0], seq_item[1], seq_item[2], seq_item[3], score_scale
        ),
        (query_rot, key_rot, value_rows, seq_lengths),
    )
    context_flat = contexts.reshape(row_count, local_width)
    attn_part = jnp.einsum("tc,oc->to", context_flat, out_w, preferred_element_type=jnp.float32)
    attn_own = lax.psum_scatter(
        attn_part.reshape(seq_count, seq_span, model_width),
        "tensor",
        scatter_dimension=1,
        tiled=True,
    )
    hidden_residual = input_rows + attn_own
    second_normed_output, second_unit_input, second_norm_factor = apply_rms_norm(
        hidden_residual, second_gain_float
    )
    ffn_in = lax.all_gather(second_normed_output.astype(jnp.bfloat16), "tensor", axis=1, tiled=True)
    ffn_flat = ffn_in.reshape(row_count, model_width)
    logits = jnp.dot(ffn_flat, router_w, preferred_element_type=jnp.float32)
    route_rows = expert_routes.reshape(row_count, 2)
    chosen = (route_rows[..., None] == jnp.arange(experts, dtype=jnp.int32)[None, None, :]).astype(
        jnp.float32
    )
    picked = jnp.sum(chosen * logits[:, None, :], axis=-1)
    gate_mix = jax.nn.softmax(picked, axis=-1)
    flat_route = route_rows.reshape(2 * row_count)
    route_hot = (flat_route[:, None] == jnp.arange(experts, dtype=jnp.int32)[None, :]).astype(
        jnp.int32
    )
    before = jnp.cumsum(route_hot, axis=0) - route_hot
    position = jnp.sum(before * route_hot, axis=-1)
    slot_index = flat_route * capacity + position
    slot_owner = (
        jnp.full((experts * capacity,), row_count, jnp.int32)
        .at[slot_index]
        .set(jnp.arange(2 * row_count, dtype=jnp.int32) // 2)
    )
    padded_rows = jnp.concatenate([ffn_flat, jnp.zeros((1, model_width), jnp.bfloat16)], axis=0)
    buffer = padded_rows[slot_owner].reshape(experts, capacity, model_width)
    gate_pre = jnp.einsum("ecd,def->ecf", buffer, gate_w, preferred_element_type=jnp.float32)
    up_pre = jnp.einsum("ecd,def->ecf", buffer, up_w, preferred_element_type=jnp.float32)
    gate_sig = jax.nn.sigmoid(gate_pre)
    inner_act = (gate_pre * gate_sig * up_pre).astype(jnp.bfloat16)
    expert_out = jnp.einsum("ecf,def->ecd", inner_act, down_w, preferred_element_type=jnp.float32)
    picked_out = expert_out.reshape(experts * capacity, model_width)[slot_index].reshape(
        row_count, 2, model_width
    )
    routed = jnp.sum(gate_mix[..., None] * picked_out, axis=1)
    shared_gate_pre = jnp.dot(ffn_flat, sgate_w, preferred_element_type=jnp.float32)
    shared_up_pre = jnp.dot(ffn_flat, sup_w, preferred_element_type=jnp.float32)
    shared_sig = jax.nn.sigmoid(shared_gate_pre)
    shared_act = (shared_gate_pre * shared_sig * shared_up_pre).astype(jnp.bfloat16)
    shared_out = jnp.einsum("tf,df->td", shared_act, sdown_w, preferred_element_type=jnp.float32)
    ffn_part = shared_out + routed
    ffn_own = lax.psum_scatter(
        ffn_part.reshape(seq_count, seq_span, model_width).astype(jnp.bfloat16),
        "tensor",
        scatter_dimension=1,
        tiled=True,
    ).astype(jnp.float32)
    layer_output = (hidden_residual + ffn_own).astype(jnp.bfloat16)
    small_set, large_set = fetch_weights(masters)
    query_w, key_w, value_w, out_w, gain_one, gain_two, router_w = small_set
    gate_w, up_w, down_w, sgate_w, sup_w, sdown_w = large_set
    part_index = lax.axis_index("tensor")
    own_places = part_index * own_len + jnp.arange(own_len, dtype=jnp.int32)
    valid_rows = (own_places[None, :] < seq_lengths[:, None]).astype(jnp.float32)
    cotangent = out_cotangent.astype(jnp.float32) * valid_rows[..., None]
    grad_ffn = lax.all_gather(cotangent.astype(jnp.bfloat16), "tensor", axis=1, tiled=True)
    grad_ffn_flat = grad_ffn.reshape(row_count, model_width)
    grad_ffn_f = grad_ffn_flat.astype(jnp.float32)
    grad_shared_act = jnp.einsum(
        "td,df->tf", grad_ffn_flat, sdown_w, preferred_element_type=jnp.float32
    )
    grad_sdown = jnp.einsum(
        "td,tf->df", grad_ffn_flat, shared_act, preferred_element_type=jnp.float32
    )
    grad_sgate_pre = (
        grad_shared_act * shared_up_pre * shared_sig * (1.0 + shared_gate_pre * (1.0 - shared_sig))
    ).astype(jnp.bfloat16)
    grad_sup_pre = (grad_shared_act * shared_gate_pre * shared_sig).astype(jnp.bfloat16)
    grad_sgate = jnp.einsum(
        "td,tf->df", ffn_flat, grad_sgate_pre, preferred_element_type=jnp.float32
    )
    grad_sup = jnp.einsum("td,tf->df", ffn_flat, grad_sup_pre, preferred_element_type=jnp.float32)
    grad_normed = jnp.einsum(
        "tf,df->td", grad_sgate_pre, sgate_w, preferred_element_type=jnp.float32
    ) + jnp.einsum("tf,df->td", grad_sup_pre, sup_w, preferred_element_type=jnp.float32)
    grad_gate_mix = jnp.sum(grad_ffn_f[:, None, :] * picked_out, axis=-1)
    grad_picked = gate_mix * (
        grad_gate_mix - jnp.sum(gate_mix * grad_gate_mix, axis=-1, keepdims=True)
    )
    grad_logits = jnp.sum(chosen * grad_picked[..., None], axis=1)
    grad_router_part = jnp.dot(ffn_flat.astype(jnp.float32).T, grad_logits, precision=highest)
    grad_normed = grad_normed + jnp.dot(
        grad_logits, router_w.astype(jnp.float32).T, precision=highest
    )
    grad_assign = (
        (gate_mix[..., None] * grad_ffn_f[:, None, :])
        .reshape(2 * row_count, model_width)
        .astype(jnp.bfloat16)
    )
    grad_expert_out = (
        jnp.zeros((experts * capacity, model_width), jnp.bfloat16).at[slot_index].set(grad_assign)
    )
    grad_expert_out = grad_expert_out.reshape(experts, capacity, model_width)
    grad_inner = jnp.einsum(
        "ecd,def->ecf", grad_expert_out, down_w, preferred_element_type=jnp.float32
    )
    grad_down = jnp.einsum(
        "ecd,ecf->def", grad_expert_out, inner_act, preferred_element_type=jnp.float32
    )
    grad_gate_pre = (grad_inner * up_pre * gate_sig * (1.0 + gate_pre * (1.0 - gate_sig))).astype(
        jnp.bfloat16
    )
    grad_up_pre = (grad_inner * gate_pre * gate_sig).astype(jnp.bfloat16)
    grad_gate = jnp.einsum(
        "ecd,ecf->def", buffer, grad_gate_pre, preferred_element_type=jnp.float32
    )
    grad_up = jnp.einsum("ecd,ecf->def", buffer, grad_up_pre, preferred_element_type=jnp.float32)
    grad_buffer = jnp.einsum(
        "ecf,def->ecd", grad_gate_pre, gate_w, preferred_element_type=jnp.float32
    ) + jnp.einsum("ecf,def->ecd", grad_up_pre, up_w, preferred_element_type=jnp.float32)
    grad_back_rows = grad_buffer.reshape(experts * capacity, model_width)[slot_index].reshape(
        row_count, 2, model_width
    )
    grad_normed = grad_normed + jnp.sum(grad_back_rows, axis=1)
    second_local_gradient = lax.psum_scatter(
        grad_normed.reshape(seq_count, seq_span, model_width).astype(jnp.bfloat16),
        "tensor",
        scatter_dimension=1,
        tiled=True,
    ).astype(jnp.float32)
    hidden_norm_gradient, second_gain_grad_piece = norm_backward_pass(
        second_local_gradient, second_unit_input, second_norm_factor, second_gain_float
    )
    grad_hidden = cotangent + hidden_norm_gradient
    grad_attn = lax.all_gather(grad_hidden.astype(jnp.bfloat16), "tensor", axis=1, tiled=True)
    grad_attn_flat = grad_attn.reshape(row_count, model_width)
    grad_out_w = jnp.einsum(
        "to,tc->oc", grad_attn_flat, context_flat, preferred_element_type=jnp.float32
    )
    grad_context = jnp.einsum(
        "to,oc->tc", grad_attn_flat, out_w, preferred_element_type=jnp.float32
    ).astype(jnp.bfloat16)
    grad_context = grad_context.reshape(head_shape)
    query_grads, key_grads, value_grads = lax.map(
        lambda seq_item: attend_backward(
            seq_item[0],
            seq_item[1],
            seq_item[2],
            seq_item[3],
            seq_item[4],
            seq_item[5],
            score_scale,
        ),
        (query_rot, key_rot, value_rows, seq_lengths, log_total, grad_context),
    )
    grad_query_pre = (
        unrotate(query_grads, cosine, sine_table)
        .reshape(row_count, local_width)
        .astype(jnp.bfloat16)
    )
    grad_key_pre = (
        unrotate(key_grads, cosine, sine_table).reshape(row_count, local_width).astype(jnp.bfloat16)
    )
    grad_value_pre = value_grads.reshape(row_count, local_width).astype(jnp.bfloat16)
    grad_query_w = jnp.einsum(
        "td,tc->dc", attn_flat, grad_query_pre, preferred_element_type=jnp.float32
    )
    grad_key_w = jnp.einsum(
        "td,tc->dc", attn_flat, grad_key_pre, preferred_element_type=jnp.float32
    )
    grad_value_w = jnp.einsum(
        "td,tc->dc", attn_flat, grad_value_pre, preferred_element_type=jnp.float32
    )
    grad_attn_in = (
        jnp.einsum("tc,dc->td", grad_query_pre, query_w, preferred_element_type=jnp.float32)
        + jnp.einsum("tc,dc->td", grad_key_pre, key_w, preferred_element_type=jnp.float32)
        + jnp.einsum("tc,dc->td", grad_value_pre, value_w, preferred_element_type=jnp.float32)
    )
    first_local_gradient = lax.psum_scatter(
        grad_attn_in.reshape(seq_count, seq_span, model_width).astype(jnp.bfloat16),
        "tensor",
        scatter_dimension=1,
        tiled=True,
    ).astype(jnp.float32)
    input_norm_gradient, first_gain_grad_piece = norm_backward_pass(
        first_local_gradient, first_unit_input, first_norm_factor, first_gain_float
    )
    grad_input = (grad_hidden + input_norm_gradient).astype(jnp.bfloat16)
    attn_shards = (
        lax.psum_scatter(grad_query_w, "dp", scatter_dimension=0, tiled=True),
        lax.psum_scatter(grad_key_w, "dp", scatter_dimension=0, tiled=True),
        lax.psum_scatter(grad_value_w, "dp", scatter_dimension=0, tiled=True),
        lax.psum_scatter(grad_out_w, "dp", scatter_dimension=0, tiled=True),
        lax.psum_scatter(first_gain_grad_piece, "dp", scatter_dimension=0, tiled=True),
        lax.psum_scatter(second_gain_grad_piece, "dp", scatter_dimension=0, tiled=True),
        lax.psum_scatter(grad_router_part, "dp", scatter_dimension=0, tiled=True),
    )
    ffn_shards = (
        lax.psum_scatter(grad_gate, "dp", scatter_dimension=0, tiled=True),
        lax.psum_scatter(grad_up, "dp", scatter_dimension=0, tiled=True),
        lax.psum_scatter(grad_down, "dp", scatter_dimension=0, tiled=True),
        lax.psum_scatter(grad_sgate, "dp", scatter_dimension=0, tiled=True),
        lax.psum_scatter(grad_sup, "dp", scatter_dimension=0, tiled=True),
        lax.psum_scatter(grad_sdown, "dp", scatter_dimension=0, tiled=True),
    )
    gain_one_grad, gain_two_grad, router_grad = lax.psum(
        (attn_shards[4], attn_shards[5], attn_shards[6]), "tensor"
    )
    return (
        layer_output,
        grad_input,
        attn_shards[0],
        attn_shards[1],
        attn_shards[2],
        attn_shards[3],
        gain_one_grad,
        gain_two_grad,
        router_grad,
        ffn_shards[0],
        ffn_shards[1],
        ffn_shards[2],
        ffn_shards[3],
        ffn_shards[4],
        ffn_shards[5],
    )


def solution(mesh):
    in_specs = (
        P("dp", "tensor", None),
        P("dp"),
        P("dp", None, None),
        P("dp", "tensor"),
        P("dp", "tensor"),
        P("dp", "tensor"),
        P("dp", "tensor"),
        P("dp"),
        P("dp"),
        P("dp", None),
        P("dp", None, "tensor"),
        P("dp", None, "tensor"),
        P("dp", None, "tensor"),
        P("dp", "tensor"),
        P("dp", "tensor"),
        P("dp", "tensor"),
        P("dp", "tensor", None),
    )
    out_specs = (
        P("dp", "tensor", None),
        P("dp", "tensor", None),
        P("dp", "tensor"),
        P("dp", "tensor"),
        P("dp", "tensor"),
        P("dp", "tensor"),
        P("dp"),
        P("dp"),
        P("dp", None),
        P("dp", None, "tensor"),
        P("dp", None, "tensor"),
        P("dp", None, "tensor"),
        P("dp", "tensor"),
        P("dp", "tensor"),
        P("dp", "tensor"),
    )
    return jax.shard_map(
        per_device, mesh=mesh, in_specs=in_specs, out_specs=out_specs, check_vma=False
    )
```

profile of v0, /device:TPU:0, one launch (start us, length us, event | category | flops | bytes accessed | tf_op | source)
XLA Modules:
  0.0 3311.2 jit_solution(7612107812086589678)
XLA Ops:
  11.0 43.5 %all-reduce.7 = (bf16[768]{0:T(1024)(128)(2,1)S(1)}, bf16[768]{0:T(1024)(128)(2,1)S(1)}) all-reduce(bf16[768]{0:T(1024)(128)(2,1)S(1)} %dynamic-update-slice, bf16[768]{0:T(1024)(128)(2,1)S(1)} %dynamic-update-slice.1), channel_id=1, replica_groups=mesh['dp'=16,'tensor'=2] {'dp'}, use_global_device_ids=true, to_apply=%add.1 | all-reduce | flops 1536 | bytes 6144
  58.3 38.7 %all_gather.65 = bf16[768,384]{1,0:T(8,128)(2,1)S(1)} all-gather(bf16[48,384]{1,0:T(8,128)(2,1)S(1)} %convert_element_type.233), channel_id=1, replica_groups=mesh['dp'=16,'tensor'=2] {'dp'}, dimensions={0}, use_global_device_ids=true | all-gather | bytes 626688 | tf_op jit(solution)/shard_map/all_gather | solution.py:152
  98.1 41.3 %all_gather.64 = bf16[768,384]{1,0:T(8,128)(2,1)S(1)} all-gather(bf16[48,384]{1,0:T(8,128)(2,1)S(1)} %convert_element_type.232), channel_id=1, replica_groups=mesh['dp'=16,'tensor'=2] {'dp'}, dimensions={0}, use_global_device_ids=true | all-gather | bytes 626688 | tf_op jit(solution)/shard_map/all_gather | solution.py:151
  141.7 40.0 %all_gather.66 = bf16[768,384]{1,0:T(8,128)(2,1)S(1)} all-gather(bf16[48,384]{1,0:T(8,128)(2,1)S(1)} %convert_element_type.234), channel_id=1, replica_groups=mesh['dp'=16,'tensor'=2] {'dp'}, dimensions={0}, use_global_device_ids=true | all-gather | bytes 626688 | tf_op jit(solution)/shard_map/all_gather | solution.py:153
  181.8 42.0 %all_gather.67 = bf16[768,384]{1,0:T(8,128)(2,1)} all-gather(bf16[48,384]{1,0:T(8,128)(2,1)S(1)} %convert_element_type.236), channel_id=1, replica_groups=mesh['dp'=16,'tensor'=2] {'dp'}, dimensions={0}, use_global_device_ids=true | all-gather | bytes 626688 | tf_op jit(solution)/shard_map/all_gather | solution.py:154
  228.6 27.5 while.47
  287.5 41.0 %all-gather = bf16[16,48,8]{1,2,0:T(8,128)(2,1)S(1)} all-gather(bf16[1,48,8]{1,2,0:T(8,128)(2,1)S(1)} %convert_bitcast_fusion), channel_id=1, replica_groups=mesh['dp'=16,'tensor'=2] {'dp'}, dimensions={0}, use_global_device_ids=true | all-gather | bytes 13056 | tf_op jit(solution)/shard_map/all_gather | solution.py:157
  328.8 8.1 scatter_custom_fusion
  344.7 8.5 mul.592
  357.1 17.8 gather_fusion
  374.9 15.1 scatter_custom_fusion.1
  395.2 23.7 all-gather.18.cloned.1.call-done
  424.1 54.6 %all-gather.20.cloned.1.call-done = bf16[768,1024]{1,0:T(8,128)(2,1)} async-done(((bf16[48,1024]{1,0:T(8,128)(2,1)}), bf16[768,1024]{1,0:T(8,128)(2,1)}) %all-gather.20.cloned.1.call-update) | async-done | bytes 1572880 | tf_op jit(solution)/shard_map/all_gather | solution.py:165
  492.8 140.4 %all-gather.22.cloned.1.call-done = bf16[768,8,1024]{2,0,1:T(8,128)(2,1)} async-done(((bf16[48,8,1024]{2,0,1:T(8,128)(2,1)}), bf16[768,8,1024]{2,0,1:T(8,128)(2,1)}) %all-gather.22.cloned.1.call-update) | async-done | bytes 12582928 | tf_op jit(solution)/shard_map/all_gather | solution.py:160
  633.2 15.7 fusion.122
  648.9 138.2 %all-gather.24.cloned.1.call-done = bf16[768,8,1024]{2,0,1:T(8,128)(2,1)} async-done(((bf16[48,8,1024]{2,0,1:T(8,128)(2,1)}), bf16[768,8,1024]{2,0,1:T(8,128)(2,1)}) %all-gather.24.cloned.1.call-update) | async-done | bytes 12582928 | tf_op jit(solution)/shard_map/all_gather | solution.py:161
  787.0 15.7 fusion.123
  802.7 137.4 %all-gather.26.cloned.1.call-done = bf16[768,8,1024]{2,0,1:T(8,128)(2,1)} async-done(((bf16[48,8,1024]{2,0,1:T(8,128)(2,1)}), bf16[768,8,1024]{2,0,1:T(8,128)(2,1)}) %all-gather.26.cloned.1.call-update) | async-done | bytes 12582928 | tf_op jit(solution)/shard_map/all_gather | solution.py:162
  940.1 27.9 multiply_convert_fusion.1
  968.1 15.4 fusion.127
  983.5 17.1 convolution_add_fusion
  1000.6 15.2 gather_fusion.2
  1015.9 8.2 reshape.584
  1024.1 15.8 fusion.124
  1039.9 15.2 gather_fusion.1
  1055.1 8.3 reshape.580
  1063.5 17.3 multiply_reduce_fusion.1
  1082.2 11.9 reduce_sum.156
  1128.0 112.2 %while.48 = (s32[]{:T(128)}, f32[1024,6,64]{0,2,1:T(8,128)}, f32[1024,6,64]{0,2,1:T(8,128)}, f32[2,512,6,64]{1,0,3,2:T(2,128)}, s32[2]{0:T(128)S(1)}, /*index=5*...) while((s32[]{:T(128)}, f32[1024,6,64]{0,2,1:T(8,128)}, ...), condition=%wide.region_25.26_spmd.clone, body=%wide.region_23.25_spmd.clone.sunk | while | flops 2063661568 | bytes 217672144 | solution.py:128
  1168.7 15.0 dynamic_update_slice.33
  1194.5 7.7 multiply_reduce_fusion.6
  1225.0 15.0 dynamic_update_slice.33
  1289.5 16.2 convolution_bitcast_fusion.2
  1305.7 25.1 copy.119
  1330.9 16.1 convolution_bitcast_fusion.1
  1347.0 25.1 copy.121
  1372.4 16.0 convolution_bitcast_fusion
  1388.4 25.1 copy.123
  1417.1 42.8 %all-reduce.5 = (f32[768]{0:T(1024)S(1)}, f32[768]{0:T(1024)S(1)}) all-reduce(f32[768]{0:T(1024)S(1)} %get-tuple-element.243, f32[768]{0:T(1024)S(1)} %copy-done.79), channel_id=10, replica_groups=mesh['dp'=16,'tensor'=2] {'dp'}, use_global_device_ids=true, to_apply=%region_33.34.clone | all-reduce | flops 1536 | bytes 12288
  1466.4 83.2 %reduce-scatter.42.cloned.1.call-done = f32[48,1024]{1,0:T(8,128)} async-done(((f32[768,1024]{1,0:T(8,128)}), f32[48,1024]{1,0:T(8,128)}) %reduce-scatter.42.cloned.1.call-update) | async-done | bytes 196624 | tf_op jit(solution)/shard_map/reduce_scatter | solution.py:439
  1549.7 136.3 %reduce-scatter.44.cloned.1.call-done = f32[48,1024]{1,0:T(8,128)} async-done(((f32[768,1024]{1,0:T(8,128)}), f32[48,1024]{1,0:T(8,128)}) %reduce-scatter.44.cloned.1.call-update) | async-done | bytes 196624 | tf_op jit(solution)/shard_map/reduce_scatter | solution.py:440
  1686.0 129.0 %reduce-scatter.26.cloned.1.call-done = f32[48,384]{1,0:T(8,128)} async-done(((f32[768,384]{1,0:T(8,128)}), f32[48,384]{1,0:T(8,128)}) %reduce-scatter.26.cloned.1.call-update) | async-done | bytes 73744 | tf_op jit(solution)/shard_map/reduce_scatter | solution.py:426
  1814.9 128.5 %reduce-scatter.28.cloned.1.call-done = f32[48,384]{1,0:T(8,128)} async-done(((f32[768,384]{1,0:T(8,128)}), f32[48,384]{1,0:T(8,128)}) %reduce-scatter.28.cloned.1.call-update) | async-done | bytes 73744 | tf_op jit(solution)/shard_map/reduce_scatter | solution.py:427
  1943.4 128.6 %reduce-scatter.30.cloned.1.call-done = f32[48,384]{1,0:T(8,128)} async-done(((f32[768,384]{1,0:T(8,128)}), f32[48,384]{1,0:T(8,128)}) %reduce-scatter.30.cloned.1.call-update) | async-done | bytes 73744 | tf_op jit(solution)/shard_map/reduce_scatter | solution.py:428
  2072.1 128.6 %reduce-scatter.32.cloned.1.call-done = f32[48,384]{1,0:T(8,128)} async-done(((f32[768,384]{1,0:T(8,128)}), f32[48,384]{1,0:T(8,128)}) %reduce-scatter.32.cloned.1.call-update) | async-done | bytes 73744 | tf_op jit(solution)/shard_map/reduce_scatter | solution.py:429
  2200.7 367.9 %reduce-scatter.34.cloned.1.call-done = f32[48,8,1024]{2,1,0:T(8,128)} async-done(((f32[768,8,1024]{2,1,0:T(8,128)}), f32[48,8,1024]{2,1,0:T(8,128)}) %reduce-scatter.34.cloned.1.call-update) | async-done | bytes 1572880 | tf_op jit(solution)/shard_map/reduce_scatter | solution.py:435
  2568.6 367.8 %reduce-scatter.36.cloned.1.call-done = f32[48,8,1024]{2,1,0:T(8,128)} async-done(((f32[768,8,1024]{2,1,0:T(8,128)}), f32[48,8,1024]{2,1,0:T(8,128)}) %reduce-scatter.36.cloned.1.call-update) | async-done | bytes 1572880 | tf_op jit(solution)/shard_map/reduce_scatter | solution.py:436
  2936.5 368.0 %reduce-scatter.38.cloned.1.call-done = f32[48,8,1024]{2,1,0:T(8,128)} async-done(((f32[768,8,1024]{2,1,0:T(8,128)}), f32[48,8,1024]{2,1,0:T(8,128)}) %reduce-scatter.38.cloned.1.call-update) | async-done | bytes 1572880 | tf_op jit(solution)/shard_map/reduce_scatter | solution.py:437
  (411 shorter events, 269.8 us)
Async XLA Ops:
  7.2 51.1 %copy-start.61 = (f32[48,384]{1,0:T(8,128)S(1)}, f32[48,384]{1,0:T(8,128)}, u32[]{:S(2)}) copy-start(f32[48,384]{1,0:T(8,128)} %param.25) | copy-start | bytes 221188
  7.2 90.9 %copy-start.62 = (f32[48,384]{1,0:T(8,128)S(1)}, f32[48,384]{1,0:T(8,128)}, u32[]{:S(2)}) copy-start(f32[48,384]{1,0:T(8,128)} %param.24) | copy-start | bytes 221188
  7.2 216.5 %all-gather.12.cloned.1.call-start = ((), (), s32[]{:S(2)}) async-start(), calls=%async_computation.15 | async-start | bytes 2359296 | tf_op jit(solution)/shard_map/all_gather | solution.py:223
  55.9 84.6 %copy-start.63 = (f32[48,384]{1,0:T(8,128)S(1)}, f32[48,384]{1,0:T(8,128)}, u32[]{:S(2)}) copy-start(f32[48,384]{1,0:T(8,128)} %param.26) | copy-start | bytes 221188
  55.9 84.6 %copy-start.64 = (f32[48,384]{1,0:T(8,128)S(1)}, f32[48,384]{1,0:T(8,128)}, u32[]{:S(2)}) copy-start(f32[48,384]{1,0:T(8,128)} %param.27) | copy-start | bytes 221188
  58.2 212.1 %reduce-scatter.18.cloned.1.call-start = ((), (), s32[]{:S(2)}) async-start(), calls=%async_computation.16 | async-start | bytes 4718592 | tf_op jit(solution)/shard_map/reduce_scatter | solution.py:240
  97.0 129.2 %copy-start.20 = (bf16[768,384]{1,0:T(8,128)(2,1)}, bf16[768,384]{1,0:T(8,128)(2,1)S(1)}, u32[]{:S(2)}) copy-start(bf16[768,384]{1,0:T(8,128)(2,1)S(1)} %all_gather.65) | copy-start | bytes 1769476
  139.4 86.9 %copy-start.22 = (bf16[768,384]{1,0:T(8,128)(2,1)}, bf16[768,384]{1,0:T(8,128)(2,1)S(1)}, u32[]{:S(2)}) copy-start(bf16[768,384]{1,0:T(8,128)(2,1)S(1)} %all_gather.64) | copy-start | bytes 1769476
  141.7 85.4 %copy-start.39 = (f32[1024,32]{0,1:T(8,128)}, f32[1024,32]{0,1:T(8,128)S(1)}, u32[]{:S(2)}) copy-start(f32[1024,32]{0,1:T(8,128)S(1)} %get-tuple-element.318) | copy-start | bytes 393220
  181.8 46.0 %copy-start.30 = (bf16[768,384]{1,0:T(8,128)(2,1)}, bf16[768,384]{1,0:T(8,128)(2,1)S(1)}, u32[]{:S(2)}) copy-start(bf16[768,384]{1,0:T(8,128)(2,1)S(1)} %all_gather.66) | copy-start | bytes 1769476
  262.4 74.5 %all-gather.28.cloned.1.call-start = ((), (), s32[]{:S(2)}) async-start(), calls=%async_computation.25 | async-start | bytes 2359296 | tf_op jit(solution)/shard_map/all_gather | solution.py:302
  266.0 87.2 %all-gather.14.cloned.1.call-start = ((), (), s32[]{:S(2)}) async-start(), calls=%async_computation.17 | async-start | bytes 2359296 | tf_op jit(solution)/shard_map/all_gather | solution.py:250
  274.3 115.7 %all-gather.16.cloned.1.call-start = ((), (), s32[]{:S(2)}) async-start(), calls=%async_computation.18 | async-start | bytes 1671168 | tf_op jit(solution)/shard_map/all_gather | solution.py:163
  275.1 143.9 %all-gather.18.cloned.1.call-start = ((), (), s32[]{:S(2)}) async-start(), calls=%async_computation.19 | async-start | bytes 1671168 | tf_op jit(solution)/shard_map/all_gather | solution.py:164
  275.8 202.9 %all-gather.20.cloned.1.call-start = ((), (), s32[]{:S(2)}) async-start(), calls=%async_computation.20 | async-start | bytes 1671168 | tf_op jit(solution)/shard_map/all_gather | solution.py:165
  277.4 355.7 %all-gather.22.cloned.1.call-start = ((), (), s32[]{:S(2)}) async-start(), calls=%async_computation.21 | async-start | bytes 13369344 | tf_op jit(solution)/shard_map/all_gather | solution.py:160
  279.3 507.8 %all-gather.24.cloned.1.call-start = ((), (), s32[]{:S(2)}) async-start(), calls=%async_computation.22 | async-start | bytes 13369344 | tf_op jit(solution)/shard_map/all_gather | solution.py:161
  281.5 658.7 %all-gather.26.cloned.1.call-start = ((), (), s32[]{:S(2)}) async-start(), calls=%async_computation.23 | async-start | bytes 13369344 | tf_op jit(solution)/shard_map/all_gather | solution.py:162
  283.3 824.9 %reduce-scatter.22.cloned.1.call-start = ((), (), s32[]{:S(2)}) async-start(), calls=%async_computation.26 | async-start | bytes 2359296 | tf_op jit(solution)/shard_map/reduce_scatter | solution.py:361
  328.6 24.7 copy-start.54
  356.0 19.0 copy-start.67
  395.2 83.5 %copy-start.18 = (bf16[1,1024,768]{2,1,0:T(8,128)(2,1)S(1)}, bf16[1,1024,768]{2,1,0:T(8,128)(2,1)}, u32[]{:S(2)}) copy-start(bf16[1,1024,768]{2,1,0:T(8,128)(2,1)} %all-gather.28.cloned.1.call-done) | copy-start | bytes 4718596
  424.1 61.7 %copy-start.82 = (bf16[768,1024]{1,0:T(8,128)(2,1)S(1)}, bf16[768,1024]{1,0:T(8,128)(2,1)}, u32[]{:S(2)}) copy-start(bf16[768,1024]{1,0:T(8,128)(2,1)} %all-gather.16.cloned.1.call-done) | copy-start | bytes 4718596
  1063.5 18.6 copy-start.47
  1063.5 18.6 copy-start.60
  1063.5 18.6 copy-start.68
  1063.5 18.7 copy-start.53
  1100.8 24.1 all-gather.30.cloned.1.call-start
  1113.7 14.3 copy-start.2
  1113.7 300.7 %reduce-scatter.46.cloned.1.call-start = ((), (), s32[]{:S(2)}) async-start(), calls=%async_computation.39 | async-start | bytes 417792
  1117.8 297.5 %reduce-scatter.24.cloned.1.call-start = ((), (), s32[]{:S(2)}) async-start(), calls=%async_computation.28 | async-start | bytes 2359296 | tf_op jit(solution)/shard_map/reduce_scatter | solution.py:415
  1251.0 212.1 %reduce-scatter.20.cloned.1.call-start = ((), (), s32[]{:S(2)}) async-start(), calls=%async_computation.24 | async-start | bytes 2359296 | tf_op jit(solution)/shard_map/reduce_scatter | solution.py:288
  1257.2 209.2 %reduce-scatter.40.cloned.1.call-start = ((), (), s32[]{:S(2)}) async-start(), calls=%async_computation.36 | async-start | bytes 3342336 | tf_op jit(solution)/shard_map/reduce_scatter | solution.py:438
  1262.4 287.3 %reduce-scatter.42.cloned.1.call-start = ((), (), s32[]{:S(2)}) async-start(), calls=%async_computation.37 | async-start | bytes 3342336 | tf_op jit(solution)/shard_map/reduce_scatter | solution.py:439
  1267.5 418.4 %reduce-scatter.44.cloned.1.call-start = ((), (), s32[]{:S(2)}) async-start(), calls=%async_computation.38 | async-start | bytes 3342336 | tf_op jit(solution)/shard_map/reduce_scatter | solution.py:440
  1274.1 540.8 %reduce-scatter.26.cloned.1.call-start = ((), (), s32[]{:S(2)}) async-start(), calls=%async_computation.29 | async-start | bytes 1253376 | tf_op jit(solution)/shard_map/reduce_scatter | solution.py:426
  1278.7 664.7 %reduce-scatter.28.cloned.1.call-start = ((), (), s32[]{:S(2)}) async-start(), calls=%async_computation.30 | async-start | bytes 1253376 | tf_op jit(solution)/shard_map/reduce_scatter | solution.py:427
  1282.3 789.7 %reduce-scatter.30.cloned.1.call-start = ((), (), s32[]{:S(2)}) async-start(), calls=%async_computation.31 | async-start | bytes 1253376 | tf_op jit(solution)/shard_map/reduce_scatter | solution.py:428
  1285.9 914.8 %reduce-scatter.32.cloned.1.call-start = ((), (), s32[]{:S(2)}) async-start(), calls=%async_computation.32 | async-start | bytes 1253376 | tf_op jit(solution)/shard_map/reduce_scatter | solution.py:429
  1289.5 1279.2 %reduce-scatter.34.cloned.1.call-start = ((), (), s32[]{:S(2)}) async-start(), calls=%async_computation.33 | async-start | bytes 26738688 | tf_op jit(solution)/shard_map/reduce_scatter | solution.py:435
  1330.8 1605.6 %reduce-scatter.36.cloned.1.call-start = ((), (), s32[]{:S(2)}) async-start(), calls=%async_computation.34 | async-start | bytes 26738688 | tf_op jit(solution)/shard_map/reduce_scatter | solution.py:436
  1372.1 1932.3 %reduce-scatter.38.cloned.1.call-start = ((), (), s32[]{:S(2)}) async-start(), calls=%async_computation.35 | async-start | bytes 26738688 | tf_op jit(solution)/shard_map/reduce_scatter | solution.py:437
  1413.5 49.6 %copy-start.8 = (f32[1,512,768]{2,1,0:T(8,128)S(1)}, f32[1,512,768]{2,1,0:T(8,128)}, u32[]{:S(2)}) copy-start(f32[1,512,768]{2,1,0:T(8,128)} %copy-done.6) | copy-start | bytes 4718596
  1413.5 49.6 %copy-start.17 = (bf16[1,512,768]{2,1,0:T(8,128)(2,1)S(1)}, bf16[1,512,768]{2,1,0:T(8,128)(2,1)}, u32[]{:S(2)}) copy-start(bf16[1,512,768]{2,1,0:T(8,128)(2,1)} %param.37) | copy-start | bytes 2359300
  1413.6 49.6 %copy-start.58 = (f32[768]{0:T(1024)S(1)}, f32[768]{0:T(1024)}, u32[]{:S(2)}) copy-start(f32[768]{0:T(1024)} %copy-done.56) | copy-start | bytes 9220
  1413.6 49.6 %copy-start.71 = (f32[512]{0:T(512)S(1)}, f32[512]{0:T(512)}, u32[]{:S(2)}) copy-start(f32[512]{0:T(512)} %copy-done.69) | copy-start | bytes 6148
  1413.6 49.6 %copy-start.74 = (f32[512]{0:T(512)S(1)}, f32[512]{0:T(512)}, u32[]{:S(2)}) copy-start(f32[512]{0:T(512)} %copy-done.72) | copy-start | bytes 6148
  1413.6 49.6 %copy-start.78 = (f32[512]{0:T(512)S(1)}, f32[512]{0:T(512)}, u32[]{:S(2)}) copy-start(f32[512]{0:T(512)} %copy-done.77) | copy-start | bytes 6148
  (74 other events, 399.6 us)
Sparse Core Ops, SparseCore 0:
  58.4 5.6 all-gather.11
  262.5 7.8 reduce-scatter.17
  272.6 10.9 all-gather.27
  285.6 10.9 all-gather.13
  300.2 59.0 all-gather.15
  362.3 56.6 all-gather.17
  422.1 56.5 all-gather.19
  482.3 150.7 all-gather.21
  636.8 150.2 all-gather.23
  789.9 150.2 all-gather.25
  1100.9 7.2 reduce-scatter.21
  1113.8 11.0 all-gather.29
  1129.5 122.8 reduce-scatter.45
  1254.6 8.1 reduce-scatter.23
  1264.9 10.2 reduce-scatter.19
  1281.4 131.9 reduce-scatter.39
  1419.6 130.0 reduce-scatter.41
  1555.8 130.0 reduce-scatter.43
  1692.0 122.8 reduce-scatter.25
  1820.8 122.5 reduce-scatter.27
  1949.5 122.5 reduce-scatter.29
  2078.1 122.5 reduce-scatter.31
  2208.0 360.6 reduce-scatter.33
  2575.8 360.6 reduce-scatter.35
  2943.7 360.6 reduce-scatter.37
where the time goes:
time: 3320 us; the launch traced here: 3310 us
  waiting for transfers between devices  2350 us (71%)
  matrix products  312 us (9%)
  blocking collectives  292 us (9%)
  local copies, waits for them, and re-layouts  230 us (7%)
  other arithmetic  98.1 us (3%)
    reduce_scatter x1, waiting for transfers between devices, per_device(): lax.psum_scatter(grad_down, 'dp', scatter_dimension=0, tiled=True)  368 us
    reduce_scatter x1, waiting for transfers between devices, per_device(): lax.psum_scatter(grad_gate, 'dp', scatter_dimension=0, tiled=True)  368 us
    reduce_scatter x1, waiting for transfers between devices, per_device(): lax.psum_scatter(grad_up, 'dp', scatter_dimension=0, tiled=True)  368 us
    all_gather x1, waiting for transfers between devices, fetch_weights(): lax.all_gather(expert_gate.astype(jnp.bfloat16), 'dp', axis=0, tiled=True)  140 us
    all_gather x1, waiting for transfers between devices, fetch_weights(): lax.all_gather(expert_up.astype(jnp.bfloat16), 'dp', axis=0, tiled=True)  138 us
    all_gather x1, waiting for transfers between devices, fetch_weights(): lax.all_gather(expert_down.astype(jnp.bfloat16), 'dp', axis=0, tiled=True)  137 us
    reduce_scatter x1, waiting for transfers between devices, per_device(): lax.psum_scatter(grad_sdown, 'dp', scatter_dimension=0, tiled=True)  136 us
    reduce_scatter x1, waiting for transfers between devices, per_device(): lax.psum_scatter(grad_query_w, 'dp', scatter_dimension=0, tiled=True)  129 us
  transfers between devices with their start and end apart: 25, of which 17 were waited for; matrix products, arithmetic and copies ran while one was open for 13% of the time, Pallas kernels for 0%

commit v1 on v0

v1 whole, which is shorter than its diff:
```python
import functools
import math

import jax
import jax.numpy as jnp
from jax import lax
from jax.experimental import pallas as pl
from jax.experimental.pallas import tpu as pltpu
from jax.sharding import PartitionSpec as P

HD = 64
LANES = 128
EPS = 1e-06
F32 = jnp.float32
BF16 = jnp.bfloat16
HIGHEST = lax.Precision.HIGHEST
VMEM_LIMIT = 56 * 1024 * 1024

NN = (((1,), (0,)), ((), ()))
NT = (((1,), (1,)), ((), ()))
TN = (((0,), (0,)), ((), ()))


def mm(left, right, dims):
    return lax.dot_general(left, right, dims, preferred_element_type=F32)


def params(count):
    return pltpu.CompilerParams(
        dimension_semantics=("arbitrary",) * count, vmem_limit_bytes=VMEM_LIMIT
    )


def cost(flops, nbytes, trans=0):
    return pl.CostEstimate(flops=int(flops), bytes_accessed=int(nbytes), transcendentals=int(trans))


def partner(values):
    lane = lax.broadcasted_iota(jnp.int32, values.shape, 1)
    return jnp.where(
        lane % HD < HD // 2,
        pltpu.roll(values, LANES - HD // 2, 1),
        pltpu.roll(values, HD // 2, 1),
    )


def head_lanes(shape, head):
    lane = lax.broadcasted_iota(jnp.int32, shape, 1)
    return (lane // HD) == head


def attn_fwd_kernel(len_ref, a_ref, w_ref, cos_ref, sin_ref, qkv_ref, ctx_ref, *, block):
    span = a_ref.shape[0]
    length = len_ref[0]
    raw = mm(a_ref[...], w_ref[...], NN)
    cosine, sine = cos_ref[...], sin_ref[...]
    query, key = raw[:, :LANES], raw[:, LANES : 2 * LANES]
    qkv_ref[:, :LANES] = (query * cosine + partner(query) * sine).astype(BF16)
    qkv_ref[:, LANES : 2 * LANES] = (key * cosine + partner(key) * sine).astype(BF16)
    qkv_ref[:, 2 * LANES :] = raw[:, 2 * LANES :].astype(BF16)
    for index in range(span // block):
        keys = (index + 1) * block
        query_rows = qkv_ref[index * block : keys, :LANES] * jnp.asarray(HD**-0.5, BF16)
        key_rows = qkv_ref[:keys, LANES : 2 * LANES]
        value_rows = qkv_ref[:keys, 2 * LANES :]
        row = index * block + lax.broadcasted_iota(jnp.int32, (block, keys), 0)
        column = lax.broadcasted_iota(jnp.int32, (block, keys), 1)
        allowed = (column <= row) & (column < length)
        parts = []
        for head in range(LANES // HD):
            masked_query = jnp.where(
                head_lanes(query_rows.shape, head), query_rows, jnp.zeros_like(query_rows)
            )
            scores = jnp.where(allowed, mm(masked_query, key_rows, NT), -1e30)
            peak = jnp.max(scores, axis=1, keepdims=True)
            powers = jnp.exp(scores - peak)
            total = jnp.sum(powers, axis=1, keepdims=True)
            prob = (powers * (1.0 / total)).astype(BF16)
            parts.append(mm(prob, value_rows, NN))
        context = jnp.where(head_lanes(parts[0].shape, 0), parts[0], parts[1])
        ctx_ref[index * block : keys, :] = context.astype(BF16)


def attn_forward(length, attn_in, qkv_w, cosine, sine):
    span, width = attn_in.shape
    pairs = qkv_w.shape[1] // (3 * LANES)
    return pl.pallas_call(
        functools.partial(attn_fwd_kernel, block=256),
        grid=(pairs,),
        in_specs=[
            pl.BlockSpec(memory_space=pltpu.SMEM),
            pl.BlockSpec((span, width), lambda i: (0, 0)),
            pl.BlockSpec((width, 3 * LANES), lambda i: (0, i)),
            pl.BlockSpec((span, LANES), lambda i: (0, 0)),
            pl.BlockSpec((span, LANES), lambda i: (0, 0)),
        ],
        out_specs=[
            pl.BlockSpec((span, 3 * LANES), lambda i: (0, i)),
            pl.BlockSpec((span, LANES), lambda i: (0, i)),
        ],
        out_shape=[
            jax.ShapeDtypeStruct((span, pairs * 3 * LANES), BF16),
            jax.ShapeDtypeStruct((span, pairs * LANES), BF16),
        ],
        compiler_params=params(1),
        cost_estimate=cost(2 * span * width * pairs * 384 + 12 * span * span * 128, 12e6, 6e6),
        name="attn_fwd",
    )(length, attn_in, qkv_w, cosine, sine)


def attn_bwd_kernel(
    len_ref, a_ref, da_in_ref, w_ref, wo_ref, qkv_ref, ctx_ref, cos_ref, sin_ref,
    gw_ref, da_ref, dctx_s, dq_s, dk_s, dv_s, *, block,
):
    span = a_ref.shape[0]
    length = len_ref[0]
    grad_rows = da_in_ref[...]
    dctx_s[...] = mm(grad_rows, wo_ref[...], NN).astype(BF16)
    gw_ref[:, 3 * LANES :] = mm(grad_rows, ctx_ref[...], TN).astype(BF16)
    dk_s[...] = jnp.zeros_like(dk_s)
    dv_s[...] = jnp.zeros_like(dv_s)
    scale = jnp.asarray(HD**-0.5, BF16)
    for index in range(span // block):
        keys = (index + 1) * block
        start = index * block
        query_rows = qkv_ref[start:keys, :LANES] * scale
        key_rows = qkv_ref[:keys, LANES : 2 * LANES]
        value_rows = qkv_ref[:keys, 2 * LANES :]
        context_grad = dctx_s[start:keys, :]
        row = lax.broadcasted_iota(jnp.int32, (keys, block), 0)
        column = start + lax.broadcasted_iota(jnp.int32, (keys, block), 1)
        allowed = (row <= column) & (row < length)
        dq_total = None
        for head in range(LANES // HD):
            lanes = head_lanes((block, LANES), head)
            masked_query = jnp.where(lanes, query_rows, jnp.zeros_like(query_rows))
            masked_grad = jnp.where(lanes, context_grad, jnp.zeros_like(context_grad))
            scores = jnp.where(allowed, mm(key_rows, masked_query, NT), -1e30)
            peak = jnp.max(scores, axis=0, keepdims=True)
            powers = jnp.exp(scores - peak)
            total = jnp.sum(powers, axis=0, keepdims=True)
            prob = powers * (1.0 / total)
            prob_grad = mm(value_rows, masked_grad, NT)
            inner = jnp.sum(prob * prob_grad, axis=0, keepdims=True)
            score_grad = (prob * (prob_grad - inner)).astype(BF16)
            dk_s[:keys, :] += mm(score_grad, masked_query, NN)
            dv_s[:keys, :] += mm(prob.astype(BF16), masked_grad, NN)
            dq_part = mm(score_grad, key_rows, TN)
            dq_total = dq_part if head == 0 else jnp.where(lanes, dq_part, dq_total)
        dq_s[start:keys, :] = dq_total * (HD**-0.5)
    cosine, sine = cos_ref[...], sin_ref[...]
    dq, dk = dq_s[...], dk_s[...]
    dq = (dq * cosine - partner(dq) * sine).astype(BF16)
    dk = (dk * cosine - partner(dk) * sine).astype(BF16)
    grads = jnp.concatenate([dq, dk, dv_s[...].astype(BF16)], axis=1)
    gw_ref[:, : 3 * LANES] = mm(a_ref[...], grads, TN).astype(BF16)
    part = mm(grads, w_ref[...], NT)

    @pl.when(pl.program_id(0) == 0)
    def _():
        da_ref[...] = part

    @pl.when(pl.program_id(0) > 0)
    def _():
        da_ref[...] += part


def attn_backward(length, attn_in, grad_attn, qkv_w, out_w, qkv_rot, context, cosine, sine):
    span, width = attn_in.shape
    pairs = qkv_w.shape[1] // (3 * LANES)
    return pl.pallas_call(
        functools.partial(attn_bwd_kernel, block=256),
        grid=(pairs,),
        in_specs=[
            pl.BlockSpec(memory_space=pltpu.SMEM),
            pl.BlockSpec((span, width), lambda i: (0, 0)),
            pl.BlockSpec((span, width), lambda i: (0, 0)),
            pl.BlockSpec((width, 3 * LANES), lambda i: (0, i)),
            pl.BlockSpec((width, LANES), lambda i: (0, i)),
            pl.BlockSpec((span, 3 * LANES), lambda i: (0, i)),
            pl.BlockSpec((span, LANES), lambda i: (0, i)),
            pl.BlockSpec((span, LANES), lambda i: (0, 0)),
            pl.BlockSpec((span, LANES), lambda i: (0, 0)),
        ],
        out_specs=[
            pl.BlockSpec((width, 4 * LANES), lambda i: (0, i)),
            pl.BlockSpec((span, width), lambda i: (0, 0)),
        ],
        out_shape=[
            jax.ShapeDtypeStruct((width, pairs * 4 * LANES), BF16),
            jax.ShapeDtypeStruct((span, width), F32),
        ],
        scratch_shapes=[
            pltpu.VMEM((span, LANES), BF16),
            pltpu.VMEM((span, LANES), F32),
            pltpu.VMEM((span, LANES), F32),
            pltpu.VMEM((span, LANES), F32),
        ],
        compiler_params=params(1),
        cost_estimate=cost(20e9, 16e6, 6e6),
        name="attn_bwd",
    )(length, attn_in, grad_attn, qkv_w, out_w, qkv_rot, context, cosine, sine)


def ffn_kernel(
    x_ref, d_ref, g_ref, wg_ref, wu_ref, wd_ref,
    y_ref, dx_ref, dg_ref, og_ref, ou_ref, od_ref, ag, au, ad,
):
    step = pl.program_id(0)
    rows = x_ref.shape[0]
    diagonal = lax.broadcasted_iota(jnp.int32, (rows, rows), 0) == lax.broadcasted_iota(
        jnp.int32, (rows, rows), 1
    )
    gate = jnp.sum(jnp.where(diagonal, g_ref[...], 0.0), axis=1, keepdims=True)
    x = x_ref[...]
    grad = d_ref[...].astype(F32)
    gate_pre = mm(x, wg_ref[...], NN)
    up_pre = mm(x, wu_ref[...], NN)
    sig = jax.nn.sigmoid(gate_pre)
    act = gate_pre * sig
    inner = (act * up_pre).astype(BF16)
    out = mm(inner, wd_ref[...], NT)
    gate_grad = jnp.sum(out * grad, axis=1, keepdims=True)
    dg_ref[...] = jnp.sum(jnp.where(diagonal, gate_grad, 0.0), axis=0, keepdims=True)
    y_ref[...] = (out * gate).astype(BF16)
    out_grad = (grad * gate).astype(BF16)
    inner_grad = mm(out_grad, wd_ref[...], NN)
    gate_pre_grad = (inner_grad * up_pre * (sig + act * (1.0 - sig))).astype(BF16)
    up_pre_grad = (inner_grad * act).astype(BF16)
    dx_ref[...] = (
        mm(gate_pre_grad, wg_ref[...], NT) + mm(up_pre_grad, wu_ref[...], NT)
    ).astype(BF16)

    @pl.when(step == 0)
    def _():
        ag[...] = jnp.zeros_like(ag)
        au[...] = jnp.zeros_like(au)
        ad[...] = jnp.zeros_like(ad)

    ag[...] += mm(x, gate_pre_grad, TN)
    au[...] += mm(x, up_pre_grad, TN)
    ad[...] += mm(out_grad, inner, TN)

    @pl.when(step == pl.num_programs(0) - 1)
    def _():
        og_ref[...] = ag[...].astype(BF16)
        ou_ref[...] = au[...].astype(BF16)
        od_ref[...] = ad[...].astype(BF16)


def ffn(rows_in, grad_in, gates, gate_w, up_w, down_w, name):
    count, width = rows_in.shape
    hidden = gate_w.shape[1]
    blocks, _, block = gates.shape
    token = pl.BlockSpec((block, width), lambda i: (i, 0))
    weight = pl.BlockSpec((width, hidden), lambda i: (0, 0), pipeline_mode=pl.Buffered(1))
    row = pl.BlockSpec((None, 1, block), lambda i: (i, 0, 0))
    return pl.pallas_call(
        ffn_kernel,
        grid=(blocks,),
        in_specs=[token, token, row, weight, weight, weight],
        out_specs=[token, token, row, weight, weight, weight],
        out_shape=[
            jax.ShapeDtypeStruct((count, width), BF16),
            jax.ShapeDtypeStruct((count, width), BF16),
            jax.ShapeDtypeStruct((blocks, 1, block), F32),
        ]
        + [jax.ShapeDtypeStruct((width, hidden), BF16)] * 3,
        scratch_shapes=[pltpu.VMEM((width, hidden), F32)] * 3,
        compiler_params=params(1),
        cost_estimate=cost(18 * count * width * hidden, 8 * count * width + 12 * width * hidden, count * hidden),
        name=name,
    )(rows_in, grad_in, gates, gate_w, up_w, down_w)


def dispatch_kernel(pos_ref, b_ref, x_ref):
    slots = x_ref.shape[0]
    tokens = b_ref.shape[0]
    slot = lax.broadcasted_iota(jnp.int32, (slots, tokens), 0)
    hot = jnp.where(slot == pos_ref[...], 1.0, 0.0).astype(BF16)
    x_ref[...] = mm(hot, b_ref[...], NN).astype(BF16)


def dispatch(places, rows, slots, name):
    experts, _, tokens = places.shape
    width = rows.shape[1]
    return pl.pallas_call(
        dispatch_kernel,
        grid=(experts,),
        in_specs=[
            pl.BlockSpec((None, 1, tokens), lambda i: (i, 0, 0)),
            pl.BlockSpec((tokens, width), lambda i: (0, 0)),
        ],
        out_specs=pl.BlockSpec((None, slots, width), lambda i: (i, 0, 0)),
        out_shape=jax.ShapeDtypeStruct((experts, slots, width), BF16),
        compiler_params=params(1),
        cost_estimate=cost(2 * experts * slots * tokens * width, 6e6),
        name=name,
    )(places, rows)


def gate_slots_kernel(pos_ref, gate_ref, out_ref):
    slots = out_ref.shape[1]
    tokens = pos_ref.shape[1]
    slot = lax.broadcasted_iota(jnp.int32, (slots, tokens), 0)
    column = jnp.sum(jnp.where(slot == pos_ref[...], gate_ref[...], 0.0), axis=1, keepdims=True)
    diagonal = lax.broadcasted_iota(jnp.int32, (slots, slots), 0) == lax.broadcasted_iota(
        jnp.int32, (slots, slots), 1
    )
    out_ref[...] = jnp.sum(jnp.where(diagonal, column, 0.0), axis=0, keepdims=True)


def gate_slots(places, gates, slots):
    experts, _, tokens = places.shape
    row = pl.BlockSpec((None, 1, tokens), lambda i: (i, 0, 0))
    return pl.pallas_call(
        gate_slots_kernel,
        grid=(experts,),
        in_specs=[row, row],
        out_specs=pl.BlockSpec((None, 1, slots), lambda i: (i, 0, 0)),
        out_shape=jax.ShapeDtypeStruct((experts, 1, slots), F32),
        compiler_params=params(1),
        cost_estimate=cost(4 * experts * slots * tokens, 1e5),
        name="gate_slots",
    )(places, gates)


def combine_hot(pos_ref, offset, experts, slots):
    tokens = pos_ref.shape[0]
    slot = lax.broadcasted_iota(jnp.int32, (tokens, slots), 1) + offset
    return jnp.concatenate(
        [
            jnp.where(slot == pos_ref[:, e : e + 1], 1.0, 0.0).astype(BF16)
            for e in range(experts)
        ],
        axis=1,
    )


def combine_kernel(core_ref, pos_ref, y_ref, base_ref, out_ref):
    experts, slots, width = y_ref.shape
    hot = combine_hot(pos_ref, core_ref[0] * slots, experts, slots)
    part = mm(hot, y_ref[...].reshape(experts * slots, width), NN)
    out_ref[...] = (part + base_ref[...].astype(F32)).astype(BF16)


def combine_grad_kernel(
    core_ref, pos_ref, y_ref, base_ref, gate_ref, dgate_ref, router_ref, out_ref, dl_ref
):
    experts, slots, width = y_ref.shape
    tokens = pos_ref.shape[0]
    hot = combine_hot(pos_ref, core_ref[0] * slots, experts, slots)
    part = mm(hot, y_ref[...].reshape(experts * slots, width), NN)
    slot = lax.broadcasted_iota(jnp.int32, (tokens, 2 * slots), 1)
    lane = lax.broadcasted_iota(jnp.int32, (tokens, experts), 1)
    gate_grad = jnp.zeros((tokens, experts), F32)
    for e in range(experts):
        found = jnp.sum(
            jnp.where(slot == pos_ref[:, e : e + 1], dgate_ref[e], 0.0), axis=1, keepdims=True
        )
        gate_grad = jnp.where(lane == e, found, gate_grad)
    gate = gate_ref[...]
    mean = jnp.sum(gate * gate_grad, axis=1, keepdims=True)
    logit_grad = gate * (gate_grad - mean)
    dl_ref[...] = logit_grad
    part += lax.dot_general(
        logit_grad, router_ref[...], NN, precision=HIGHEST, preferred_element_type=F32
    )
    out_ref[...] = (part + base_ref[...].astype(F32)).astype(BF16)


def combine(core, places, slots_in, base, extra=None, block=256):
    tokens, experts = places.shape
    _, slots, width = slots_in.shape
    token = pl.BlockSpec((block, width), lambda i: (i, 0))
    small = pl.BlockSpec((block, experts), lambda i: (i, 0))
    in_specs = [
        pl.BlockSpec(memory_space=pltpu.SMEM),
        small,
        pl.BlockSpec((experts, slots, width), lambda i: (0, 0, 0)),
        token,
    ]
    out_specs, out_shape = token, jax.ShapeDtypeStruct((tokens, width), BF16)
    kernel, args = combine_kernel, [core, places, slots_in, base]
    if extra is not None:
        gates, gate_grads, router = extra
        kernel = combine_grad_kernel
        in_specs += [
            small,
            pl.BlockSpec(gate_grads.shape, lambda i: (0, 0, 0)),
            pl.BlockSpec(router.shape, lambda i: (0, 0)),
        ]
        args += [gates, gate_grads, router]
        out_specs = [token, small]
        out_shape = [out_shape, jax.ShapeDtypeStruct((tokens, experts), F32)]
    return pl.pallas_call(
        kernel,
        grid=(tokens // block,),
        in_specs=in_specs,
        out_specs=out_specs,
        out_shape=out_shape,
        compiler_params=params(1),
        cost_estimate=cost(2 * tokens * experts * slots * width, 8e6),
        name="combine" if extra is None else "combine_grad",
    )(*args)


def swap(values):
    return lax.ppermute(values, "tensor", [(0, 1), (1, 0)])


def both_halves(own):
    other = swap(own)
    first = lax.axis_index("tensor") == 0
    return jnp.concatenate([jnp.where(first, own, other), jnp.where(first, other, own)], axis=0)


def half_of(values, index):
    rows = values.shape[0] // 2
    return lax.dynamic_slice_in_dim(values, index * rows, rows, 0)


def sum_halves(part):
    core = lax.axis_index("tensor")
    other = swap(half_of(part, 1 - core))
    return half_of(part, core).astype(F32) + other.astype(F32)


def to_all(values, groups=None):
    count = lax.axis_size("dp") if groups is None else len(groups[0])
    copies = jnp.broadcast_to(values[None], (count,) + values.shape)
    return lax.all_to_all(copies, "dp", 0, 0, axis_index_groups=groups, tiled=True)


def after(values, *earlier):
    return lax.optimization_barrier((values,) + earlier)[0]


def rms_parts(values):
    factor = lax.rsqrt(jnp.mean(values * values, axis=-1, keepdims=True) + EPS)
    return values * factor, factor


def norm_back(grad, normed, factor, gain):
    hat = grad * gain
    back = factor * (hat - normed * jnp.mean(hat * normed, axis=-1, keepdims=True))
    return back, jnp.sum(grad * normed, axis=0)


def per_device(
    layer_input, seq_lengths, expert_routes, w_query, w_key, w_value, w_output,
    gain_attn, gain_ffn, router_weight, expert_gate, expert_up, expert_down,
    shared_gate, shared_up, shared_down, out_cotangent,
):
    ranks = lax.axis_size("dp")
    core = lax.axis_index("tensor")
    _, own_len, width = layer_input.shape
    span = 2 * own_len
    shard = w_query.shape[0]
    pairs = w_query.shape[1] // LANES
    experts, hidden = expert_gate.shape[1:]
    capacity = 4 * span // experts
    slots = capacity // 2
    groups = [list(range(s, s + experts)) for s in range(0, ranks, experts)]

    qkv_own = jnp.stack([w_query, w_key, w_value], axis=1).reshape(shard, 3, pairs, LANES)
    qkv_own = qkv_own.transpose(0, 2, 1, 3).reshape(shard, pairs * 3 * LANES)
    small_own = jnp.concatenate(
        [gain_attn[:, None], gain_ffn[:, None], router_weight], axis=1
    )
    small_own = jnp.pad(small_own, ((0, 0), (0, LANES - small_own.shape[1])))
    first_own = jnp.concatenate([qkv_own, small_own], axis=1).astype(BF16)
    first_all = to_all(first_own).reshape(width, pairs * 3 * LANES + LANES)
    qkv_w = first_all[:, : pairs * 3 * LANES]
    small = first_all[:, pairs * 3 * LANES :]
    gain_one = small[:, 0].astype(F32)
    gain_two = small[:, 1].astype(F32)
    router_w = small[:, 2 : 2 + experts]

    routes = expert_routes.reshape(span, 2)
    names = jnp.arange(experts, dtype=jnp.int32)
    chosen = (routes[:, 0:1] == names[None, :]) | (routes[:, 1:2] == names[None, :])
    counts = jnp.cumsum(chosen.astype(jnp.int32), axis=0)
    places = jnp.where(chosen, counts - 1, -1)
    own_places = jnp.where(chosen, counts - 1 - core * slots, -1).T[:, None, :]
    core_arg = core.reshape(1).astype(jnp.int32)

    length = seq_lengths[0]
    valid = (core * own_len + jnp.arange(own_len, dtype=jnp.int32)) < length
    cotangent = out_cotangent[0].astype(F32) * valid.astype(F32)[:, None]
    grad_ffn = both_halves(cotangent.astype(BF16))
    grad_slots = dispatch(own_places, grad_ffn, slots, "dispatch_grad")
    grad_slots = after(grad_slots, first_all)
    grad_slots = lax.all_to_all(grad_slots, "dp", 0, 0, axis_index_groups=groups, tiled=True)
    grad_rows = grad_slots.reshape(experts * slots, width)
    grad_rows = jnp.concatenate([grad_rows, swap(grad_rows)], axis=0)

    expert_own = jnp.stack([expert_gate, expert_up, expert_down], axis=0).astype(BF16)
    expert_own = expert_own.transpose(2, 0, 1, 3).reshape(1, experts, 3 * shard, hidden)
    expert_own = jnp.broadcast_to(
        expert_own, (ranks // experts, experts, 3 * shard, hidden)
    ).reshape(ranks, 3 * shard, hidden)
    expert_own = after(expert_own, first_all)
    expert_all = lax.all_to_all(expert_own, "dp", 0, 0, tiled=True)
    expert_all = expert_all.reshape(ranks, 3, shard, hidden).transpose(1, 0, 2, 3)
    expert_all = expert_all.reshape(3, width, hidden)

    shared_own = jnp.concatenate(
        [w_output, shared_gate, shared_up, shared_down], axis=1
    ).astype(BF16)
    near = [list(range(s, s + 4)) for s in range(0, ranks, 4)]
    far = [list(range(s, ranks, 4)) for s in range(4)]
    shared_own = after(shared_own, first_all)
    shared_all = to_all(to_all(shared_own, far), near)
    heads_width = w_output.shape[1]
    shared_all = shared_all.reshape(4, ranks // 4, shard, heads_width + 3 * hidden)
    shared_all = shared_all.transpose(1, 0, 2, 3).reshape(width, heads_width + 3 * hidden)
    out_w = shared_all[:, :heads_width]
    sgate_w, sup_w, sdown_w = (
        shared_all[:, heads_width + k * hidden : heads_width + (k + 1) * hidden] for k in range(3)
    )

    half = HD // 2
    inverse = jnp.exp(jnp.arange(half, dtype=F32) * (-math.log(10000.0) / half))
    angles = jnp.arange(span, dtype=F32)[:, None] * inverse[None, :]
    cos_half, sin_half = jnp.cos(angles), jnp.sin(angles)
    cosine = jnp.concatenate([cos_half] * 4, axis=1)
    sine = jnp.concatenate([-sin_half, sin_half] * 2, axis=1)
    input_rows = layer_input[0].astype(F32)
    unit_one, factor_one = rms_parts(input_rows)
    attn_in = both_halves((unit_one * gain_one).astype(BF16))
    qkv_rot, context = attn_forward(seq_lengths, attn_in, qkv_w, cosine, sine)
    attn_part = mm(context, out_w, NT)
    hidden_rows = input_rows + sum_halves(attn_part)
    unit_two, factor_two = rms_parts(hidden_rows)
    ffn_in = both_halves((unit_two * gain_two).astype(BF16))

    logits = mm(ffn_in, router_w, NN)
    top = jnp.max(jnp.where(chosen, logits, -jnp.inf), axis=1, keepdims=True)
    powers = jnp.where(chosen, jnp.exp(logits - top), 0.0)
    gates = powers / jnp.sum(powers, axis=1, keepdims=True)

    x_slots = dispatch(own_places, ffn_in, slots, "dispatch_rows")
    x_slots = lax.all_to_all(x_slots, "dp", 0, 0, axis_index_groups=groups, tiled=True)
    g_slots = gate_slots(own_places, gates.T[:, None, :], slots)
    g_slots = lax.all_to_all(g_slots, "dp", 0, 0, axis_index_groups=groups, tiled=True)
    x_rows = x_slots.reshape(experts * slots, width)
    x_rows = jnp.concatenate([x_rows, swap(x_rows)], axis=0)
    g_rows = g_slots.reshape(1, experts * slots)
    g_rows = jnp.concatenate([g_rows, swap(g_rows)], axis=0)
    block = 512
    g_rows = g_rows.reshape(2 * experts * slots // block, 1, block)

    ones = jnp.ones((span // block, 1, block), F32)
    shared_y, shared_dx, _, shared_gg, shared_gu, shared_gd = ffn(
        ffn_in, grad_ffn, ones, sgate_w, sup_w, sdown_w, "ffn_shared"
    )
    shared_grads = jnp.concatenate([shared_gg, shared_gu, shared_gd], axis=1)
    shared_grads = lax.all_to_all(
        shared_grads.reshape(ranks, shard, 3 * hidden), "dp", 0, 0, tiled=True
    )

    y_rows, dx_rows, gate_grads, expert_gg, expert_gu, expert_gd = ffn(
        x_rows, grad_rows, g_rows, expert_all[0], expert_all[1], expert_all[2], "ffn_expert"
    )
    half_rows = experts * slots

    def back_home(rows):
        total = rows[:half_rows].astype(F32) + swap(rows[half_rows:]).astype(F32)
        total = total.astype(BF16).reshape(experts, slots, width)
        return lax.all_to_all(total, "dp", 0, 0, axis_index_groups=groups, tiled=True)

    dx_home = back_home(dx_rows)
    gate_grads = gate_grads.reshape(2, experts, slots).transpose(1, 0, 2)
    gate_grads = lax.all_to_all(gate_grads, "dp", 0, 0, axis_index_groups=groups, tiled=True)
    first = core == 0
    gate_grads = jnp.concatenate(
        [
            jnp.where(first, gate_grads[:, 0], gate_grads[:, 1]),
            jnp.where(first, gate_grads[:, 1], gate_grads[:, 0]),
        ],
        axis=1,
    )[:, None, :]
    y_rows = after(y_rows, dx_home)
    y_home = back_home(y_rows)
    expert_grads = jnp.stack([expert_gg, expert_gu, expert_gd], axis=0)
    expert_grads = expert_grads.reshape(3, ranks, shard, hidden).transpose(1, 0, 2, 3)
    expert_grads = after(expert_grads, dx_home)
    expert_grads = lax.all_to_all(expert_grads, "dp", 0, 0, tiled=True)

    db_part, logit_grads = combine(
        core_arg, places, dx_home, shared_dx,
        (gates, gate_grads, router_w.astype(F32).T),
    )
    grad_router = lax.dot_general(
        ffn_in.astype(F32), logit_grads, TN, precision=HIGHEST, preferred_element_type=F32
    )
    back_two, gain_two_grad = norm_back(sum_halves(db_part), unit_two, factor_two, gain_two)
    grad_hidden = cotangent + back_two
    grad_attn = both_halves(grad_hidden.astype(BF16))
    attn_grads, da_part = attn_backward(
        seq_lengths, attn_in, grad_attn, qkv_w, out_w, qkv_rot, context, cosine, sine
    )
    attn_grads = lax.all_to_all(
        attn_grads.reshape(ranks, shard, pairs * 4 * LANES), "dp", 0, 0, tiled=True
    )
    back_one, gain_one_grad = norm_back(
        sum_halves(da_part.astype(BF16)), unit_one, factor_one, gain_one
    )
    grad_input = (grad_hidden + back_one).astype(BF16)

    ffn_part = combine(core_arg, places, y_home, shared_y)
    layer_output = (hidden_rows + sum_halves(ffn_part)).astype(BF16)

    small_grads = jnp.concatenate(
        [gain_one_grad[:, None], gain_two_grad[:, None], grad_router], axis=1
    )
    small_grads = lax.all_to_all(
        small_grads.reshape(ranks, shard, 2 + experts), "dp", 0, 0, tiled=True
    )
    small_grads = jnp.sum(small_grads, axis=0)
    small_grads = small_grads + swap(small_grads)

    attn_grads = jnp.sum(attn_grads.astype(F32), axis=0).reshape(shard, pairs, 4, LANES)
    attn_grads = [attn_grads[:, :, k].reshape(shard, pairs * LANES) for k in range(4)]
    shared_grads = jnp.sum(shared_grads.astype(F32), axis=0)
    shared_grads = [shared_grads[:, k * hidden : (k + 1) * hidden] for k in range(3)]
    expert_grads = expert_grads.reshape(ranks // experts, experts, 3, shard, hidden)
    expert_grads = jnp.sum(expert_grads.astype(F32), axis=0)
    expert_grads = [expert_grads[:, k].transpose(1, 0, 2) for k in range(3)]
    return (
        layer_output[None], grad_input[None],
        attn_grads[0], attn_grads[1], attn_grads[2], attn_grads[3],
        small_grads[:, 0], small_grads[:, 1], small_grads[:, 2:],
        expert_grads[0], expert_grads[1], expert_grads[2],
        shared_grads[0], shared_grads[1], shared_grads[2],
    )


def solution(mesh):
    tokens = P("dp", "tensor", None)
    matrix = P("dp", "tensor")
    expert = P("dp", None, "tensor")
    in_specs = (
        (tokens, P("dp"), P("dp", None, None))
        + (matrix,) * 4
        + (P("dp"), P("dp"), P("dp", None))
        + (expert,) * 3
        + (matrix,) * 3
        + (tokens,)
    )
    out_specs = (
        (tokens, tokens)
        + (matrix,) * 4
        + (P("dp"), P("dp"), P("dp", None))
        + (expert,) * 3
        + (matrix,) * 3
    )
    return jax.shard_map(
        per_device, mesh=mesh, in_specs=in_specs, out_specs=out_specs, check_vma=False
    )
```

time: 3320 us -> 876 us (0.26)
  waiting for transfers between devices: 2350 us -> 345 us
  matrix products: 312 us -> 3.78 us
  blocking collectives: 292 us -> 67.8 us
  Pallas kernels: 0 us -> 196 us
  local copies, waits for them, and re-layouts: 230 us -> 55.9 us
  starting transfers between devices: 1.91 us -> 107 us
    reduce_scatter x14 -> x0, waiting for transfers between devices: 1850 us -> none  [the longest x1 368 us: per_device(): lax.psum_scatter(grad_down, 'dp', scatter_dimension=0, tiled=True)]
    all_gather x10 -> x0, waiting for transfers between devices: 501 us -> none  [the longest x1 140 us: fetch_weights(): lax.all_gather(expert_gate.astype(jnp.bfloat16), 'dp', axis=0, tiled=True)]
    all_to_all x0 -> x12, waiting for transfers between devices: none -> 326 us  [the longest x1 75.6 us: per_device(): lax.all_to_all(shared_grads.reshape(ranks, shard, 3 * hidden), 'dp', 0, 0...]
    dot_general x46 -> x3, matrix products: 308 us -> 3.78 us  [the longest x2 2.93 us: mm(): return lax.dot_general(left, right, dims, preferred_element_type=F32)]
    all_gather x5 -> x0, blocking collectives: 203 us -> none  [the longest x1 42 us: fetch_weights(): lax.all_gather(w_output.astype(jnp.bfloat16), 'dp', axis=0, tiled=True)]
    pallas_call x0 -> x9, Pallas kernels: none -> 196 us  [the longest x2 102 us: ffn(): pl.pallas_call(ffn_kernel, grid=(blocks,), in_specs=[token, token, row, w...]
    all_to_all x0 -> x12, starting transfers between devices: none -> 104 us  [the longest x2 27 us: back_home(): lax.all_to_all(total, 'dp', 0, 0, axis_index_groups=groups, tiled=True)]
    unnamed x2 -> x0, blocking collectives: 86.3 us -> none
  transfers between devices with their start and end apart: 25 -> 26, of which waited for: 17 -> 16; matrix products, arithmetic and copies ran while one was open for 13% -> 14% of each run, Pallas kernels for 0% -> 14%
where the time goes in v1:
time: 876 us; the launch traced here: 863 us
  waiting for transfers between devices  345 us (39%)
  Pallas kernels  196 us (22%)
  starting transfers between devices  107 us (12%)
  other arithmetic  85.7 us (10%)
  blocking collectives  67.8 us (8%)
  local copies, waits for them, and re-layouts  55.9 us (6%)
    pallas_call x2, Pallas kernels, ffn(): pl.pallas_call(ffn_kernel, grid=(blocks,), in_specs=[token, token, row, w...  102 us
    all_to_all x1, waiting for transfers between devices, per_device(): lax.all_to_all(shared_grads.reshape(ranks, shard, 3 * hidden), 'dp', 0, 0...  75.6 us
    all_to_all x2, waiting for transfers between devices, to_all(): lax.all_to_all(copies, 'dp', 0, 0, axis_index_groups=groups, tiled=True)  74.9 us
    all_to_all x1, waiting for transfers between devices, per_device(): expert_all = lax.all_to_all(expert_own, 'dp', 0, 0, tiled=True)  74.9 us
    all_to_all x1, blocking collectives, to_all(): lax.all_to_all(copies, 'dp', 0, 0, axis_index_groups=groups, tiled=True)  38.4 us
    all_to_all x2, waiting for transfers between devices, back_home(): lax.all_to_all(total, 'dp', 0, 0, axis_index_groups=groups, tiled=True)  35.6 us
    pallas_call x1, Pallas kernels, attn_backward(): pl.pallas_call(functools.partial(attn_bwd_kernel, block=256), grid=(pairs...  34.7 us
    all_to_all x1, blocking collectives, per_device(): lax.all_to_all(small_grads.reshape(ranks, shard, 2 + experts), 'dp', 0, 0...  29.4 us
  transfers between devices with their start and end apart: 26, of which 16 were waited for; matrix products, arithmetic and copies ran while one was open for 14% of the time, Pallas kernels for 14%

profile of v1, /device:TPU:0, one launch (start us, length us, event | category | flops | bytes accessed | tf_op | source)
XLA Modules:
  0.0 862.8 jit_solution(14128210454227163438)
XLA Ops:
  6.7 8.5 all-to-all-start
  15.3 40.7 %all-to-all-done = bf16[16,48,1280]{2,1,0:T(8,128)(2,1)S(1)} async-done(((bf16[16,48,1280]{2,1,0:T(8,128)(2,1)}), bf16[16,48,1280]{2,1,0:T(8,128)(2,1)S(1)}, u32[]{:S(2)}, u32[]{:S(2)}) %all-to-all-start) | async-done | bytes 1966112 | tf_op jit(solution)/shard_map/all_to_all | solution.py:432
  56.1 38.4 %all_to_all.70 = bf16[4,48,3456]{2,1,0:T(8,128)(2,1)S(1)} all-to-all(bf16[4,48,3456]{2,1,0:T(8,128)(2,1)S(1)} %broadcast_in_dim.41), channel_id=1, replica_groups={{0,8,16,24},{2,10,18,26},{4,12,20,28},{6,14,22,30},{1,9,17,25},{3,11,19..., dimensions={0} | all-to-all | bytes 2654208 | tf_op jit(solution)/shard_map/all_to_all | solution.py:432
  97.2 5.3 all-to-all-start.2
  117.5 7.6 dispatch_grad.1
  126.5 34.2 %all-to-all-done.2 = bf16[4,4,48,3456]{3,2,1,0:T(8,128)(2,1)} async-done(((bf16[4,4,48,3456]{3,2,1,0:T(8,128)(2,1)}), bf16[4,4,48,3456]{3,2,1,0:T(8,128)(2,1)}, u32[]{:S(2)}, u32[]{:S(2)}) %all-to-all-start.2) | async-done | bytes 5308448 | tf_op jit(solution)/shard_map/all_to_all | solution.py:432
  160.7 4.6 all-to-all-start.4
  168.2 17.1 %attn_fwd.1 = (bf16[1024,1152]{1,0:T(8,128)(2,1)}, bf16[1024,384]{1,0:T(8,128)(2,1)}) custom-call(s32[1]{0:T(128)} %copy.94.len_ref, bf16[1024,768]{1,0:T(8,128)(2,1)} %pad_maximum_fusion.4.a_ref, bf16[768,1152]{1,0:T(8,128)(2,1)} %slice.146.w_ref, f32[1024,128]{1,0:T(8,128)} %get-tuple-element.126.cos_ref, f32[1024,128]{1,0:T(8,128)} %get-tuple-element.127.sin_ref), custom_call_target="tpu_custom_call" | custom-call | flops 3422552064 | bytes 12000000 | tf_op jit(solution)/shard_map/attn_fwd/pallas_call | solution.py:87
  185.2 3.0 copy.51
  193.3 3.5 collective-permute-done.1
  206.6 4.8 gate_slots.1
  213.7 5.1 all-to-all-start.5
  218.8 7.5 dispatch_rows.1
  226.3 5.1 all-to-all-start.3
  239.3 29.4 %all-to-all-done.3 = bf16[8,256,768]{2,1,0:T(8,128)(2,1)} async-done(((bf16[8,256,768]{2,1,0:T(8,128)(2,1)}), bf16[8,256,768]{2,1,0:T(8,128)(2,1)}, u32[]{:S(2)}, u32[]{:S(2)}) %all-to-all-start.3) | async-done | bytes 3145760 | tf_op jit(solution)/shard_map/all_to_all | solution.py:544
  268.6 8.2 all-to-all-start.6
  277.5 5.1 collective-permute-done.6
  283.3 6.0 pad_maximum_fusion.1.d_ref
  289.3 74.9 %all-to-all-done.6 = bf16[16,144,1024]{2,1,0:T(8,128)(2,1)} async-done(((bf16[16,144,1024]{2,1,0:T(8,128)(2,1)}), bf16[16,144,1024]{2,1,0:T(8,128)(2,1)}, u32[]{:S(2)}, u32[]{:S(2)}) %all-to-all-start.6) | async-done | bytes 4718624 | tf_op jit(solution)/shard_map/all_to_all | solution.py:504
  364.1 4.7 fusion.41
  368.9 6.0 pad_maximum_fusion.x_ref
  374.8 77.6 %ffn_expert.1 = (bf16[4096,768]{1,0:T(8,128)(2,1)}, bf16[4096,768]{1,0:T(8,128)(2,1)}, f32[8,1,512]{2,1,0:T(1,128)}, bf16[768,1024]{1,0:T(8,128)(2,1)}, bf16[768...) custom-call(bf16[4096,768]{1,0:T(8,128)(2,1)} %pad_maximum_fusion.x_ref, bf16[4096,768]{1,0:T(8,128)(2,1)} %pad_maximum_fusion.1.d_ref, ...), custom_call_target="tpu_custom_call" | custom-call | flops 57982058496 | bytes 34603008 | tf_op jit(solution)/shard_map/ffn_expert/pallas_call | solution.py:258
  452.4 3.8 slice.124
  456.9 21.1 %all-to-all-start.9 = ((f32[8,2,256]{2,1,0:T(2,128)}), f32[8,2,256]{2,1,0:T(2,128)S(1)}, u32[]{:S(2)}, u32[]{:S(2)}) async-start(f32[8,2,256]{2,1,0:T(2,128)} %bitcast.141), calls=%async_computation.9 | async-start | bytes 32768 | tf_op jit(solution)/shard_map/all_to_all | solution.py:575
  478.1 5.3 add_convert_fusion.1
  483.7 5.3 all-to-all-start.7
  489.0 4.7 fusion.40
  494.2 24.7 %ffn_shared.1 = (bf16[1024,768]{1,0:T(8,128)(2,1)}, bf16[1024,768]{1,0:T(8,128)(2,1)}, f32[2,1,512]{2,1,0:T(1,128)}, bf16[768,1024]{1,0:T(8,128)(2,1)}, bf16[768...) custom-call(bf16[1024,768]{1,0:T(8,128)(2,1)} %pad_maximum_fusion.5.b_ref.x_ref, ...), custom_call_target="tpu_custom_call" | custom-call | flops 14495514624 | bytes 15728640 | tf_op jit(solution)/shard_map/ffn_shared/pallas_call | solution.py:258
  518.9 4.0 pad_maximum_fusion.2
  522.9 3.8 all-to-all-done.7.y_ref
  526.7 8.1 all-to-all-start.13
  537.0 5.6 collective-permute-done.8
  542.7 4.6 add_convert_fusion
  547.3 75.6 %all-to-all-done.13 = bf16[16,48,3072]{2,1,0:T(8,128)(2,1)} async-done(((bf16[16,48,3072]{2,1,0:T(8,128)(2,1)}), bf16[16,48,3072]{2,1,0:T(8,128)(2,1)}, u32[]{:S(2)}, u32[]{:S(2)}) %all-to-all-start.13) | async-done | bytes 4718624 | tf_op jit(solution)/shard_map/all_to_all | solution.py:559
  622.9 21.7 %all-to-all-start.8 = ((bf16[8,256,768]{2,1,0:T(8,128)(2,1)}), bf16[8,256,768]{2,1,0:T(8,128)(2,1)}, u32[]{:S(2)}, u32[]{:S(2)}) async-start(bf16[8,256,768]{2,1,0:T(8,128)(2,1)} %bitcast.150), calls=%async_computation.8 | async-start | bytes 6291456 | tf_op jit(solution)/shard_map/all_to_all | solution.py:571
  644.6 5.1 maximum_bitcast_fusion
  649.7 31.8 %all-to-all-done.8.y_ref = bf16[8,256,768]{2,1,0:T(8,128)(2,1)} async-done(((bf16[8,256,768]{2,1,0:T(8,128)(2,1)}), bf16[8,256,768]{2,1,0:T(8,128)(2,1)}, u32[]{:S(2)}, u32[]{:S(2)}) %all-to-all-start.8) | async-done | bytes 3145760 | tf_op jit(solution)/shard_map/all_to_all | solution.py:571
  681.5 6.1 all-to-all-start.12
  693.0 14.2 %combine_grad.1 = (bf16[1024,768]{1,0:T(8,128)(2,1)}, f32[1024,8]{1,0:T(8,128)}) custom-call(s32[1]{0:T(128)} %bitcast.8.core_ref, s32[1024,8]{1,0:T(8,128)} %bitcast_select_fusion.pos_ref, bf16[8,256,768]{2,1,0:T(8,128)(2,1)} %all-to-all-done.7.y_ref, bf16[1024,768]{1,0:T(8,128)(2,1)} %get-tuple-element.45.base_ref, f32[1024,8]{1,0:T(8,128)} %fusion.25.gate_ref, ...), custom_call_target="tpu_custom_call" | custom-call | flops 3221225472 | bytes 8000000 | tf_op jit(solution)/shard_map/combine_grad/pallas_call | solution.py:396
  708.5 7.5 combine.1
  725.8 34.7 %attn_bwd.1 = (bf16[768,1536]{1,0:T(8,128)(2,1)}, f32[1024,768]{1,0:T(8,128)}) custom-call(s32[1]{0:T(128)} %copy.94.len_ref, bf16[1024,768]{1,0:T(8,128)(2,1)} %pad_maximum_fusion.4.a_ref, bf16[1024,768]{1,0:T(8,128)(2,1)} %pad_maximum_fusion.7.da_in_ref, bf16[768,1152]{1,0:T(8,128)(2,1)} %slice.146.w_ref, bf16[768,384]{1,0:T(8,128)(2,1)} %slice.147.wo_ref, ...), custom_call_target="tpu_custom_call" | custom-call | flops 20000000000 | bytes 16000000 | tf_op jit(solution)/shard_map/attn_bwd/pallas_call | solution.py:171
  767.0 10.2 %all-to-all-done.12 = bf16[16,3,48,1024]{3,2,1,0:T(8,128)(2,1)} async-done(((bf16[16,3,48,1024]{3,2,1,0:T(8,128)(2,1)}), bf16[16,3,48,1024]{3,2,1,0:T(8,128)(2,1)}, u32[]{:S(2)}, u32[]{:S(2)}) %all-to-all-start.12) | async-done | bytes 4718624 | tf_op jit(solution)/shard_map/all_to_all | solution.py:589
  777.2 29.4 %all_to_all.71 = f32[16,1,480]{2,1,0:T(1,128)S(1)} all-to-all(f32[16,1,480]{2,1,0:T(1,128)S(1)} %reshape.324), channel_id=1, replica_groups=mesh['dp'=16,'tensor'=2] {'dp'}, dimensions={0} | all-to-all | bytes 61440 | tf_op jit(solution)/shard_map/all_to_all | solution.py:618
  806.6 4.6 all-to-all-start.10
  811.2 3.3 convert_reduce_fusion.1
  815.3 4.2 convert_reduce_fusion
  827.6 2.8 fusion.17
  831.5 25.5 %all-to-all-done.10 = bf16[16,48,1536]{2,1,0:T(8,128)(2,1)} async-done(((bf16[16,48,1536]{2,1,0:T(8,128)(2,1)}), bf16[16,48,1536]{2,1,0:T(8,128)(2,1)}, u32[]{:S(2)}, u32[]{:S(2)}) %all-to-all-start.10) | async-done | bytes 2359328 | tf_op jit(solution)/shard_map/all_to_all | solution.py:604
  (201 shorter events, 95.3 us)
Async XLA Ops:
  6.7 8.5 copy-start.22
  6.7 8.5 copy-start.16
  6.7 8.5 copy-start.17
  6.7 8.6 copy-start.18
  6.7 49.3 %all-to-all-start = ((bf16[16,48,1280]{2,1,0:T(8,128)(2,1)}), bf16[16,48,1280]{2,1,0:T(8,128)(2,1)S(1)}, u32[]{:S(2)}, u32[]{:S(2)}) async-start(bf16[16,48,1280]{2,1,0:T(8,128)(2,1)} %broadcast_in_dim.40), calls=%async_computation | async-start | bytes 3932160 | tf_op jit(solution)/shard_map/all_to_all | solution.py:432
  56.0 38.5 %copy-start.4 = (bf16[16,48,1280]{2,1,0:T(8,128)(2,1)}, bf16[16,48,1280]{2,1,0:T(8,128)(2,1)S(1)}, u32[]{:S(2)}) copy-start(bf16[16,48,1280]{2,1,0:T(8,128)(2,1)S(1)} %all-to-all-done) | copy-start | bytes 5898244
  97.2 6.1 copy-start.6
  97.2 63.5 %all-to-all-start.2 = ((bf16[4,4,48,3456]{3,2,1,0:T(8,128)(2,1)}), bf16[4,4,48,3456]{3,2,1,0:T(8,128)(2,1)}, u32[]{:S(2)}, u32[]{:S(2)}) async-start(bf16[4,4,48,3456]{3,2,1,0:T(8,128)(2,1)} %broadcast_in_dim.42), calls=%async_computation.2 | async-start | bytes 10616832 | tf_op jit(solution)/shard_map/all_to_all | solution.py:432
  102.5 3.8 copy-start
  103.2 11.5 %copy-start.25 = (f32[512]{0:T(512)}, f32[512]{0:T(512)S(1)}, u32[]{:S(2)}) copy-start(f32[512]{0:T(512)S(1)} %fusion.34) | copy-start | bytes 6148
  103.5 11.2 %collective-permute-start.4 = (bf16[512,768]{1,0:T(8,128)(2,1)S(1)}, bf16[512,768]{1,0:T(8,128)(2,1)}, u32[]{:S(2)}, u32[]{:S(2)}) collective-permute-start(bf16[512,768]{1,0:T(8,128)(2,1)S(1)} %fusion.13), channel_id=1, source_target_pairs={{0,1},{1,0},{2,3},{3,2},{4,5},{5,4},{6,7},{7,6},{8,9},{9,8},{10,11... | collective-permute-start | bytes 2359304 | tf_op jit(solution)/shard_map/ppermute | solution.py:409
  106.6 58.8 %copy-start.23 = (f32[512]{0:T(512)}, f32[512]{0:T(512)S(1)}, u32[]{:S(2)}) copy-start(f32[512]{0:T(512)S(1)} %add_rsqrt_fusion.1) | copy-start | bytes 6148
  111.2 54.1 %copy-start.20 = (f32[768]{0:T(1024)}, f32[768]{0:T(1024)S(1)}, u32[]{:S(2)}) copy-start(f32[768]{0:T(1024)S(1)} %get-tuple-element.79) | copy-start | bytes 9220
  112.3 53.0 %collective-permute-start = (bf16[512,768]{1,0:T(8,128)(2,1)}, bf16[512,768]{1,0:T(8,128)(2,1)}, u32[]{:S(2)}, u32[]{:S(2)}) collective-permute-start(bf16[512,768]{1,0:T(8,128)(2,1)} %fusion.4), channel_id=1, source_target_pairs={{0,1},{1,0},{2,3},{3,2},{4,5},{5,4},{6,7},{7,6},{8,9},{9,8},{10,11... | collective-permute-start | bytes 2359304 | tf_op jit(solution)/shard_map/ppermute | solution.py:409
  117.5 7.6 copy-start.5
  160.7 53.1 %all-to-all-start.4 = ((bf16[8,256,768]{2,1,0:T(8,128)(2,1)}), bf16[8,256,768]{2,1,0:T(8,128)(2,1)}, u32[]{:S(2)}, u32[]{:S(2)}) async-start(bf16[8,256,768]{2,1,0:T(8,128)(2,1)} %dispatch_grad.1), calls=%async_computation.4 | async-start | bytes 6291456 | tf_op jit(solution)/shard_map/all_to_all | solution.py:494
  185.2 5.4 copy-start.15
  193.3 3.5 collective-permute-start.1
  199.3 2.4 collective-permute-start.2
  202.1 9.3 %copy-start.9 = (bf16[512,768]{1,0:T(8,128)(2,1)}, bf16[512,768]{1,0:T(8,128)(2,1)S(1)}, u32[]{:S(2)}) copy-start(bf16[512,768]{1,0:T(8,128)(2,1)S(1)} %get-tuple-element.104) | copy-start | bytes 2359300
  213.7 12.6 %all-to-all-start.5 = ((f32[8,1,256]{2,1,0:T(1,128)}), f32[8,1,256]{2,1,0:T(1,128)S(1)}, u32[]{:S(2)}, u32[]{:S(2)}) async-start(f32[8,1,256]{2,1,0:T(1,128)} %gate_slots.1), calls=%async_computation.5 | async-start | bytes 16384 | tf_op jit(solution)/shard_map/all_to_all | solution.py:546
  226.3 42.3 %all-to-all-start.3 = ((bf16[8,256,768]{2,1,0:T(8,128)(2,1)}), bf16[8,256,768]{2,1,0:T(8,128)(2,1)}, u32[]{:S(2)}, u32[]{:S(2)}) async-start(bf16[8,256,768]{2,1,0:T(8,128)(2,1)} %dispatch_rows.1), calls=%async_computation.3 | async-start | bytes 6291456 | tf_op jit(solution)/shard_map/all_to_all | solution.py:544
  268.6 95.5 %all-to-all-start.6 = ((bf16[16,144,1024]{2,1,0:T(8,128)(2,1)}), bf16[16,144,1024]{2,1,0:T(8,128)(2,1)}, u32[]{:S(2)}, u32[]{:S(2)}) async-start(bf16[16,144,1024]{2,1,0:T(8,128)(2,1)} %bitcast.147), calls=%async_computation.6 | async-start | bytes 9437184 | tf_op jit(solution)/shard_map/all_to_all | solution.py:504
  276.9 6.4 collective-permute-start.5
  277.0 91.9 %collective-permute-start.3 = (bf16[2048,768]{1,0:T(8,128)(2,1)}, bf16[2048,768]{1,0:T(8,128)(2,1)}, u32[]{:S(2)}, u32[]{:S(2)}) collective-permute-start(bf16[2048,768]{1,0:T(8,128)(2,1)} %bitcast.17), channel_id=1, source_target_pairs={{0,1},{1,0},{2,3},{3,2},{4,5},{5,4},{6,7},{7,6},{8,9},{9,8},{10,11... | collective-permute-start | bytes 9437192 | tf_op jit(solution)/shard_map/ppermute | solution.py:409
  277.5 5.2 collective-permute-start.6
  452.4 3.8 copy-start.27
  456.2 21.8 %collective-permute-start.7 = (bf16[2048,768]{1,0:T(8,128)(2,1)}, bf16[2048,768]{1,0:T(8,128)(2,1)}, u32[]{:S(2)}, u32[]{:S(2)}) collective-permute-start(bf16[2048,768]{1,0:T(8,128)(2,1)} %slice.124), channel_id=1, source_target_pairs={{0,1},{1,0},{2,3},{3,2},{4,5},{5,4},{6,7},{7,6},{8,9},{9,8},{10,11... | collective-permute-start | bytes 9437192 | tf_op jit(solution)/shard_map/ppermute | solution.py:409
  456.9 26.8 %all-to-all-start.9 = ((f32[8,2,256]{2,1,0:T(2,128)}), f32[8,2,256]{2,1,0:T(2,128)S(1)}, u32[]{:S(2)}, u32[]{:S(2)}) async-start(f32[8,2,256]{2,1,0:T(2,128)} %bitcast.141), calls=%async_computation.9 | async-start | bytes 32768 | tf_op jit(solution)/shard_map/all_to_all | solution.py:575
  483.7 43.0 %all-to-all-start.7 = ((bf16[8,256,768]{2,1,0:T(8,128)(2,1)}), bf16[8,256,768]{2,1,0:T(8,128)(2,1)}, u32[]{:S(2)}, u32[]{:S(2)}) async-start(bf16[8,256,768]{2,1,0:T(8,128)(2,1)} %bitcast.149), calls=%async_computation.7 | async-start | bytes 6291456 | tf_op jit(solution)/shard_map/all_to_all | solution.py:571
  526.7 96.2 %all-to-all-start.13 = ((bf16[16,48,3072]{2,1,0:T(8,128)(2,1)}), bf16[16,48,3072]{2,1,0:T(8,128)(2,1)}, u32[]{:S(2)}, u32[]{:S(2)}) async-start(bf16[16,48,3072]{2,1,0:T(8,128)(2,1)} %bitcast.148), calls=%async_computation.13 | async-start | bytes 9437184 | tf_op jit(solution)/shard_map/all_to_all | solution.py:559
  536.9 5.7 collective-permute-start.8
  622.9 58.6 %all-to-all-start.8 = ((bf16[8,256,768]{2,1,0:T(8,128)(2,1)}), bf16[8,256,768]{2,1,0:T(8,128)(2,1)}, u32[]{:S(2)}, u32[]{:S(2)}) async-start(bf16[8,256,768]{2,1,0:T(8,128)(2,1)} %bitcast.150), calls=%async_computation.8 | async-start | bytes 6291456 | tf_op jit(solution)/shard_map/all_to_all | solution.py:571
  649.7 38.0 %copy-start.19 = (s32[8,8,128]{2,1,0:T(8,128)S(1)}, s32[8,8,128]{2,1,0:T(8,128)}, u32[]{:S(2)}) copy-start(s32[8,8,128]{2,1,0:T(8,128)} %get-tuple-element.89) | copy-start | bytes 98308
  681.5 95.7 %all-to-all-start.12 = ((bf16[16,3,48,1024]{3,2,1,0:T(8,128)(2,1)}), bf16[16,3,48,1024]{3,2,1,0:T(8,128)(2,1)}, u32[]{:S(2)}, u32[]{:S(2)}) async-start(bf16[16,3,48,1024]{3,2,1,0:T(8,128)(2,1)} %maximum_bitcast_fusion), calls=%async_computation.12 | async-start | bytes 9437184 | tf_op jit(solution)/shard_map/all_to_all | solution.py:589
  708.4 9.5 %collective-permute-start.10 = (bf16[512,768]{1,0:T(8,128)(2,1)S(1)}, bf16[512,768]{1,0:T(8,128)(2,1)S(1)}, u32[]{:S(2)}, u32[]{:S(2)}) collective-permute-start(bf16[512,768]{1,0:T(8,128)(2,1)S(1)} %constant_dynamic-slice_fusion.1), channel_id=1, source_target_pairs={{0,1},{1,0},{2,3},{3,2},{4,5},{5,4},{6,7},{7,6},{8,9},{9,8},{10,11... | collective-permute-start | bytes 2359304 | tf_op jit(solution)/shard_map/ppermute | solution.py:409
  717.3 2.5 copy-start.7
  717.4 2.5 copy-start.13
  717.4 2.5 copy-start.26
  717.4 2.5 collective-permute-start.9
  722.1 2.3 collective-permute-start.11
  760.4 3.4 copy-start.29
  763.5 2.5 copy-start.1
  763.5 2.5 copy-start.21
  763.5 2.5 copy-start.24
  763.5 2.5 collective-permute-start.12
  806.6 50.4 %all-to-all-start.10 = ((bf16[16,48,1536]{2,1,0:T(8,128)(2,1)}), bf16[16,48,1536]{2,1,0:T(8,128)(2,1)}, u32[]{:S(2)}, u32[]{:S(2)}) async-start(bf16[16,48,1536]{2,1,0:T(8,128)(2,1)} %bitcast.156), calls=%async_computation.10 | async-start | bytes 4718592 | tf_op jit(solution)/shard_map/all_to_all | solution.py:604
  827.5 2.9 collective-permute-start.13
  (8 other events, 14.0 us)

commit v2 on v1

--- a/solution.py
+++ b/solution.py
@@ -33,6 +33,167 @@
 
 def cost(flops, nbytes, trans=0):
     return pl.CostEstimate(flops=int(flops), bytes_accessed=int(nbytes), transcendentals=int(trans))
+
+
+def flip(index, offset):
+    bit = 1
+    while bit <= offset:
+        if offset & bit:
+            index = index + bit - 2 * bit * lax.rem(lax.div(index, bit), 2)
+        bit *= 2
+    return index
+
+
+def device(rank, core):
+    return {"dp": rank, "tensor": core}
+
+
+def greet(devices):
+    barrier = pltpu.get_barrier_semaphore()
+    for target in devices:
+        pl.semaphore_signal(barrier, inc=1, device_id=target, device_id_type=pl.DeviceIdType.MESH)
+    pl.semaphore_wait(barrier, len(devices))
+
+
+def remote(src, dst, send, recv, target):
+    return pltpu.make_async_remote_copy(
+        src_ref=src, dst_ref=dst, send_sem=send, recv_sem=recv,
+        device_id=target, device_id_type=pl.DeviceIdType.MESH,
+    )
+
+
+def gather_kernel(own_ref, out_ref, own_sem, z_send, z_recv, s_send, s_recv, f_send, f_recv, *, cut):
+    me, core = lax.axis_index("dp"), lax.axis_index("tensor")
+    z = lax.div(me, 4)
+    x_rank, y_rank = flip(me, 1), flip(me, 2)
+    up, down = lax.min(me + 4, 15), lax.max(me - 4, 0)
+    barrier = pltpu.get_barrier_semaphore()
+
+    def hello(target):
+        pl.semaphore_signal(
+            barrier, inc=1, device_id=device(target, core), device_id_type=pl.DeviceIdType.MESH
+        )
+
+    hello(x_rank)
+    hello(y_rank)
+    pl.when(z < 3)(lambda: hello(up))
+    pl.when(z > 0)(lambda: hello(down))
+    pl.semaphore_wait(barrier, 2 + lax.min(z, 1) + lax.min(3 - z, 1))
+
+    own = pltpu.make_async_copy(own_ref, out_ref.at[me], own_sem)
+    own.start()
+
+    def z_copy(rank, step, upward):
+        src = own_ref if step == 1 else out_ref.at[rank]
+        index = step - 1 if upward else step + 2
+        return remote(
+            src, out_ref.at[rank], z_send.at[index], z_recv.at[index],
+            device(up if upward else down, core),
+        )
+
+    def side_copy(rank, place, axis):
+        src = own_ref if place == 0 else out_ref.at[rank]
+        return remote(
+            src, out_ref.at[rank], s_send.at[axis, place], s_recv.at[axis, place],
+            device(x_rank if axis == 0 else y_rank, core),
+        )
+
+    def onward_copy(rank, place, axis):
+        columns = pl.ds(0, cut) if axis == 0 else pl.ds(cut, own_ref.shape[1] - cut)
+        return remote(
+            out_ref.at[rank, :, columns], out_ref.at[rank, :, columns],
+            f_send.at[axis, place], f_recv.at[axis, place],
+            device(y_rank if axis == 0 else x_rank, core),
+        )
+
+    def has(place):
+        if place == 0:
+            return None
+        return z >= place if place <= 3 else z + (place - 3) <= 3
+
+    def rank_at(place):
+        return me - 4 * place if place <= 3 else me + 4 * (place - 3)
+
+    def guarded(condition, body):
+        if condition is None:
+            body()
+        else:
+            pl.when(condition)(body)
+
+    def sides(place):
+        for axis in range(2):
+            side_copy(rank_at(place), place, axis).start()
+
+    def onward(place):
+        for axis in range(2):
+            rank = flip(rank_at(place), 1 + axis)
+            side_copy(rank, place, axis).wait_recv()
+            onward_copy(rank, place, axis).start()
+
+    def arrive(place):
+        step = place if place <= 3 else place - 3
+        upward = place <= 3
+        rank = rank_at(place)
+        z_copy(rank, step, upward).wait_recv()
+        if step < 3:
+            further = z < 3 if upward else z > 0
+            pl.when(further)(lambda: z_copy(rank, step + 1, upward).start())
+        sides(place)
+
+    pl.when(z < 3)(lambda: z_copy(me, 1, True).start())
+    pl.when(z > 0)(lambda: z_copy(me, 1, False).start())
+    sides(0)
+    order = (0, 1, 4, 2, 5, 3, 6)
+    for turn, place in enumerate(order):
+        if place > 0:
+            guarded(has(place), functools.partial(arrive, place))
+        if turn >= 2:
+            guarded(has(order[turn - 2]), functools.partial(onward, order[turn - 2]))
+    for place in order[-2:]:
+        guarded(has(place), functools.partial(onward, place))
+
+    def finish(place):
+        for axis in range(2):
+            rank = flip(rank_at(place), 1 + axis)
+            side_copy(rank_at(place), place, axis).wait_send()
+            onward_copy(rank, place, axis).wait_send()
+            onward_copy(flip(rank_at(place), 3), place, axis).wait_recv()
+
+    for place in order:
+        guarded(has(place), functools.partial(finish, place))
+    for step in range(1, 4):
+        pl.when((z < 3) & (z >= step - 1))(
+            lambda step=step: z_copy(me - 4 * (step - 1), step, True).wait_send()
+        )
+        pl.when((z > 0) & (z + step - 1 <= 3))(
+            lambda step=step: z_copy(me + 4 * (step - 1), step, False).wait_send()
+        )
+    own.wait()
+
+
+def gather_all(own):
+    ranks = lax.axis_size("dp")
+    rows, width = own.shape
+    if ranks != 16:
+        return to_all(own)
+    return pl.pallas_call(
+        functools.partial(gather_kernel, cut=width // 2 // LANES * LANES),
+        in_specs=[pl.BlockSpec(memory_space=pl.ANY)],
+        out_specs=pl.BlockSpec(memory_space=pl.ANY),
+        out_shape=jax.ShapeDtypeStruct((ranks, rows, width), own.dtype),
+        scratch_shapes=[
+            pltpu.SemaphoreType.DMA,
+            pltpu.SemaphoreType.DMA((6,)),
+            pltpu.SemaphoreType.DMA((6,)),
+            pltpu.SemaphoreType.DMA((2, 7)),
+            pltpu.SemaphoreType.DMA((2, 7)),
+            pltpu.SemaphoreType.DMA((2, 7)),
+            pltpu.SemaphoreType.DMA((2, 7)),
+        ],
+        compiler_params=pltpu.CompilerParams(collective_id=1, has_side_effects=True),
+        cost_estimate=cost(1e6, 60e6),
+        name="gather_attn",
+    )(own)
 
 
 def partner(values):
@@ -202,127 +363,306 @@
     )(length, attn_in, grad_attn, qkv_w, out_w, qkv_rot, context, cosine, sine)
 
 
-def ffn_kernel(
-    x_ref, d_ref, g_ref, wg_ref, wu_ref, wd_ref,
-    y_ref, dx_ref, dg_ref, og_ref, ou_ref, od_ref, ag, au, ad,
-):
-    step = pl.program_id(0)
-    rows = x_ref.shape[0]
-    diagonal = lax.broadcasted_iota(jnp.int32, (rows, rows), 0) == lax.broadcasted_iota(
-        jnp.int32, (rows, rows), 1
-    )
-    gate = jnp.sum(jnp.where(diagonal, g_ref[...], 0.0), axis=1, keepdims=True)
-    x = x_ref[...]
-    grad = d_ref[...].astype(F32)
-    gate_pre = mm(x, wg_ref[...], NN)
-    up_pre = mm(x, wu_ref[...], NN)
+def column_of(row):
+    count = row.shape[1]
+    shape = (count, count)
+    same = lax.broadcasted_iota(jnp.int32, shape, 0) == lax.broadcasted_iota(jnp.int32, shape, 1)
+    return jnp.sum(jnp.where(same, row, 0.0), axis=1, keepdims=True)
+
+
+def row_of(column):
+    count = column.shape[0]
+    shape = (count, count)
+    same = lax.broadcasted_iota(jnp.int32, shape, 0) == lax.broadcasted_iota(jnp.int32, shape, 1)
+    return jnp.sum(jnp.where(same, column, 0.0), axis=0, keepdims=True)
+
+
+def ffn_block(x, grad, gate, gate_w, up_w, down_w, sums):
+    gate_pre = mm(x, gate_w, NN)
+    up_pre = mm(x, up_w, NN)
     sig = jax.nn.sigmoid(gate_pre)
     act = gate_pre * sig
     inner = (act * up_pre).astype(BF16)
-    out = mm(inner, wd_ref[...], NT)
-    gate_grad = jnp.sum(out * grad, axis=1, keepdims=True)
-    dg_ref[...] = jnp.sum(jnp.where(diagonal, gate_grad, 0.0), axis=0, keepdims=True)
-    y_ref[...] = (out * gate).astype(BF16)
-    out_grad = (grad * gate).astype(BF16)
-    inner_grad = mm(out_grad, wd_ref[...], NN)
+    out = mm(inner, down_w, NT)
+    gate_grad, out_grad = None, grad
+    if gate is not None:
+        wide = grad.astype(F32)
+        gate_grad = jnp.sum(out * wide, axis=1, keepdims=True)
+        out = out * gate
+        out_grad = (wide * gate).astype(BF16)
+    inner_grad = mm(out_grad, down_w, NN)
     gate_pre_grad = (inner_grad * up_pre * (sig + act * (1.0 - sig))).astype(BF16)
     up_pre_grad = (inner_grad * act).astype(BF16)
-    dx_ref[...] = (
-        mm(gate_pre_grad, wg_ref[...], NT) + mm(up_pre_grad, wu_ref[...], NT)
-    ).astype(BF16)
+    row_grad = mm(gate_pre_grad, gate_w, NT) + mm(up_pre_grad, up_w, NT)
+    sums[0][...] += mm(x, gate_pre_grad, TN)
+    sums[1][...] += mm(x, up_pre_grad, TN)
+    sums[2][...] += mm(out_grad, inner, TN)
+    return out, row_grad, gate_grad
+
+
+def slots_kernel(
+    places_ref, gates_ref, b_ref, d_ref, wg_ref, wu_ref, wd_ref,
+    xr, dr, gr, y_ref, dx_ref, og_ref, ou_ref, od_ref,
+    xs, ds, gs, ag, au, ad, send, recv, core_send, core_recv, local, *, block,
+):
+    me, core = lax.axis_index("dp"), lax.axis_index("tensor")
+    experts, slots, width = xs.shape
+    mine = lax.rem(me, experts)
+    other = device(me, 1 - core)
+    greet([device(flip(me, k), core) for k in range(1, experts)] + [other])
+    tokens = b_ref.shape[0]
+    slot = lax.broadcasted_iota(jnp.int32, (slots, tokens), 0)
+    outs, ins = (xr, dr, gr), (xs, ds, gs)
+
+    def copy(k, part):
+        return remote(
+            ins[part].at[k], outs[part].at[k, 0], send.at[part, k], recv.at[part, k],
+            device(flip(me, k), core),
+        )
+
+    def core_copy(k, part):
+        src = ins[part].at[0] if k == 0 else outs[part].at[k, 0]
+        return remote(
+            src, outs[part].at[k, 1], core_send.at[part, k], core_recv.at[part, k], other
+        )
+
+    def own_copy(part):
+        return pltpu.make_async_copy(ins[part].at[0], outs[part].at[0, 0], local.at[part])
+
+    order = tuple(sorted(range(1, experts), key=lambda k: (bin(k).count("1"), k)))
+    for k in order + (0,):
+        target = flip(mine, k)
+        found = slot == places_ref[target]
+        hot = jnp.where(found, 1.0, 0.0).astype(BF16)
+        xs[k] = mm(hot, b_ref[...], NN).astype(BF16)
+        ds[k] = mm(hot, d_ref[...], NN).astype(BF16)
+        gate = jnp.sum(jnp.where(found, gates_ref[target], 0.0), axis=1, keepdims=True)
+        gs[k] = jnp.broadcast_to(row_of(gate), (8, slots))
+        for part in range(3):
+            if k:
+                copy(k, part).start()
+            else:
+                own_copy(part).start()
+                core_copy(k, part).start()
+    for total in (ag, au, ad):
+        total[...] = jnp.zeros_like(total)
+
+    def shared(index, carry):
+        rows = pl.ds(index * block, block)
+        out, row_grad, _ = ffn_block(
+            b_ref[rows, :], d_ref[rows, :], None, wg_ref[...], wu_ref[...], wd_ref[...],
+            (ag, au, ad),
+        )
+        y_ref[rows, :] = out.astype(BF16)
+        dx_ref[rows, :] = row_grad.astype(BF16)
+        return carry
+
+    lax.fori_loop(0, tokens // block, shared, 0)
+    og_ref[...] = ag[...].astype(BF16)
+    ou_ref[...] = au[...].astype(BF16)
+    od_ref[...] = ad[...].astype(BF16)
+    for k in order:
+        for part in range(3):
+            copy(k, part).wait_recv()
+            core_copy(k, part).start()
+    for part in range(3):
+        own_copy(part).wait()
+        for k in range(experts):
+            core_copy(k, part).wait()
+            if k:
+                copy(k, part).wait_send()
+
+
+def slots_and_shared(places, gates, rows, grads, shared_w, slots, block):
+    experts, _, tokens = places.shape
+    width = rows.shape[1]
+    hidden = shared_w.shape[1] // 3
+    vmem = pl.BlockSpec(memory_space=pltpu.VMEM)
+    far = pl.BlockSpec(memory_space=pl.ANY)
+    one = pl.Buffered(1)
+
+    def whole(shape):
+        return pl.BlockSpec(shape, lambda i: (0,) * len(shape), pipeline_mode=one)
+
+    weights = [
+        pl.BlockSpec((width, hidden), lambda i, k=k: (0, k), pipeline_mode=one) for k in range(3)
+    ]
+    return pl.pallas_call(
+        functools.partial(slots_kernel, block=block),
+        grid=(1,),
+        in_specs=[whole(places.shape)] * 2 + [whole(rows.shape)] * 2 + weights,
+        out_specs=[far] * 3 + [whole(rows.shape)] * 2 + [whole((width, hidden))] * 3,
+        out_shape=[
+            jax.ShapeDtypeStruct((experts, 2, slots, width), BF16),
+            jax.ShapeDtypeStruct((experts, 2, slots, width), BF16),
+            jax.ShapeDtypeStruct((experts, 2, 8, slots), F32),
+        ]
+        + [jax.ShapeDtypeStruct(rows.shape, BF16)] * 2
+        + [jax.ShapeDtypeStruct((width, hidden), BF16)] * 3,
+        scratch_shapes=[
+            pltpu.VMEM((experts, slots, width), BF16),
+            pltpu.VMEM((experts, slots, width), BF16),
+            pltpu.VMEM((experts, 8, slots), F32),
+        ]
+        + [pltpu.VMEM((width, hidden), F32)] * 3
+        + [pltpu.SemaphoreType.DMA((3, experts))] * 4
+        + [pltpu.SemaphoreType.DMA((3,))],
+        compiler_params=pltpu.CompilerParams(
+            collective_id=2, has_side_effects=True, vmem_limit_bytes=VMEM_LIMIT,
+            dimension_semantics=("arbitrary",),
+        ),
+        cost_estimate=cost(18 * tokens * width * hidden + 4 * experts * slots * tokens * width, 40e6),
+        name="slots_shared",
+    )(places, gates, rows, grads, shared_w, shared_w, shared_w)
+
+
+def expert_kernel(
+    x_ref, d_ref, g_ref, wg_ref, wu_ref, wd_ref,
+    y_home, dx_home, dg_home, og_ref,
+    ag, au, ad, own_y, own_dx, ys, dxs, yp, dxp, yt, dxt, dgs,
+    core_send, core_recv, send, recv, local, *, experts,
+):
+    step = pl.program_id(0)
+    block = experts - 1 - step
+    me, core = lax.axis_index("dp"), lax.axis_index("tensor")
+    mine = lax.rem(me, experts)
+    other = device(me, 1 - core)
+    slots = x_ref.shape[1]
+    width = x_ref.shape[2]
+    shape = (width, wg_ref.shape[-1])
+
+    def rank_at(k):
+        total, bit = me - mine, 1
+        while bit < experts:
+            total += bit * lax.rem(lax.div(mine, bit) + lax.div(k, bit), 2)
+            bit *= 2
+        return total
+
+    def core_copy(k, part):
+        src, dst = ((ys, yp), (dxs, dxp))[part]
+        return remote(
+            src.at[lax.rem(k, 2)], dst.at[k], core_send.at[part, k], core_recv.at[part, k], other
+        )
+
+    def home_copy(k, part):
+        src, dst = ((yt, y_home), (dxt, dx_home), (dgs, dg_home))[part]
+        return remote(
+            src.at[k], dst.at[mine], send.at[part, k], recv.at[part, k],
+            device(rank_at(k), core),
+        )
+
+    def own_copy(part):
+        src, dst = ((yt, y_home), (dxt, dx_home), (dgs, dg_home))[part]
+        return pltpu.make_async_copy(src.at[0], dst.at[mine], local.at[part])
+
+    def go_home(k, part):
+        @pl.when(k == 0)
+        def _():
+            own_copy(part).start()
+
+        @pl.when(k > 0)
+        def _():
+            home_copy(k, part).start()
 
     @pl.when(step == 0)
     def _():
-        ag[...] = jnp.zeros_like(ag)
-        au[...] = jnp.zeros_like(au)
-        ad[...] = jnp.zeros_like(ad)
-
-    ag[...] += mm(x, gate_pre_grad, TN)
-    au[...] += mm(x, up_pre_grad, TN)
-    ad[...] += mm(out_grad, inner, TN)
-
-    @pl.when(step == pl.num_programs(0) - 1)
+        greet([device(flip(me, k), core) for k in range(1, experts)] + [other])
+        for total in (ag, au, ad):
+            total[...] = jnp.zeros_like(total)
+
+    def settle(k):
+        for part in (1, 0):
+            core_copy(k, part).wait_recv()
+            own, shared, total = ((own_y, yp, yt), (own_dx, dxp, dxt))[part]
+            total[k] = (own[...] + shared[k].astype(F32)).astype(BF16)
+            go_home(k, part)
+
+    @pl.when(step < experts)
     def _():
-        og_ref[...] = ag[...].astype(BF16)
-        ou_ref[...] = au[...].astype(BF16)
-        od_ref[...] = ad[...].astype(BF16)
-
-
-def ffn(rows_in, grad_in, gates, gate_w, up_w, down_w, name):
-    count, width = rows_in.shape
-    hidden = gate_w.shape[1]
-    blocks, _, block = gates.shape
-    token = pl.BlockSpec((block, width), lambda i: (i, 0))
-    weight = pl.BlockSpec((width, hidden), lambda i: (0, 0), pipeline_mode=pl.Buffered(1))
-    row = pl.BlockSpec((None, 1, block), lambda i: (i, 0, 0))
+        gate = column_of(jnp.concatenate([g_ref[0, 0:1, :], g_ref[1, 0:1, :]], axis=1))
+        out, row_grad, gate_grad = ffn_block(
+            x_ref[...].reshape(2 * slots, width), d_ref[...].reshape(2 * slots, width), gate,
+            wg_ref[...].reshape(shape), wu_ref[...].reshape(shape), wd_ref[...].reshape(shape),
+            (ag, au, ad),
+        )
+
+        @pl.when(step >= 1)
+        def _():
+            settle(block + 1)
+
+        for part in (1, 0):
+
+            @pl.when(step >= 2)
+            def _():
+                core_copy(block + 2, part).wait_send()
+
+            own, half = ((own_y, ys), (own_dx, dxs))[part]
+            value = (out, row_grad)[part]
+            own[...] = value[:slots]
+            half[lax.rem(block, 2)] = value[slots:].astype(BF16)
+            core_copy(block, part).start()
+        dgs[block] = jnp.broadcast_to(row_of(gate_grad), (8, 2 * slots))
+        go_home(block, 2)
+
+    @pl.when(step == experts)
+    def _():
+        settle(block + 1)
+        for index, total in enumerate((ag, au, ad)):
+            og_ref[:, index] = total[...].astype(BF16).reshape(og_ref.shape[0], *og_ref.shape[2:])
+        for part in (0, 1):
+            for k in (0, 1):
+                core_copy(k, part).wait_send()
+        for part in range(3):
+            own_copy(part).wait()
+            for k in range(1, experts):
+                home_copy(k, part).wait()
+
+
+def expert_ffn(x_slots, d_slots, g_slots, weights):
+    experts, _, slots, width = x_slots.shape
+    parts, _, shard, hidden = weights.shape
+    far = pl.BlockSpec(memory_space=pl.ANY)
+    one = pl.Buffered(1)
+
+    def group(shape):
+        return pl.BlockSpec(
+            (None,) + shape, lambda i: (jnp.maximum(experts - 1 - i, 0),) + (0,) * len(shape)
+        )
+
+    rows = group((2, slots, width))
+    matrices = [
+        pl.BlockSpec(
+            (parts, None, shard, hidden), lambda i, k=k: (0, k, 0, 0), pipeline_mode=one
+        )
+        for k in range(3)
+    ]
     return pl.pallas_call(
-        ffn_kernel,
-        grid=(blocks,),
-        in_specs=[token, token, row, weight, weight, weight],
-        out_specs=[token, token, row, weight, weight, weight],
+        functools.partial(expert_kernel, experts=experts),
+        grid=(experts + 1,),
+        in_specs=[rows, rows, group((2, 8, slots))] + matrices,
+        out_specs=[far, far, far]
+        + [pl.BlockSpec(weights.shape, lambda i: (0, 0, 0, 0), pipeline_mode=one)],
         out_shape=[
-            jax.ShapeDtypeStruct((count, width), BF16),
-            jax.ShapeDtypeStruct((count, width), BF16),
-            jax.ShapeDtypeStruct((blocks, 1, block), F32),
-        ]
-        + [jax.ShapeDtypeStruct((width, hidden), BF16)] * 3,
-        scratch_shapes=[pltpu.VMEM((width, hidden), F32)] * 3,
-        compiler_params=params(1),
-        cost_estimate=cost(18 * count * width * hidden, 8 * count * width + 12 * width * hidden, count * hidden),
-        name=name,
-    )(rows_in, grad_in, gates, gate_w, up_w, down_w)
-
-
-def dispatch_kernel(pos_ref, b_ref, x_ref):
-    slots = x_ref.shape[0]
-    tokens = b_ref.shape[0]
-    slot = lax.broadcasted_iota(jnp.int32, (slots, tokens), 0)
-    hot = jnp.where(slot == pos_ref[...], 1.0, 0.0).astype(BF16)
-    x_ref[...] = mm(hot, b_ref[...], NN).astype(BF16)
-
-
-def dispatch(places, rows, slots, name):
-    experts, _, tokens = places.shape
-    width = rows.shape[1]
-    return pl.pallas_call(
-        dispatch_kernel,
-        grid=(experts,),
-        in_specs=[
-            pl.BlockSpec((None, 1, tokens), lambda i: (i, 0, 0)),
-            pl.BlockSpec((tokens, width), lambda i: (0, 0)),
+            jax.ShapeDtypeStruct((experts, slots, width), BF16),
+            jax.ShapeDtypeStruct((experts, slots, width), BF16),
+            jax.ShapeDtypeStruct((experts, 8, 2 * slots), F32),
+            jax.ShapeDtypeStruct(weights.shape, BF16),
         ],
-        out_specs=pl.BlockSpec((None, slots, width), lambda i: (i, 0, 0)),
-        out_shape=jax.ShapeDtypeStruct((experts, slots, width), BF16),
-        compiler_params=params(1),
-        cost_estimate=cost(2 * experts * slots * tokens * width, 6e6),
-        name=name,
-    )(places, rows)
-
-
-def gate_slots_kernel(pos_ref, gate_ref, out_ref):
-    slots = out_ref.shape[1]
-    tokens = pos_ref.shape[1]
-    slot = lax.broadcasted_iota(jnp.int32, (slots, tokens), 0)
-    column = jnp.sum(jnp.where(slot == pos_ref[...], gate_ref[...], 0.0), axis=1, keepdims=True)
-    diagonal = lax.broadcasted_iota(jnp.int32, (slots, slots), 0) == lax.broadcasted_iota(
-        jnp.int32, (slots, slots), 1
-    )
-    out_ref[...] = jnp.sum(jnp.where(diagonal, column, 0.0), axis=0, keepdims=True)
-
-
-def gate_slots(places, gates, slots):
-    experts, _, tokens = places.shape
-    row = pl.BlockSpec((None, 1, tokens), lambda i: (i, 0, 0))
-    return pl.pallas_call(
-        gate_slots_kernel,
-        grid=(experts,),
-        in_specs=[row, row],
-        out_specs=pl.BlockSpec((None, 1, slots), lambda i: (i, 0, 0)),
-        out_shape=jax.ShapeDtypeStruct((experts, 1, slots), F32),
-        compiler_params=params(1),
-        cost_estimate=cost(4 * experts * slots * tokens, 1e5),
-        name="gate_slots",
-    )(places, gates)
+        scratch_shapes=[pltpu.VMEM((width, hidden), F32)] * 3
+        + [pltpu.VMEM((slots, width), F32)] * 2
+        + [pltpu.VMEM((2, slots, width), BF16)] * 2
+        + [pltpu.VMEM((experts, slots, width), BF16)] * 4
+        + [pltpu.VMEM((experts, 8, 2 * slots), F32)]
+        + [pltpu.SemaphoreType.DMA((2, experts))] * 2
+        + [pltpu.SemaphoreType.DMA((3, experts))] * 2
+        + [pltpu.SemaphoreType.DMA((3,))],
+        compiler_params=pltpu.CompilerParams(
+            collective_id=3, has_side_effects=True, vmem_limit_bytes=VMEM_LIMIT,
+            dimension_semantics=("arbitrary",),
+        ),
+        cost_estimate=cost(36 * experts * slots * width * hidden, 40e6),
+        name="ffn_expert",
+    )(x_slots, d_slots, g_slots, weights, weights, weights)
 
 
 def combine_hot(pos_ref, offset, experts, slots):
@@ -352,11 +692,14 @@
     hot = combine_hot(pos_ref, core_ref[0] * slots, experts, slots)
     part = mm(hot, y_ref[...].reshape(experts * slots, width), NN)
     slot = lax.broadcasted_iota(jnp.int32, (tokens, 2 * slots), 1)
+    slot = jnp.where(
+        slot < slots, slot + core_ref[0] * slots, slot - core_ref[0] * slots
+    )
     lane = lax.broadcasted_iota(jnp.int32, (tokens, experts), 1)
     gate_grad = jnp.zeros((tokens, experts), F32)
     for e in range(experts):
         found = jnp.sum(
-            jnp.where(slot == pos_ref[:, e : e + 1], dgate_ref[e], 0.0), axis=1, keepdims=True
+            jnp.where(slot == pos_ref[:, e : e + 1], dgate_ref[e, 0:1, :], 0.0), axis=1, keepdims=True
         )
         gate_grad = jnp.where(lane == e, found, gate_grad)
     gate = gate_ref[...]
@@ -469,10 +812,11 @@
         [gain_attn[:, None], gain_ffn[:, None], router_weight], axis=1
     )
     small_own = jnp.pad(small_own, ((0, 0), (0, LANES - small_own.shape[1])))
-    first_own = jnp.concatenate([qkv_own, small_own], axis=1).astype(BF16)
-    first_all = to_all(first_own).reshape(width, pairs * 3 * LANES + LANES)
+    first_own = jnp.concatenate([qkv_own, w_output, small_own], axis=1).astype(BF16)
+    first_all = gather_all(first_own).reshape(width, first_own.shape[1])
     qkv_w = first_all[:, : pairs * 3 * LANES]
-    small = first_all[:, pairs * 3 * LANES :]
+    out_w = first_all[:, pairs * 3 * LANES : pairs * 4 * LANES]
+    small = first_all[:, pairs * 4 * LANES :]
     gain_one = small[:, 0].astype(F32)
     gain_two = small[:, 1].astype(F32)
     router_w = small[:, 2 : 2 + experts]
@@ -489,11 +833,6 @@
     valid = (core * own_len + jnp.arange(own_len, dtype=jnp.int32)) < length
     cotangent = out_cotangent[0].astype(F32) * valid.astype(F32)[:, None]
     grad_ffn = both_halves(cotangent.astype(BF16))
-    grad_slots = dispatch(own_places, grad_ffn, slots, "dispatch_grad")
-    grad_slots = after(grad_slots, first_all)
-    grad_slots = lax.all_to_all(grad_slots, "dp", 0, 0, axis_index_groups=groups, tiled=True)
-    grad_rows = grad_slots.reshape(experts * slots, width)
-    grad_rows = jnp.concatenate([grad_rows, swap(grad_rows)], axis=0)
 
     expert_own = jnp.stack([expert_gate, expert_up, expert_down], axis=0).astype(BF16)
     expert_own = expert_own.transpose(2, 0, 1, 3).reshape(1, experts, 3 * shard, hidden)
@@ -502,23 +841,13 @@
     ).reshape(ranks, 3 * shard, hidden)
     expert_own = after(expert_own, first_all)
     expert_all = lax.all_to_all(expert_own, "dp", 0, 0, tiled=True)
-    expert_all = expert_all.reshape(ranks, 3, shard, hidden).transpose(1, 0, 2, 3)
-    expert_all = expert_all.reshape(3, width, hidden)
-
-    shared_own = jnp.concatenate(
-        [w_output, shared_gate, shared_up, shared_down], axis=1
-    ).astype(BF16)
-    near = [list(range(s, s + 4)) for s in range(0, ranks, 4)]
-    far = [list(range(s, ranks, 4)) for s in range(4)]
-    shared_own = after(shared_own, first_all)
-    shared_all = to_all(to_all(shared_own, far), near)
-    heads_width = w_output.shape[1]
-    shared_all = shared_all.reshape(4, ranks // 4, shard, heads_width + 3 * hidden)
-    shared_all = shared_all.transpose(1, 0, 2, 3).reshape(width, heads_width + 3 * hidden)
-    out_w = shared_all[:, :heads_width]
-    sgate_w, sup_w, sdown_w = (
-        shared_all[:, heads_width + k * hidden : heads_width + (k + 1) * hidden] for k in range(3)
-    )
+    expert_all = expert_all.reshape(ranks, 3, shard, hidden)
+    direct = shard % 16 == 0
+    if not direct:
+        expert_all = expert_all.transpose(1, 0, 2, 3).reshape(1, 3, width, hidden)
+
+    shared_own = jnp.concatenate([shared_gate, shared_up, shared_down], axis=1).astype(BF16)
+    shared_all = lax.all_gather(shared_own, "dp", axis=0, tiled=True)
 
     half = HD // 2
     inverse = jnp.exp(jnp.arange(half, dtype=F32) * (-math.log(10000.0) / half))
@@ -540,52 +869,20 @@
     powers = jnp.where(chosen, jnp.exp(logits - top), 0.0)
     gates = powers / jnp.sum(powers, axis=1, keepdims=True)
 
-    x_slots = dispatch(own_places, ffn_in, slots, "dispatch_rows")
-    x_slots = lax.all_to_all(x_slots, "dp", 0, 0, axis_index_groups=groups, tiled=True)
-    g_slots = gate_slots(own_places, gates.T[:, None, :], slots)
-    g_slots = lax.all_to_all(g_slots, "dp", 0, 0, axis_index_groups=groups, tiled=True)
-    x_rows = x_slots.reshape(experts * slots, width)
-    x_rows = jnp.concatenate([x_rows, swap(x_rows)], axis=0)
-    g_rows = g_slots.reshape(1, experts * slots)
-    g_rows = jnp.concatenate([g_rows, swap(g_rows)], axis=0)
-    block = 512
-    g_rows = g_rows.reshape(2 * experts * slots // block, 1, block)
-
-    ones = jnp.ones((span // block, 1, block), F32)
-    shared_y, shared_dx, _, shared_gg, shared_gu, shared_gd = ffn(
-        ffn_in, grad_ffn, ones, sgate_w, sup_w, sdown_w, "ffn_shared"
+    x_slots, d_slots, g_slots, shared_y, shared_dx, shared_gg, shared_gu, shared_gd = (
+        slots_and_shared(
+            own_places, gates.T[:, None, :], ffn_in, grad_ffn, shared_all, slots, 512
+        )
     )
     shared_grads = jnp.concatenate([shared_gg, shared_gu, shared_gd], axis=1)
     shared_grads = lax.all_to_all(
         shared_grads.reshape(ranks, shard, 3 * hidden), "dp", 0, 0, tiled=True
     )
 
-    y_rows, dx_rows, gate_grads, expert_gg, expert_gu, expert_gd = ffn(
-        x_rows, grad_rows, g_rows, expert_all[0], expert_all[1], expert_all[2], "ffn_expert"
-    )
-    half_rows = experts * slots
-
-    def back_home(rows):
-        total = rows[:half_rows].astype(F32) + swap(rows[half_rows:]).astype(F32)
-        total = total.astype(BF16).reshape(experts, slots, width)
-        return lax.all_to_all(total, "dp", 0, 0, axis_index_groups=groups, tiled=True)
-
-    dx_home = back_home(dx_rows)
-    gate_grads = gate_grads.reshape(2, experts, slots).transpose(1, 0, 2)
-    gate_grads = lax.all_to_all(gate_grads, "dp", 0, 0, axis_index_groups=groups, tiled=True)
-    first = core == 0
-    gate_grads = jnp.concatenate(
-        [
-            jnp.where(first, gate_grads[:, 0], gate_grads[:, 1]),
-            jnp.where(first, gate_grads[:, 1], gate_grads[:, 0]),
-        ],
-        axis=1,
-    )[:, None, :]
-    y_rows = after(y_rows, dx_home)
-    y_home = back_home(y_rows)
-    expert_grads = jnp.stack([expert_gg, expert_gu, expert_gd], axis=0)
-    expert_grads = expert_grads.reshape(3, ranks, shard, hidden).transpose(1, 0, 2, 3)
-    expert_grads = after(expert_grads, dx_home)
+    y_home, dx_home, gate_grads, expert_grads = expert_ffn(x_slots, d_slots, g_slots, expert_all)
+    if not direct:
+        expert_grads = expert_grads.reshape(3, ranks, shard, hidden).transpose(1, 0, 2, 3)
+    dx_home = after(dx_home, shared_grads)
     expert_grads = lax.all_to_all(expert_grads, "dp", 0, 0, tiled=True)
 
     db_part, logit_grads = combine(
@@ -601,6 +898,7 @@
     attn_grads, da_part = attn_backward(
         seq_lengths, attn_in, grad_attn, qkv_w, out_w, qkv_rot, context, cosine, sine
     )
+    attn_grads = after(attn_grads, expert_grads)
     attn_grads = lax.all_to_all(
         attn_grads.reshape(ranks, shard, pairs * 4 * LANES), "dp", 0, 0, tiled=True
     )

time: 876 us -> 654 us (0.75)
  waiting for transfers between devices: 345 us -> 83.7 us
  Pallas kernels: 196 us -> 393 us
  blocking collectives: 67.8 us -> 0 us
  starting transfers between devices: 107 us -> 55.3 us
  other arithmetic: 85.7 us -> 59.8 us
  local copies, waits for them, and re-layouts: 55.9 us -> 32.3 us
  between operations: 2.34 us -> 15.9 us
    pallas_call x5 -> x3, Pallas kernels: 122 us -> 319 us  [the longest x1 173 us: expert_ffn(): pl.pallas_call(functools.partial(expert_kernel, experts=experts), grid=(e...]
    all_to_all x8 -> x1, waiting for transfers between devices: 140 us -> 7.4 us  [per_device(): lax.all_to_all(small_grads.reshape(ranks, shard, 2 + experts), 'dp', 0, 0...]
    all_to_all x1, waiting for transfers between devices: 75.6 us -> 0.01 us  [per_device(): lax.all_to_all(shared_grads.reshape(ranks, shard, 3 * hidden), 'dp', 0, 0...]
    all_to_all x1, waiting for transfers between devices: 74.9 us -> 0.01 us  [per_device(): expert_all = lax.all_to_all(expert_own, 'dp', 0, 0, tiled=True)]
    all_to_all x2 -> x0, blocking collectives: 67.8 us -> none  [the longest x1 38.4 us: to_all(): lax.all_to_all(copies, 'dp', 0, 0, axis_index_groups=groups, tiled=True)]
    all_to_all x8 -> x1, starting transfers between devices: 76.7 us -> 22.4 us  [per_device(): lax.all_to_all(small_grads.reshape(ranks, shard, 2 + experts), 'dp', 0, 0...]
    all_gather x0 -> x1, waiting for transfers between devices: none -> 41.2 us  [per_device(): shared_all = lax.all_gather(shared_own, 'dp', axis=0, tiled=True)]
    ppermute x14 -> x9, waiting for transfers between devices: 18.5 us -> 2.05 us  [swap(): return lax.ppermute(values, 'tensor', [(0, 1), (1, 0)])]
  transfers between devices with their start and end apart: 26 -> 15, of which waited for: 16 -> 6; matrix products, arithmetic and copies ran while one was open for 14% -> 13% of each run, Pallas kernels for 14% -> 61%
where the time goes in v2:
time: 654 us; the launch traced here: 644 us
  Pallas kernels  393 us (60%)
  waiting for transfers between devices  83.7 us (13%)
  other arithmetic  59.8 us (9%)
  starting transfers between devices  55.3 us (8%)
  local copies, waits for them, and re-layouts  32.3 us (5%)
  between operations  15.9 us (2%)
    pallas_call x1, Pallas kernels, expert_ffn(): pl.pallas_call(functools.partial(expert_kernel, experts=experts), grid=(e...  173 us
    pallas_call x1, Pallas kernels, slots_and_shared(): pl.pallas_call(functools.partial(slots_kernel, block=block), grid=(1,), i...  111 us
    all_gather x1, waiting for transfers between devices, per_device(): shared_all = lax.all_gather(shared_own, 'dp', axis=0, tiled=True)  41.2 us
    pallas_call x1, Pallas kernels, gather_all(): pl.pallas_call(functools.partial(gather_kernel, cut=width // 2 // LANES *...  34.8 us
    pallas_call x1, Pallas kernels, attn_backward(): pl.pallas_call(functools.partial(attn_bwd_kernel, block=256), grid=(pairs...  34.6 us
    all_to_all x1, waiting for transfers between devices, per_device(): lax.all_to_all(attn_grads.reshape(ranks, shard, pairs * 4 * LANES), 'dp',...  25.4 us
    all_to_all x1, starting transfers between devices, per_device(): lax.all_to_all(small_grads.reshape(ranks, shard, 2 + experts), 'dp', 0, 0...  22.4 us
    pallas_call x2, Pallas kernels, combine(): pl.pallas_call(kernel, grid=(tokens // block,), in_specs=in_specs, out_sp...  21.7 us
  transfers between devices with their start and end apart: 15, of which 6 were waited for; matrix products, arithmetic and copies ran while one was open for 13% of the time, Pallas kernels for 61%

profile of v2, /device:TPU:0, one launch (start us, length us, event | category | flops | bytes accessed | tf_op | source)
XLA Modules:
  0.0 644.3 jit_solution(12593355968646279214)
XLA Ops:
  12.3 34.8 %gather_attn.1 = bf16[16,48,1664]{2,1,0:T(8,128)(2,1)} custom-call(bf16[48,1664]{1,0:T(8,128)(2,1)} %fusion.31.own_ref), custom_call_target="tpu_custom_call" | custom-call | flops 1000000 | bytes 60000000 | tf_op jit(solution)/shard_map/gather_attn/pallas_call | solution.py:179
  47.2 1.4 convert_reduce_fusion.3
  52.0 1.3 copy.60
  53.3 2.7 broadcast_in_dim.61
  56.1 5.1 all-to-all-start
  61.2 1.4 slice.93.w_ref
  63.2 2.0 fusion.28
  65.2 1.9 pad_maximum_fusion.6
  67.1 1.6 broadcast_select_fusion.7
  69.9 17.1 %attn_fwd.1 = (bf16[1024,1152]{1,0:T(8,128)(2,1)}, bf16[1024,384]{1,0:T(8,128)(2,1)}) custom-call(s32[1]{0:T(128)} %copy.79.len_ref, bf16[1024,768]{1,0:T(8,128)(2,1)} %pad_maximum_fusion.2.a_ref, bf16[768,1152]{1,0:T(8,128)(2,1)} %slice.93.w_ref, f32[1024,128]{1,0:T(8,128)} %get-tuple-element.114.cos_ref, f32[1024,128]{1,0:T(8,128)} %get-tuple-element.115.sin_ref), custom_call_target="tpu_custom_call" | custom-call | flops 3422552064 | bytes 12000000 | tf_op jit(solution)/shard_map/attn_fwd/pallas_call | solution.py:248
  87.0 2.1 fusion.35
  89.2 1.5 copy-done.2
  92.3 2.3 reduce-window.6
  95.1 2.2 multiply_reduce_fusion.2
  98.4 1.5 broadcast_select_fusion.3
  101.6 1.9 select_reduce_fusion
  104.5 1.8 fusion.19
  106.3 1.8 copy.59.gates_ref
  108.2 2.6 pad_maximum_fusion.3.b_ref
  110.8 41.2 %all-gather.2.cloned.1.call-done.wg_ref.wu_ref.wd_ref = bf16[768,3072]{1,0:T(8,128)(2,1)} async-done(((bf16[48,3072]{1,0:T(8,128)(2,1)}), bf16[768,3072]{1,0:T(8,128)(2,1)}) %all-gather.2.cloned.1.call-update) | async-done | bytes 4718608 | tf_op jit(solution)/shard_map/all_gather | solution.py:850
  152.0 111.5 %slots_shared.1 = (bf16[8,2,256,768]{3,2,1,0:T(8,128)(2,1)}, bf16[8,2,256,768]{3,2,1,0:T(8,128)(2,1)}, f32[8,2,8,256]{3,2,1,0:T(8,128)}, bf16[1024,768]{1,0:T(8,...) custom-call(s32[8,1,1024]{2,1,0:T(1,128)} %or_select_fusion.places_r, ...), custom_call_target="tpu_custom_call" | custom-call | flops 20937965568 | bytes 40000000 | tf_op jit(solution)/shard_map/slots_shared/pallas_call | solution.py:490
  263.5 4.0 pad_maximum_fusion
  267.5 5.8 all-to-all-start.1
  273.3 172.8 %ffn_expert.1 = (bf16[8,256,768]{2,1,0:T(8,128)(2,1)}, bf16[8,256,768]{2,1,0:T(8,128)(2,1)}, f32[8,8,512]{2,1,0:T(8,128)}, bf16[16,3,48,1024]{3,2,1,0:T(8,128)(2,1)}) custom-call(bf16[8,2,256,768]{3,2,1,0:T(8,128)(2,1)} %get-tuple-element.37.x_ref, bf16[8,2,256,768]{3,2,1,0:T(8,128)(2,1)} %get-tuple-element.38.d_ref, ...), custom_call_target="tpu_custom_call" | custom-call | flops 57982058496 | bytes 40000000 | tf_op jit(solution)/shard_map/ffn_expert/pallas_call | solution.py:639
  446.1 15.3 %all-to-all-start.2 = ((bf16[16,3,48,1024]{3,2,1,0:T(8,128)(2,1)}), bf16[16,3,48,1024]{3,2,1,0:T(8,128)(2,1)}, u32[]{:S(2)}, u32[]{:S(2)}) async-start(bf16[16,3,48,1024]{3,2,1,0:T(8,128)(2,1)} %get-tuple-element.54), calls=%async_computation.2 | async-start | bytes 9437184 | tf_op jit(solution)/shard_map/all_to_all | solution.py:886
  464.2 2.2 bitcast_select_fusion.pos_ref
  466.4 2.7 fusion.25.gate_ref
  469.1 14.2 %combine_grad.1 = (bf16[1024,768]{1,0:T(8,128)(2,1)}, f32[1024,8]{1,0:T(8,128)}) custom-call(s32[1]{0:T(128)} %bitcast.6.core_ref, s32[1024,8]{1,0:T(8,128)} %bitcast_select_fusion.pos_ref, bf16[8,256,768]{2,1,0:T(8,128)(2,1)} %get-tuple-element.47.y_ref, bf16[1024,768]{1,0:T(8,128)(2,1)} %get-tuple-element.48.base_ref, f32[1024,8]{1,0:T(8,128)} %fusion.25.gate_ref, ...), custom_call_target="tpu_custom_call" | custom-call | flops 3221225472 | bytes 8000000 | tf_op jit(solution)/shard_map/combine_grad/pallas_call | solution.py:739
  484.6 7.5 %combine.1 = bf16[1024,768]{1,0:T(8,128)(2,1)} custom-call(s32[1]{0:T(128)} %bitcast.6.core_ref, s32[1024,8]{1,0:T(8,128)} %bitcast_select_fusion.pos_ref, bf16[8,256,768]{2,1,0:T(8,128)(2,1)} %get-tuple-element.41.y_ref, bf16[1024,768]{1,0:T(8,128)(2,1)} %get-tuple-element.42.base_ref), custom_call_target="tpu_custom_call" | custom-call | flops 3221225472 | bytes 8000000 | tf_op jit(solution)/shard_map/combine/pallas_call | solution.py:739
  492.1 1.3 constant_dynamic-slice_fusion.2
  494.6 1.3 collective-permute-done.4
  495.9 2.2 fusion.38
  498.5 1.9 slice.94.wo_ref
  500.5 1.2 pad_maximum_fusion.5.da_in_ref
  501.8 34.6 %attn_bwd.1 = (bf16[768,1536]{1,0:T(8,128)(2,1)}, f32[1024,768]{1,0:T(8,128)}) custom-call(s32[1]{0:T(128)} %copy.79.len_ref, bf16[1024,768]{1,0:T(8,128)(2,1)} %pad_maximum_fusion.2.a_ref, bf16[1024,768]{1,0:T(8,128)(2,1)} %pad_maximum_fusion.5.da_in_ref, bf16[768,1152]{1,0:T(8,128)(2,1)} %slice.93.w_ref, bf16[768,384]{1,0:T(8,128)(2,1)} %slice.94.wo_ref, ...), custom_call_target="tpu_custom_call" | custom-call | flops 20000000000 | bytes 16000000 | tf_op jit(solution)/shard_map/attn_bwd/pallas_call | solution.py:332
  536.4 2.1 convert_element_type.121
  543.5 7.5 %all-to-all-done.2 = bf16[16,3,48,1024]{3,2,1,0:T(8,128)(2,1)} async-done(((bf16[16,3,48,1024]{3,2,1,0:T(8,128)(2,1)}), bf16[16,3,48,1024]{3,2,1,0:T(8,128)(2,1)}, u32[]{:S(2)}, u32[]{:S(2)}) %all-to-all-start.2) | async-done | bytes 4718624 | tf_op jit(solution)/shard_map/all_to_all | solution.py:886
  551.1 22.4 %all-to-all-start.4 = ((f32[16,1,480]{2,1,0:T(1,128)}), f32[16,1,480]{2,1,0:T(1,128)S(1)}, u32[]{:S(2)}, u32[]{:S(2)}) async-start(f32[16,1,480]{2,1,0:T(1,128)} %reshape.258), calls=%async_computation.4 | async-start | bytes 65536 | tf_op jit(solution)/shard_map/all_to_all | solution.py:916
  573.5 7.4 %all-to-all-done.4 = f32[16,1,480]{2,1,0:T(1,128)S(1)} async-done(((f32[16,1,480]{2,1,0:T(1,128)}), f32[16,1,480]{2,1,0:T(1,128)S(1)}, u32[]{:S(2)}, u32[]{:S(2)}) %all-to-all-start.4) | async-done | bytes 30752 | tf_op jit(solution)/shard_map/all_to_all | solution.py:916
  580.9 4.7 all-to-all-start.3
  585.6 4.2 convert_reduce_fusion
  590.2 2.1 copy.65
  592.3 2.1 copy.64
  594.4 2.1 copy.63
  596.4 3.3 convert_reduce_fusion.1
  602.0 2.8 fusion.17
  606.0 25.4 %all-to-all-done.3 = bf16[16,48,1536]{2,1,0:T(8,128)(2,1)} async-done(((bf16[16,48,1536]{2,1,0:T(8,128)(2,1)}), bf16[16,48,1536]{2,1,0:T(8,128)(2,1)}, u32[]{:S(2)}, u32[]{:S(2)}) %all-to-all-start.3) | async-done | bytes 2359328 | tf_op jit(solution)/shard_map/all_to_all | solution.py:902
  631.4 2.0 convert_reduce_fusion.2
  (155 shorter events, 33.4 us)
Async XLA Ops:
  7.2 3.8 copy-start.27
  7.2 3.8 copy-start.28
  7.2 3.8 copy-start.29
  7.2 3.9 copy-start.14
  7.2 4.0 copy-start.15
  7.2 4.0 copy-start.16
  7.2 4.4 copy-start.17
  7.3 144.8 %all-gather.2.cloned.1.call-start = ((), (), s32[]{:S(2)}) async-start(), calls=%async_computation.5 | async-start | bytes 5013504 | tf_op jit(solution)/shard_map/all_gather | solution.py:850
  12.3 36.3 %copy-start = (bf16[1,512,768]{2,1,0:T(8,128)(2,1)S(1)}, bf16[1,512,768]{2,1,0:T(8,128)(2,1)}, u32[]{:S(2)}) copy-start(bf16[1,512,768]{2,1,0:T(8,128)(2,1)} %param.17) | copy-start | bytes 2359300
  47.2 2.8 copy-start.10
  48.9 18.2 %copy-start.18 = (f32[512]{0:T(512)}, f32[512]{0:T(512)S(1)}, u32[]{:S(2)}) copy-start(f32[512]{0:T(512)S(1)} %add_rsqrt_fusion.1) | copy-start | bytes 6148
  48.9 1.7 copy-start.13
  50.0 1.5 copy-start.12
  50.0 17.1 %collective-permute-start = (bf16[512,768]{1,0:T(8,128)(2,1)}, bf16[512,768]{1,0:T(8,128)(2,1)}, u32[]{:S(2)}, u32[]{:S(2)}) collective-permute-start(bf16[512,768]{1,0:T(8,128)(2,1)} %fusion.4), channel_id=1, source_target_pairs={{0,1},{1,0},{2,3},{3,2},{4,5},{5,4},{6,7},{7,6},{8,9},{9,8},{10,11... | collective-permute-start | bytes 2359304 | tf_op jit(solution)/shard_map/ppermute | solution.py:752
  56.1 5.1 copy-start.1
  56.1 211.4 %all-to-all-start = ((bf16[16,144,1024]{2,1,0:T(8,128)(2,1)}), bf16[16,144,1024]{2,1,0:T(8,128)(2,1)}, u32[]{:S(2)}, u32[]{:S(2)}) async-start(bf16[16,144,1024]{2,1,0:T(8,128)(2,1)} %bitcast.108), calls=%async_computation | async-start | bytes 9437184 | tf_op jit(solution)/shard_map/all_to_all | solution.py:843
  89.1 1.6 copy-start.2
  89.1 1.7 copy-start.3
  90.7 1.6 copy-start.26
  90.7 4.3 collective-permute-start.1
  90.8 7.6 %copy-start.24 = (f32[512]{0:T(512)}, f32[512]{0:T(512)S(1)}, u32[]{:S(2)}) copy-start(f32[512]{0:T(512)S(1)} %fusion.34) | copy-start | bytes 6148
  91.9 6.5 %collective-permute-start.3 = (bf16[512,768]{1,0:T(8,128)(2,1)}, bf16[512,768]{1,0:T(8,128)(2,1)}, u32[]{:S(2)}, u32[]{:S(2)}) collective-permute-start(bf16[512,768]{1,0:T(8,128)(2,1)} %fusion.13), channel_id=1, source_target_pairs={{0,1},{1,0},{2,3},{3,2},{4,5},{5,4},{6,7},{7,6},{8,9},{9,8},{10,11... | collective-permute-start | bytes 2359304 | tf_op jit(solution)/shard_map/ppermute | solution.py:752
  97.3 3.9 copy-start.20
  97.5 3.7 collective-permute-start.2
  101.6 2.0 copy-start.6
  101.6 2.0 copy-start.8
  103.6 1.0 copy-start.4
  103.6 7.2 %copy-start.22 = (f32[1024]{0:T(1024)}, f32[1024]{0:T(1024)S(1)}, u32[]{:S(2)}) copy-start(f32[1024]{0:T(1024)S(1)} %get-tuple-element.110) | copy-start | bytes 12292
  104.5 6.3 copy-start.23
  267.5 178.6 %all-to-all-start.1 = ((bf16[16,48,3072]{2,1,0:T(8,128)(2,1)}), bf16[16,48,3072]{2,1,0:T(8,128)(2,1)}, u32[]{:S(2)}, u32[]{:S(2)}) async-start(bf16[16,48,3072]{2,1,0:T(8,128)(2,1)} %bitcast.109), calls=%async_computation.1 | async-start | bytes 9437184 | tf_op jit(solution)/shard_map/all_to_all | solution.py:878
  446.1 104.9 %all-to-all-start.2 = ((bf16[16,3,48,1024]{3,2,1,0:T(8,128)(2,1)}), bf16[16,3,48,1024]{3,2,1,0:T(8,128)(2,1)}, u32[]{:S(2)}, u32[]{:S(2)}) async-start(bf16[16,3,48,1024]{3,2,1,0:T(8,128)(2,1)} %get-tuple-element.54), calls=%async_computation.2 | async-start | bytes 9437184 | tf_op jit(solution)/shard_map/all_to_all | solution.py:886
  484.5 9.5 %collective-permute-start.5 = (bf16[512,768]{1,0:T(8,128)(2,1)S(1)}, bf16[512,768]{1,0:T(8,128)(2,1)S(1)}, u32[]{:S(2)}, u32[]{:S(2)}) collective-permute-start(bf16[512,768]{1,0:T(8,128)(2,1)S(1)} %constant_dynamic-slice_fusion.1), channel_id=1, source_target_pairs={{0,1},{1,0},{2,3},{3,2},{4,5},{5,4},{6,7},{7,6},{8,9},{9,8},{10,11... | collective-permute-start | bytes 2359304 | tf_op jit(solution)/shard_map/ppermute | solution.py:752
  484.6 9.4 %copy-start.21 = (f32[512]{0:T(512)S(1)}, f32[512]{0:T(512)}, u32[]{:S(2)}) copy-start(f32[512]{0:T(512)} %copy-done.20) | copy-start | bytes 6148
  492.1 1.9 copy-start.5
  493.4 2.5 copy-start.11
  493.5 2.5 copy-start.25
  493.5 2.5 collective-permute-start.4
  498.1 2.3 collective-permute-start.6
  536.4 3.4 copy-start.30
  538.5 1.4 copy-start.7
  538.5 1.6 copy-start.9
  539.4 2.5 copy-start.19
  539.4 2.5 collective-permute-start.7
  551.1 29.8 %all-to-all-start.4 = ((f32[16,1,480]{2,1,0:T(1,128)}), f32[16,1,480]{2,1,0:T(1,128)S(1)}, u32[]{:S(2)}, u32[]{:S(2)}) async-start(f32[16,1,480]{2,1,0:T(1,128)} %reshape.258), calls=%async_computation.4 | async-start | bytes 65536 | tf_op jit(solution)/shard_map/all_to_all | solution.py:916
  580.9 50.5 %all-to-all-start.3 = ((bf16[16,48,1536]{2,1,0:T(8,128)(2,1)}), bf16[16,48,1536]{2,1,0:T(8,128)(2,1)}, u32[]{:S(2)}, u32[]{:S(2)}) async-start(bf16[16,48,1536]{2,1,0:T(8,128)(2,1)} %bitcast.117), calls=%async_computation.3 | async-start | bytes 4718592 | tf_op jit(solution)/shard_map/all_to_all | solution.py:902
  601.9 2.9 collective-permute-start.8
Sparse Core Ops, SparseCore 0:
  11.1 140.8 all-gather.1

commit v3 on v2

v3 whole, which is shorter than its diff:
```python
import functools
import math

import jax
import jax.numpy as jnp
import numpy as np
from jax import lax
from jax.experimental import pallas as pl
from jax.experimental.pallas import tpu as pltpu
from jax.sharding import PartitionSpec as P

HD = 64
LANES = 128
EPS = 1e-06
F32 = jnp.float32
BF16 = jnp.bfloat16
HIGHEST = lax.Precision.HIGHEST
VMEM_LIMIT = 60 * 1024 * 1024

NN = (((1,), (0,)), ((), ()))
NT = (((1,), (1,)), ((), ()))
TN = (((0,), (0,)), ((), ()))


def mm(left, right, dims):
    return lax.dot_general(left, right, dims, preferred_element_type=F32)


def params(count):
    return pltpu.CompilerParams(
        dimension_semantics=("arbitrary",) * count, vmem_limit_bytes=VMEM_LIMIT
    )


def remote_params(number):
    return pltpu.CompilerParams(
        collective_id=number, has_side_effects=True, vmem_limit_bytes=VMEM_LIMIT,
        dimension_semantics=("arbitrary",),
    )


def cost(flops, nbytes, trans=0):
    return pl.CostEstimate(flops=int(flops), bytes_accessed=int(nbytes), transcendentals=int(trans))


def flip(index, offset):
    bit = 1
    while bit <= offset:
        if offset & bit:
            index = index + bit - 2 * bit * lax.rem(lax.div(index, bit), 2)
        bit *= 2
    return index


def device(rank, core):
    return {"dp": rank, "tensor": core}


def greet(devices):
    barrier = pltpu.get_barrier_semaphore()
    for target in devices:
        pl.semaphore_signal(barrier, inc=1, device_id=target, device_id_type=pl.DeviceIdType.MESH)
    pl.semaphore_wait(barrier, len(devices))


def remote(src, dst, send, recv, target):
    return pltpu.make_async_remote_copy(
        src_ref=src, dst_ref=dst, send_sem=send, recv_sem=recv,
        device_id=target, device_id_type=pl.DeviceIdType.MESH,
    )


class Gather:
    order = (0, 1, 4, 2, 5, 3, 6)
    turns = 9

    def __init__(self, own_ref, out_ref, sems, which):
        self.own_ref, self.out_ref = own_ref, out_ref
        self.own_sem, self.z_send, self.z_recv, self.s_send, self.s_recv, self.f_send, self.f_recv = (
            sem.at[which] for sem in sems
        )
        self.cut = own_ref.shape[1] // 2 // LANES * LANES
        self.me, self.core = lax.axis_index("dp"), lax.axis_index("tensor")
        self.z = lax.div(self.me, 4)
        self.up, self.down = lax.min(self.me + 4, 15), lax.max(self.me - 4, 0)
        self.sides_of = (flip(self.me, 1), flip(self.me, 2))

    @staticmethod
    def semaphores(count):
        dma = pltpu.SemaphoreType.DMA
        return [dma((count,)), dma((count, 6)), dma((count, 6))] + [dma((count, 2, 7))] * 4

    def rank_at(self, place):
        return self.me - 4 * place if place <= 3 else self.me + 4 * (place - 3)

    def at(self, place, body):
        if place == 0:
            body()
        else:
            pl.when(self.z >= place if place <= 3 else self.z + (place - 3) <= 3)(body)

    def own_copy(self):
        return pltpu.make_async_copy(self.own_ref, self.out_ref.at[self.me], self.own_sem)

    def z_copy(self, rank, step, upward):
        index = step - 1 if upward else step + 2
        return remote(
            self.own_ref if step == 1 else self.out_ref.at[rank], self.out_ref.at[rank],
            self.z_send.at[index], self.z_recv.at[index],
            device(self.up if upward else self.down, self.core),
        )

    def side_copy(self, rank, place, axis):
        return remote(
            self.own_ref if place == 0 else self.out_ref.at[rank], self.out_ref.at[rank],
            self.s_send.at[axis, place], self.s_recv.at[axis, place],
            device(self.sides_of[axis], self.core),
        )

    def onward_copy(self, rank, place, axis):
        width = self.own_ref.shape[1]
        columns = pl.ds(0, self.cut) if axis == 0 else pl.ds(self.cut, width - self.cut)
        part = self.out_ref.at[rank, :, columns]
        return remote(
            part, part, self.f_send.at[axis, place], self.f_recv.at[axis, place],
            device(self.sides_of[1 - axis], self.core),
        )

    def begin(self):
        self.own_copy().start()
        pl.when(self.z < 3)(lambda: self.z_copy(self.me, 1, True).start())
        pl.when(self.z > 0)(lambda: self.z_copy(self.me, 1, False).start())
        for axis in range(2):
            self.side_copy(self.me, 0, axis).start()

    def arrive(self, place):
        upward = place <= 3
        step = place if upward else place - 3
        rank = self.rank_at(place)
        self.z_copy(rank, step, upward).wait_recv()
        if step < 3:
            further = self.z < 3 if upward else self.z > 0
            pl.when(further)(lambda: self.z_copy(rank, step + 1, upward).start())
        for axis in range(2):
            self.side_copy(rank, place, axis).start()

    def onward(self, place):
        for axis in range(2):
            rank = flip(self.rank_at(place), 1 + axis)
            self.side_copy(rank, place, axis).wait_recv()
            self.onward_copy(rank, place, axis).start()

    def turn(self, index):
        if index < 7:
            self.at(self.order[index], functools.partial(self.arrive, self.order[index]))
        if index >= 2:
            self.at(self.order[index - 2], functools.partial(self.onward, self.order[index - 2]))

    def finish(self, place):
        for axis in range(2):
            rank = flip(self.rank_at(place), 1 + axis)
            self.side_copy(self.rank_at(place), place, axis).wait_send()
            self.onward_copy(rank, place, axis).wait_send()
            self.onward_copy(flip(self.rank_at(place), 3), place, axis).wait_recv()

    def end(self):
        z = self.z
        for place in self.order:
            self.at(place, functools.partial(self.finish, place))
        for step in range(1, 4):
            pl.when((z < 3) & (z >= step - 1))(
                lambda step=step: self.z_copy(self.me - 4 * (step - 1), step, True).wait_send()
            )
            pl.when((z > 0) & (z + step - 1 <= 3))(
                lambda step=step: self.z_copy(self.me + 4 * (step - 1), step, False).wait_send()
            )
        self.own_copy().wait()


def gather_kernel(own_ref, out_ref, *sems):
    gather = Gather(own_ref, out_ref, sems, 0)
    z, core = gather.z, gather.core
    barrier = pltpu.get_barrier_semaphore()

    def hello(rank):
        pl.semaphore_signal(
            barrier, inc=1, device_id=device(rank, core), device_id_type=pl.DeviceIdType.MESH
        )

    for rank in gather.sides_of:
        hello(rank)
    pl.when(z < 3)(lambda: hello(gather.up))
    pl.when(z > 0)(lambda: hello(gather.down))
    pl.semaphore_wait(barrier, 2 + lax.min(z, 1) + lax.min(3 - z, 1))
    gather.begin()
    for turn in range(1, gather.turns):
        gather.turn(turn)
    gather.end()


def gather_all(own):
    ranks = lax.axis_size("dp")
    if ranks != 16:
        return to_all(own)
    return pl.pallas_call(
        gather_kernel,
        in_specs=[pl.BlockSpec(memory_space=pl.ANY)],
        out_specs=pl.BlockSpec(memory_space=pl.ANY),
        out_shape=jax.ShapeDtypeStruct((ranks,) + own.shape, own.dtype),
        scratch_shapes=Gather.semaphores(1),
        compiler_params=pltpu.CompilerParams(collective_id=1, has_side_effects=True),
        cost_estimate=cost(1e6, 60e6),
        name="gather_attn",
    )(own)


def partner(values):
    lane = lax.broadcasted_iota(jnp.int32, values.shape, 1)
    return jnp.where(
        lane % HD < HD // 2,
        pltpu.roll(values, LANES - HD // 2, 1),
        pltpu.roll(values, HD // 2, 1),
    )


def head_lanes(shape, head):
    lane = lax.broadcasted_iota(jnp.int32, shape, 1)
    return (lane // HD) == head


def offsets(count):
    return sorted(range(1, count), key=lambda k: (bin(k).count("1"), k))


class Trip:
    def __init__(self, ins, outs, send, recv, core_send, core_recv, local, part):
        self.ins, self.outs, self.part = ins, outs, part
        self.send, self.recv, self.local = send, recv, local
        self.core_send, self.core_recv = core_send, core_recv
        self.me, self.core = lax.axis_index("dp"), lax.axis_index("tensor")
        self.count = ins.shape[0]

    def copy(self, k):
        return remote(
            self.ins.at[k], self.outs.at[k, 0],
            self.send.at[self.part, k], self.recv.at[self.part, k],
            device(flip(self.me, k), self.core),
        )

    def core_copy(self, k):
        src = self.ins.at[0] if k == 0 else self.outs.at[k, 0]
        return remote(
            src, self.outs.at[k, 1],
            self.core_send.at[self.part, k], self.core_recv.at[self.part, k],
            device(self.me, 1 - self.core),
        )

    def own(self):
        return pltpu.make_async_copy(self.ins.at[0], self.outs.at[0, 0], self.local.at[self.part])

    def go(self, k):
        if k:
            self.copy(k).start()
        else:
            self.own().start()
            self.core_copy(0).start()

    def pass_on(self, k):
        self.copy(k).wait_recv()
        self.core_copy(k).start()

    def end(self):
        self.own().wait()
        for k in range(self.count):
            self.core_copy(k).wait()
            if k:
                self.copy(k).wait_send()


def cluster_and_core(count):
    me, core = lax.axis_index("dp"), lax.axis_index("tensor")
    return [device(flip(me, k), core) for k in range(1, count)] + [device(me, 1 - core)]


def rms(values):
    return values * lax.rsqrt(jnp.mean(values * values, axis=-1, keepdims=True) + EPS)


def whole(shape):
    return pl.BlockSpec(shape, lambda i: (0,) * len(shape), pipeline_mode=pl.Buffered(1))


def attn_fwd_kernel(
    len_ref, x_ref, c_ref, routes_ref, w_ref, wo_ref, small_ref, shared_ref, cos_ref, sin_ref,
    a_ref, qkv_ref, ctx_ref, h_ref, b_ref, d_ref, places_ref, rows_ref, gates_ref, y_ref, dx_ref, dr, xr, gr, og_ref, shared_all,
    ds, xs, gs, ag, au, ad, shared_w, part, x_in, h_in, b_out, b_in, c_out, c_in,
    send, recv, core_send, core_recv, local, pair_send, pair_recv, load, *gather_sems,
    block, gathers,
):
    step = pl.program_id(0)
    me, core = lax.axis_index("dp"), lax.axis_index("tensor")
    other = device(me, 1 - core)
    experts, slots, _ = ds.shape
    trips = [
        Trip(ins, outs, send, recv, core_send, core_recv, local, index)
        for index, (ins, outs) in enumerate(((ds, dr), (xs, xr), (gs, gr)))
    ]
    slot = core * slots + lax.broadcasted_iota(jnp.int32, (slots, a_ref.shape[0]), 0)
    slot = slot.astype(F32)
    mine = lax.rem(me, experts)
    span, width = a_ref.shape
    half = span // 2
    length = len_ref[0]
    own = pl.ds(pl.multiple_of(core * half, half), half)
    away = pl.ds(pl.multiple_of((1 - core) * half, half), half)
    pairs = pl.num_programs(0)
    if gathers:
        shared = Gather(shared_ref, shared_all, gather_sems, 0)

    def to_other(src, dst, index):
        return remote(src, dst, pair_send.at[index], pair_recv.at[index], other)

    @pl.when(step == 0)
    def _():
        if gathers:
            z = lax.div(me, 4)
            barrier = pltpu.get_barrier_semaphore()

            def hello(target):
                pl.semaphore_signal(
                    barrier, inc=1, device_id=target, device_id_type=pl.DeviceIdType.MESH
                )

            for target in cluster_and_core(experts):
                hello(target)
            pl.when(z == 1)(lambda: hello(device(shared.up, core)))
            pl.when(z == 2)(lambda: hello(device(shared.down, core)))
            pl.semaphore_wait(barrier, experts + lax.min(z, 1) * lax.min(3 - z, 1))
        else:
            greet(cluster_and_core(experts))
        token = core * half + lax.broadcasted_iota(jnp.int32, c_ref.shape, 0)
        valid = jnp.where(token < length, c_ref[...].astype(F32), 0.0).astype(BF16)
        c_out[...] = valid
        d_ref[own, :] = valid
        swap_c = to_other(c_out, c_in, 0)
        swap_c.start()
        swap_x = to_other(x_ref, x_in, 1)
        swap_x.start()

        name = lax.broadcasted_iota(jnp.int32, (experts, span), 0)
        chosen = (name == routes_ref[0:1, :]) | (name == routes_ref[1:2, :])
        earlier = lax.broadcasted_iota(jnp.int32, (span, span), 0) < lax.broadcasted_iota(
            jnp.int32, (span, span), 1
        )
        counts = mm(
            jnp.where(chosen, 1.0, 0.0).astype(BF16), jnp.where(earlier, 1.0, 0.0).astype(BF16), NN
        )
        places_ref[...] = jnp.where(chosen, counts, -1.0)

        swap_c.wait_recv()
        d_ref[away, :] = c_in[...]
        for k in offsets(experts) + [0]:
            place = places_ref[pl.ds(flip(mine, k), 1), :]
            hot = jnp.where(slot == place, 1.0, 0.0).astype(BF16)
            ds[k] = mm(hot, d_ref[...], NN).astype(BF16)
            trips[0].go(k)
        if gathers:
            shared.begin()
        rows_ref[...] = small_ref[...].astype(F32).T[: rows_ref.shape[0], :]
        swap_x.wait_recv()
        gain = rows_ref[0:1, :]
        a_ref[own, :] = (rms(x_ref[...].astype(F32)) * gain).astype(BF16)
        a_ref[away, :] = (rms(x_in[...].astype(F32)) * gain).astype(BF16)
        part[...] = jnp.zeros_like(part)
        swap_c.wait_send()
        swap_x.wait_send()

    raw = mm(a_ref[...], w_ref[...], NN)
    cosine, sine = cos_ref[...], sin_ref[...]
    query, key = raw[:, :LANES], raw[:, LANES : 2 * LANES]
    qkv_ref[:, :LANES] = (query * cosine + partner(query) * sine).astype(BF16)
    qkv_ref[:, LANES : 2 * LANES] = (key * cosine + partner(key) * sine).astype(BF16)
    qkv_ref[:, 2 * LANES :] = raw[:, 2 * LANES :].astype(BF16)
    for index in range(span // block):
        keys = (index + 1) * block
        query_rows = qkv_ref[index * block : keys, :LANES] * jnp.asarray(HD**-0.5, BF16)
        key_rows = qkv_ref[:keys, LANES : 2 * LANES]
        value_rows = qkv_ref[:keys, 2 * LANES :]
        row = index * block + lax.broadcasted_iota(jnp.int32, (block, keys), 0)
        column = lax.broadcasted_iota(jnp.int32, (block, keys), 1)
        allowed = (column <= row) & (column < length)
        parts = []
        for head in range(LANES // HD):
            masked_query = jnp.where(
                head_lanes(query_rows.shape, head), query_rows, jnp.zeros_like(query_rows)
            )
            scores = jnp.where(allowed, mm(masked_query, key_rows, NT), -1e30)
            peak = jnp.max(scores, axis=1, keepdims=True)
            powers = jnp.exp(scores - peak)
            total = jnp.sum(powers, axis=1, keepdims=True)
            prob = (powers * (1.0 / total)).astype(BF16)
            parts.append(mm(prob, value_rows, NN))
        context = jnp.where(head_lanes(parts[0].shape, 0), parts[0], parts[1]).astype(BF16)
        ctx_ref[index * block : keys, :] = context
        part[index * block : keys, :] += mm(context, wo_ref[...], NT)

    if gathers:
        for turn in range(1, 3):
            pl.when(step == turn - 1)(functools.partial(shared.turn, turn))

    @pl.when(step == pairs - 1)
    def _():
        swap_h = to_other(part.at[away], h_in, 2)
        swap_h.start()
        rows = x_ref[...].astype(F32) + part[own, :]
        swap_h.wait_recv()
        rows = rows + h_in[...]
        h_ref[...] = rows
        normed = (rms(rows) * rows_ref[1:2, :]).astype(BF16)
        b_out[...] = normed
        swap_b = to_other(b_out, b_in, 3)
        swap_b.start()
        b_ref[own, :] = normed
        swap_b.wait_recv()
        b_ref[away, :] = b_in[...]
        chosen = places_ref[...] >= 0
        logits = mm(rows_ref[2 : 2 + experts, :].astype(BF16), b_ref[...], NT)
        top = jnp.max(jnp.where(chosen, logits, -1e30), axis=0, keepdims=True)
        powers = jnp.where(chosen, jnp.exp(jnp.minimum(logits - top, 0.0)), 0.0)
        gates_ref[...] = powers / jnp.sum(powers, axis=0, keepdims=True)
        for k in offsets(experts) + [0]:
            target = pl.ds(flip(mine, k), 1)
            found = slot == places_ref[target, :]
            xs[k] = mm(jnp.where(found, 1.0, 0.0).astype(BF16), b_ref[...], NN).astype(BF16)
            trips[1].go(k)
            gate = jnp.sum(jnp.where(found, gates_ref[target, :], 0.0), axis=1, keepdims=True)
            gs[k] = jnp.broadcast_to(row_of(gate), gs.shape[1:])
            trips[2].go(k)
        swap_h.wait_send()
        swap_b.wait_send()
        for total in (ag, au, ad):
            total[...] = jnp.zeros_like(total)
        if gathers:
            for turn in range(3, shared.turns):
                shared.turn(turn)
            shared.end()
        read = pltpu.make_async_copy(shared_all if gathers else shared_ref, shared_w, load)
        read.start()
        read.wait()
        for k in offsets(experts):
            trips[0].pass_on(k)
        hidden = ag.shape[1]

        def matrix(index):
            return shared_w[:, :, index * hidden : (index + 1) * hidden].reshape(width, hidden)

        def branch(index, carry):
            rows = pl.ds(pl.multiple_of(index * block, block), block)
            out, row_grad, _ = ffn_block(
                b_ref[rows, :], d_ref[rows, :], None, matrix(0), matrix(1), matrix(2), (ag, au, ad)
            )
            y_ref[rows, :] = out.astype(BF16)
            dx_ref[rows, :] = row_grad.astype(BF16)
            return carry

        lax.fori_loop(0, span // block, branch, 0)
        for index, total in enumerate((ag, au, ad)):
            shared_w[:, :, index * hidden : (index + 1) * hidden] = (
                total[...].astype(BF16).reshape(shared_w.shape[0], -1, hidden)
            )
        write = pltpu.make_async_copy(shared_w, og_ref, load)
        write.start()
        for k in offsets(experts):
            trips[1].pass_on(k)
            trips[2].pass_on(k)
        for trip in trips:
            trip.end()
        write.wait()


def attn_forward(length, rows, cotangent, routes, first_all, shared_own, cosine, sine, experts, slots):
    half, width = rows.shape
    span = 2 * half
    ranks = lax.axis_size("dp")
    pairs = (first_all.shape[1] - LANES) // (4 * LANES)
    gathers = ranks == 16
    far = pl.BlockSpec(memory_space=pl.ANY)
    hidden = shared_own.shape[1] // 3
    if gathers:
        shared, parts = shared_own, (ranks,) + shared_own.shape
    else:
        parts = (1, width, shared_own.shape[1])
        shared = to_all(shared_own).reshape(parts)
    return pl.pallas_call(
        functools.partial(attn_fwd_kernel, block=256, gathers=gathers),
        grid=(pairs,),
        in_specs=[
            pl.BlockSpec(memory_space=pltpu.SMEM),
            whole((half, width)),
            whole((half, width)),
            whole(routes.shape),
            pl.BlockSpec((width, 3 * LANES), lambda i: (0, i)),
            pl.BlockSpec((width, LANES), lambda i: (0, 3 * pairs + i)),
            pl.BlockSpec((width, LANES), lambda i: (0, 4 * pairs)),
            far,
            whole((span, LANES)),
            whole((span, LANES)),
        ],
        out_specs=[
            whole((span, width)),
            pl.BlockSpec((span, 3 * LANES), lambda i: (0, i)),
            pl.BlockSpec((span, LANES), lambda i: (0, i)),
            whole((half, width)),
            whole((span, width)),
            whole((span, width)),
            whole((experts, span)),
            whole((16, width)),
            whole((experts, span)),
            whole((span, width)),
            whole((span, width)),
        ]
        + [far] * 5,
        out_shape=[
            jax.ShapeDtypeStruct((span, width), BF16),
            jax.ShapeDtypeStruct((span, pairs * 3 * LANES), BF16),
            jax.ShapeDtypeStruct((span, pairs * LANES), BF16),
            jax.ShapeDtypeStruct((half, width), F32),
            jax.ShapeDtypeStruct((span, width), BF16),
            jax.ShapeDtypeStruct((span, width), BF16),
            jax.ShapeDtypeStruct((experts, span), F32),
            jax.ShapeDtypeStruct((16, width), F32),
            jax.ShapeDtypeStruct((experts, span), F32),
            jax.ShapeDtypeStruct((span, width), BF16),
            jax.ShapeDtypeStruct((span, width), BF16),
            jax.ShapeDtypeStruct((experts, 2, slots, width), BF16),
            jax.ShapeDtypeStruct((experts, 2, slots, width), BF16),
            jax.ShapeDtypeStruct((experts, 2, 8, slots), F32),
            jax.ShapeDtypeStruct(parts, BF16),
            jax.ShapeDtypeStruct(parts if gathers else (1, 16, LANES), BF16),
        ],
        scratch_shapes=[
            pltpu.VMEM((experts, slots, width), BF16),
            pltpu.VMEM((experts, slots, width), BF16),
            pltpu.VMEM((experts, 8, slots), F32),
            pltpu.VMEM((width, hidden), F32),
            pltpu.VMEM((width, hidden), F32),
            pltpu.VMEM((width, hidden), F32),
            pltpu.VMEM(parts, BF16),
            pltpu.VMEM((span, width), F32),
            pltpu.VMEM((half, width), BF16),
            pltpu.VMEM((half, width), F32),
        ]
        + [pltpu.VMEM((half, width), BF16)] * 4
        + [pltpu.SemaphoreType.DMA((3, experts))] * 4
        + [pltpu.SemaphoreType.DMA((3,))]
        + [pltpu.SemaphoreType.DMA((4,))] * 2
        + [pltpu.SemaphoreType.DMA]
        + Gather.semaphores(1),
        compiler_params=remote_params(4),
        cost_estimate=cost(20e9, 60e6, 6e6),
        name="attn_fwd",
    )(length, rows, cotangent, routes, first_all, first_all, first_all, shared, cosine, sine)


def norm_back(grad, values, gain):
    factor = lax.rsqrt(jnp.mean(values * values, axis=-1, keepdims=True) + EPS)
    normed = values * factor
    hat = grad * gain
    back = factor * (hat - normed * jnp.mean(hat * normed, axis=-1, keepdims=True))
    return back, jnp.sum(grad * normed, axis=0, keepdims=True)


def slot_table(places, experts, slots, offset):
    slot = lax.broadcasted_iota(jnp.int32, (places.shape[0], slots), 1) + offset
    slot = slot.astype(F32)
    return jnp.concatenate(
        [jnp.where(slot == places[:, e : e + 1], 1.0, 0.0).astype(BF16) for e in range(experts)],
        axis=1,
    )


def attn_bwd_kernel(
    len_ref, places_ref, gates_ref, rows_ref, dx_ref, dg_ref, base_ref, b_ref, h_ref, d_ref,
    x_ref, a_ref, w_ref, wo_ref, qkv_ref, ctx_ref, cos_ref, sin_ref, sy_ref, y_ref, share_ref, late_ref, early_ref,
    gi_ref, lo_ref, *rest, block, ranks, halves, sends,
):
    if sends:
        go_refs, gx_refs, gsh_refs, gs_ref = rest[:4], rest[4:7], rest[7:10], rest[10]
        gw_ref, total_ref, late_in, early_in, small_in = rest[11:16]
        rest = rest[16:]
    else:
        gw_ref, gs_ref = rest[:2]
        rest = rest[2:]
    (
        db_s, dl_s, db_out, db_in, dh_s, grad_s, da_s, sums_s, sums_in, turned_s,
        yh_s, gw_s, dctx_s, dq_s, dk_s, dv_s, send, recv, local, pair_send, pair_recv,
        y_send, y_recv, y_local, z_send, z_recv,
    ) = rest
    step = pl.program_id(0)
    last = pl.num_programs(0) - 1
    me, core = lax.axis_index("dp"), lax.axis_index("tensor")
    other = device(me, 1 - core)
    experts, slots, width = dx_ref.shape
    span = a_ref.shape[0]
    half = span // 2
    length = len_ref[0]
    own = pl.ds(pl.multiple_of(core * half, half), half)
    away = pl.ds(pl.multiple_of((1 - core) * half, half), half)
    shard = width // ranks
    pairs = gw_s.shape[0]

    def to_other(src, dst, index):
        return remote(src, dst, pair_send.at[index], pair_recv.at[index], other)

    small, late = pairs, pairs + 1

    def part_of(index, rank):
        rows = pl.ds(pl.multiple_of(rank * shard, shard), shard)
        if index is late:
            return late_ref.at[rank]
        return turned_s.at[rows] if index is small else gw_s.at[index, rows]

    def place_of(index, rank):
        if index is late:
            return late_in.at[rank]
        return small_in.at[rank] if index is small else gw_ref.at[rank, index]

    def share(index, offset):
        rank = lax.rem(me + offset, ranks)
        return remote(
            part_of(index, rank), place_of(index, me), send.at[index, offset],
            recv.at[index, offset], device(rank, core),
        )

    def own_share(index):
        return pltpu.make_async_copy(part_of(index, me), place_of(index, me), local.at[index])

    def give(index):
        own_share(index).start()

        def one(offset, carry):
            share(index, offset).start()
            return carry

        lax.fori_loop(1, ranks, one, 0)

    def take(index):
        own_share(index).wait()

        def done(offset, carry):
            share(index, offset).wait()
            return carry

        lax.fori_loop(1, ranks, done, 0)

    def all_ranks(ref, *index):
        total = ref[(0,) + index].astype(F32)
        for rank in range(1, ref.shape[0]):
            total += ref[(rank,) + index].astype(F32)
        return total

    def put_experts(ref, columns):
        for kind in range(3):
            for expert in range(experts):
                total = ref[expert, kind].astype(F32)
                for cluster in range(1, ranks // experts):
                    total += ref[cluster * experts + expert, kind].astype(F32)
                gx_refs[kind][:, expert, columns] = total

    def y_copy(k):
        return remote(
            y_ref.at[k], yh_s.at[k], y_send.at[k], y_recv.at[k], device(flip(me, k), core)
        )

    def z_copy(k):
        rank = flip(me, 4 * k)
        return remote(
            share_ref.at[lax.div(rank, 4)], total_ref.at[k], z_send.at[k], z_recv.at[k],
            device(rank, core),
        )

    def own_rows():
        copies = [pltpu.make_async_copy(y_ref.at[0], yh_s.at[0], y_local.at[0])]
        if halves:
            copies.append(
                pltpu.make_async_copy(share_ref.at[lax.div(me, 4)], total_ref.at[0], y_local.at[1])
            )
        return copies

    def put_together(table, values, index, tokens):
        here = pl.ds(pl.multiple_of(index * tokens, tokens), tokens)
        places = table(here)
        hot = slot_table(places, experts, slots, core * slots)
        return here, places, mm(hot, values[...].reshape(experts * slots, width), NN)

    @pl.when(step == 0)
    def _():
        if sends:
            greet([device(lax.rem(me + k, ranks), core) for k in range(1, ranks)] + [other])
        else:
            greet(cluster_and_core(experts))
        for copy in own_rows():
            copy.start()
        for k in range(1, experts):
            y_copy(k).start()
        if halves:
            for k in range(1, 4):
                z_copy(k).start()
        if sends:
            give(late)
            pltpu.make_async_copy(early_ref, early_in, y_local.at[2]).start()
        router = rows_ref[2 : 2 + experts, :]
        tokens = 256

        def gather(index, carry):
            here, places, total = put_together(
                lambda rows: places_ref[:, rows].T, dx_ref, index, tokens
            )
            gate = gates_ref[:, here].T
            slot = lax.broadcasted_iota(jnp.int32, (tokens, 2 * slots), 1)
            slot = jnp.where(slot < slots, slot + core * slots, slot - core * slots).astype(F32)
            lane = lax.broadcasted_iota(jnp.int32, (tokens, experts), 1)
            gate_grad = jnp.zeros((tokens, experts), F32)
            for e in range(experts):
                found = jnp.where(slot == places[:, e : e + 1], dg_ref[e, 0:1, :], 0.0)
                gate_grad = jnp.where(lane == e, jnp.sum(found, axis=1, keepdims=True), gate_grad)
            mean = jnp.sum(gate * gate_grad, axis=1, keepdims=True)
            logit_grad = gate * (gate_grad - mean)
            dl_s[here, :] = logit_grad
            total += lax.dot_general(
                logit_grad, router, NN, precision=HIGHEST, preferred_element_type=F32
            )
            db_s[here, :] = total + base_ref[here, :].astype(F32)
            return carry

        lax.fori_loop(0, span // tokens, gather, 0)
        db_out[...] = db_s[away, :].astype(BF16)
        swap_b = to_other(db_out, db_in.at[0], 0)
        swap_b.start()
        sums_s[...] = jnp.zeros_like(sums_s)
        sums_s[2 : 2 + experts, :] = lax.dot_general(
            dl_s[...], b_ref[...].astype(F32), TN, precision=HIGHEST, preferred_element_type=F32
        )
        swap_b.wait()
        db = db_s[own, :] + db_in[0].astype(F32)
        back, sums_s[1:2, :] = norm_back(db, h_ref[...], rows_ref[1:2, :])
        rows = d_ref[own, :].astype(F32) + back
        dh_s[...] = rows
        db_out[...] = rows.astype(BF16)
        grad_s[own, :] = rows.astype(BF16)
        swap_a = to_other(db_out, db_in.at[1], 1)
        swap_a.start()
        da_s[...] = jnp.zeros_like(da_s)
        swap_a.wait()
        grad_s[away, :] = db_in[1]

    grad_rows = grad_s[...]
    dctx_s[...] = mm(grad_rows, wo_ref[...], NN).astype(BF16)
    gw_s[step, :, 3 * LANES :] = mm(grad_rows, ctx_ref[...], TN).astype(BF16)
    dk_s[...] = jnp.zeros_like(dk_s)
    dv_s[...] = jnp.zeros_like(dv_s)
    scale = jnp.asarray(HD**-0.5, BF16)
    for index in range(span // block):
        keys = (index + 1) * block
        start = index * block
        query_rows = qkv_ref[start:keys, :LANES] * scale
        key_rows = qkv_ref[:keys, LANES : 2 * LANES]
        value_rows = qkv_ref[:keys, 2 * LANES :]
        context_grad = dctx_s[start:keys, :]
        row = lax.broadcasted_iota(jnp.int32, (keys, block), 0)
        column = start + lax.broadcasted_iota(jnp.int32, (keys, block), 1)
        allowed = (row <= column) & (row < length)
        dq_total = None
        for head in range(LANES // HD):
            lanes = head_lanes((block, LANES), head)
            masked_query = jnp.where(lanes, query_rows, jnp.zeros_like(query_rows))
            masked_grad = jnp.where(lanes, context_grad, jnp.zeros_like(context_grad))
            scores = jnp.where(allowed, mm(key_rows, masked_query, NT), -1e30)
            peak = jnp.max(scores, axis=0, keepdims=True)
            powers = jnp.exp(scores - peak)
            total = jnp.sum(powers, axis=0, keepdims=True)
            prob = powers * (1.0 / total)
            prob_grad = mm(value_rows, masked_grad, NT)
            inner = jnp.sum(prob * prob_grad, axis=0, keepdims=True)
            score_grad = (prob * (prob_grad - inner)).astype(BF16)
            dk_s[:keys, :] += mm(score_grad, masked_query, NN)
            dv_s[:keys, :] += mm(prob.astype(BF16), masked_grad, NN)
            dq_part = mm(score_grad, key_rows, TN)
            dq_total = dq_part if head == 0 else jnp.where(lanes, dq_part, dq_total)
        dq_s[start:keys, :] = dq_total * (HD**-0.5)
    cosine, sine = cos_ref[...], sin_ref[...]
    dq, dk = dq_s[...], dk_s[...]
    dq = (dq * cosine - partner(dq) * sine).astype(BF16)
    dk = (dk * cosine - partner(dk) * sine).astype(BF16)
    grads = jnp.concatenate([dq, dk, dv_s[...].astype(BF16)], axis=1)
    gw_s[step, :, : 3 * LANES] = mm(a_ref[...], grads, TN).astype(BF16)
    if sends:
        give(step)
    else:
        gw_ref[step] = gw_s[step]
    da_s[...] += mm(grads, w_ref[...], NT)

    @pl.when(step == last)
    def _():
        db_out[...] = da_s[away, :].astype(BF16)
        swap_d = to_other(db_out, db_in.at[0], 2)
        swap_d.start()
        swap_d.wait()
        da = da_s[own, :] + db_in[0].astype(F32)
        back, sums_s[0:1, :] = norm_back(da, x_ref[...].astype(F32), rows_ref[0:1, :])
        swap_s = to_other(sums_s, sums_in, 3)
        swap_s.start()
        gi_ref[...] = (dh_s[...] + back).astype(BF16)
        swap_s.wait()
        turned = (sums_s[...] + sums_in[...]).T
        if sends:
            turned_s[...] = jnp.zeros_like(turned_s)
            turned_s[:, : turned.shape[1]] = turned
            give(small)
            pltpu.make_async_copy(early_ref, early_in, y_local.at[2]).wait()
            put_experts(early_in, pl.ds(0, early_in.shape[-1]))
        for copy in own_rows():
            copy.wait()
        for k in range(1, experts):
            y_copy(k).wait()
        mine = lax.rem(me, experts)

        def near(rows):
            table = [places_ref[pl.ds(flip(mine, k), 1), rows] for k in range(experts)]
            return jnp.concatenate(table, axis=0).T

        def add(index, carry):
            here, _, total = put_together(near, yh_s, index, 256)
            db_s[here, :] = total + sy_ref[here, :].astype(F32)
            return carry

        lax.fori_loop(0, span // 256, add, 0)
        db_out[...] = db_s[away, :].astype(BF16)
        swap_y = to_other(db_out, db_in.at[1], 4)
        swap_y.start()
        swap_y.wait()
        out = db_s[own, :] + db_in[1].astype(F32)
        lo_ref[...] = (h_ref[...] + out).astype(BF16)
        if sends:
            take(late)
            put_experts(late_in, pl.ds(early_in.shape[-1], late_in.shape[-1]))
            for k in range(1, 4):
                z_copy(k).wait()
            total = all_ranks(total_ref)
            hidden = total.shape[1] // 3
            for kind in range(3):
                gsh_refs[kind][...] = total[:, kind * hidden : (kind + 1) * hidden]
            for pair in range(pairs):
                take(pair)
                total = all_ranks(gw_ref, pair)
                for kind in range(4):
                    go_refs[kind][:, pair * LANES : (pair + 1) * LANES] = total[
                        :, kind * LANES : (kind + 1) * LANES
                    ]
            take(small)
            gs_ref[...] = all_ranks(small_in)
        else:
            gs_ref[:, : turned.shape[1]] = turned


def attn_backward(
    length, places, gates, rows, dx_home, gate_grads, y_near, shared_y, shares, late, early,
    shared_dx, ffn_in, hidden_rows, grad_ffn, layer_rows, attn_in, first_all, qkv_rot, context,
    cosine, sine, ranks, halves,
):
    span, width = attn_in.shape
    half = span // 2
    experts = places.shape[0]
    pairs = context.shape[1] // LANES
    shard = width // ranks
    sends = halves
    far = pl.BlockSpec(memory_space=pl.ANY)
    if sends:
        hidden = shares.shape[-1] // 3
        forms = (
            [(shard, pairs * LANES)] * 4
            + [(shard, experts, hidden)] * 3
            + [(shard, hidden)] * 3
            + [(shard, LANES)]
        )
        outs = [(form, F32) for form in forms]
        extra = [
            pltpu.VMEM((ranks, pairs, shard, 4 * LANES), BF16),
            pltpu.VMEM(shares.shape, BF16),
            pltpu.VMEM(late.shape, BF16),
            pltpu.VMEM(early.shape, BF16),
            pltpu.VMEM((ranks, shard, LANES), F32),
        ]
    else:
        outs = [((pairs, width, 4 * LANES), BF16), ((width, LANES), F32)]
        extra = []
    outs = [((half, width), BF16)] * 2 + outs
    return pl.pallas_call(
        functools.partial(attn_bwd_kernel, block=256, ranks=ranks, halves=halves, sends=sends),
        grid=(pairs,),
        in_specs=[pl.BlockSpec(memory_space=pltpu.SMEM)]
        + [
            whole(v.shape)
            for v in (
                places, gates, rows, dx_home, gate_grads, shared_dx, ffn_in, hidden_rows, grad_ffn,
                layer_rows, attn_in,
            )
        ]
        + [
            pl.BlockSpec((width, 3 * LANES), lambda i: (0, i)),
            pl.BlockSpec((width, LANES), lambda i: (0, 3 * pairs + i)),
            pl.BlockSpec((span, 3 * LANES), lambda i: (0, i)),
            pl.BlockSpec((span, LANES), lambda i: (0, i)),
            whole((span, LANES)),
            whole((span, LANES)),
            whole((span, width)),
        ]
        + [far] * 4,
        out_specs=[whole(form) for form, _ in outs],
        out_shape=[jax.ShapeDtypeStruct(form, kind) for form, kind in outs],
        scratch_shapes=extra
        + [
            pltpu.VMEM((span, width), F32),
            pltpu.VMEM((span, experts), F32),
            pltpu.VMEM((half, width), BF16),
            pltpu.VMEM((2, half, width), BF16),
            pltpu.VMEM((half, width), F32),
            pltpu.VMEM((span, width), BF16),
            pltpu.VMEM((span, width), F32),
            pltpu.VMEM((16, width), F32),
            pltpu.VMEM((16, width), F32),
            pltpu.VMEM((width, LANES), F32),
            pltpu.VMEM(y_near.shape, BF16),
            pltpu.VMEM((pairs, width, 4 * LANES), BF16),
            pltpu.VMEM((span, LANES), BF16),
            pltpu.VMEM((span, LANES), F32),
            pltpu.VMEM((span, LANES), F32),
            pltpu.VMEM((span, LANES), F32),
            pltpu.SemaphoreType.DMA((pairs + 2, ranks)),
            pltpu.SemaphoreType.DMA((pairs + 2, ranks)),
            pltpu.SemaphoreType.DMA((pairs + 2,)),
            pltpu.SemaphoreType.DMA((5,)),
            pltpu.SemaphoreType.DMA((5,)),
            pltpu.SemaphoreType.DMA((experts,)),
            pltpu.SemaphoreType.DMA((experts,)),
            pltpu.SemaphoreType.DMA((3,)),
            pltpu.SemaphoreType.DMA((4,)),
            pltpu.SemaphoreType.DMA((4,)),
        ],
        compiler_params=remote_params(5),
        cost_estimate=cost(40e9, 40e6, 6e6),
        name="attn_bwd",
    )(
        length, places, gates, rows, dx_home, gate_grads, shared_dx, ffn_in, hidden_rows, grad_ffn,
        layer_rows, attn_in, first_all, first_all, qkv_rot, context, cosine, sine, shared_y,
        y_near, shares, late, early,
    )


def column_of(row):
    count = row.shape[1]
    shape = (count, count)
    same = lax.broadcasted_iota(jnp.int32, shape, 0) == lax.broadcasted_iota(jnp.int32, shape, 1)
    return jnp.sum(jnp.where(same, row, 0.0), axis=1, keepdims=True)


def row_of(column):
    count = column.shape[0]
    shape = (count, count)
    same = lax.broadcasted_iota(jnp.int32, shape, 0) == lax.broadcasted_iota(jnp.int32, shape, 1)
    return jnp.sum(jnp.where(same, column, 0.0), axis=0, keepdims=True)


def ffn_block(x, grad, gate, gate_w, up_w, down_w, sums):
    gate_pre = mm(x, gate_w, NN)
    up_pre = mm(x, up_w, NN)
    sig = jax.nn.sigmoid(gate_pre)
    act = gate_pre * sig
    inner = (act * up_pre).astype(BF16)
    out = mm(inner, down_w, NT)
    gate_grad, out_grad = None, grad
    if gate is not None:
        wide = grad.astype(F32)
        gate_grad = jnp.sum(out * wide, axis=1, keepdims=True)
        out = out * gate
        out_grad = (wide * gate).astype(BF16)
    inner_grad = mm(out_grad, down_w, NN)
    gate_pre_grad = (inner_grad * up_pre * (sig + act * (1.0 - sig))).astype(BF16)
    up_pre_grad = (inner_grad * act).astype(BF16)
    row_grad = mm(gate_pre_grad, gate_w, NT) + mm(up_pre_grad, up_w, NT)
    sums[0][...] += mm(x, gate_pre_grad, TN)
    sums[1][...] += mm(x, up_pre_grad, TN)
    sums[2][...] += mm(out_grad, inner, TN)
    return out, row_grad, gate_grad


def sides(rank):
    x, y = lax.rem(rank, 2), lax.rem(lax.div(rank, 2), 2)
    return x, y, flip(rank, 1), flip(rank, 2)


def block_of(x_ref, d_ref, g_ref, w_refs, sums):
    slots, width = x_ref.shape[1:]
    shape = (width, w_refs[0].shape[-1])
    gate = column_of(jnp.concatenate([g_ref[0, 0:1, :], g_ref[1, 0:1, :]], axis=1))
    return ffn_block(
        x_ref[...].reshape(2 * slots, width), d_ref[...].reshape(2 * slots, width), gate,
        *(w_ref[...].reshape(shape) for w_ref in w_refs), sums,
    )


def put_sums(og_ref, sums):
    for index, total in enumerate(sums):
        og_ref[:, index] = total[...].astype(BF16).reshape(og_ref.shape[0], *og_ref.shape[2:])


def expert_first_kernel(
    x_ref, d_ref, g_ref, wg_ref, wu_ref, wd_ref, share_ref,
    y_ref, dx_ref, dg_ref, og_ref, sx_ref, sy_ref,
    ag, au, ad, own_x, own_y, in_x, in_y, send, recv, local, *, halves,
):
    step = pl.program_id(0)
    sums = (ag, au, ad)
    me, core = lax.axis_index("dp"), lax.axis_index("tensor")
    x, y, x_rank, y_rank = sides(me)
    cut = share_ref.shape[-1] // 2
    low, high = pl.ds(0, cut), pl.ds(cut, cut)

    def over_x(place):
        return share_ref.at[:, :, place, :, low]

    def over_y(place):
        return share_ref.at[:, place, :, :, high]

    def copies():
        return (
            remote(over_x(1 - x), in_x, send.at[0], recv.at[0], device(x_rank, core)),
            remote(over_y(1 - y), in_y, send.at[1], recv.at[1], device(y_rank, core)),
        )

    def loads():
        return (
            pltpu.make_async_copy(over_x(x), own_x, local.at[0]),
            pltpu.make_async_copy(over_y(y), own_y, local.at[1]),
        )

    @pl.when(step == 0)
    def _():
        for total in sums:
            total[...] = jnp.zeros_like(total)
        if halves:
            greet([device(x_rank, core), device(y_rank, core)])
            for copy in copies() + loads():
                copy.start()

    out, row_grad, gate_grad = block_of(x_ref, d_ref, g_ref, (wg_ref, wu_ref, wd_ref), sums)
    y_ref[...] = out
    dx_ref[...] = row_grad
    dg_ref[...] = jnp.broadcast_to(row_of(gate_grad), dg_ref.shape)

    @pl.when(step == pl.num_programs(0) - 1)
    def _():
        put_sums(og_ref, sums)
        if halves:
            for copy in copies() + loads():
                copy.wait()
            sx_ref[...] = (own_x[...].astype(F32) + in_x[...].astype(F32)).astype(BF16)
            sy_ref[...] = (own_y[...].astype(F32) + in_y[...].astype(F32)).astype(BF16)


def expert_specs(experts, slots, width, weights, order):
    def group(shape):
        return pl.BlockSpec((None,) + shape, lambda i: (order(i),) + (0,) * len(shape))

    parts, _, shard, hidden = weights.shape
    matrices = [
        pl.BlockSpec(
            (parts, None, shard, hidden), lambda i, k=k: (0, k, 0, 0),
            pipeline_mode=pl.Buffered(1),
        )
        for k in range(3)
    ]
    return group, matrices, [pltpu.VMEM((width, hidden), F32)] * 3


def expert_first(x_slots, d_slots, g_slots, weights, shares, halves):
    experts, _, slots, width = x_slots.shape
    hidden = weights.shape[-1]
    group, matrices, sums = expert_specs(experts, slots, width, weights, lambda i: i)
    rows = group((2, slots, width))
    if halves:
        _, _, _, shard, columns = shares.shape
        part = (shares.shape[0], 2, shard, columns // 2)
    else:
        part = (1, 1, 16, LANES)
    return pl.pallas_call(
        functools.partial(expert_first_kernel, halves=halves),
        grid=(experts,),
        in_specs=[rows, rows, group((2, 8, slots))]
        + matrices
        + [pl.BlockSpec(memory_space=pl.ANY)],
        out_specs=[group((2 * slots, width))] * 2
        + [group((8, 2 * slots)), whole(weights.shape), whole(part), whole(part)],
        out_shape=[jax.ShapeDtypeStruct((experts, 2 * slots, width), F32)] * 2
        + [
            jax.ShapeDtypeStruct((experts, 8, 2 * slots), F32),
            jax.ShapeDtypeStruct(weights.shape, BF16),
            jax.ShapeDtypeStruct(part, BF16),
            jax.ShapeDtypeStruct(part, BF16),
        ],
        scratch_shapes=sums
        + [pltpu.VMEM(part, BF16)] * 4
        + [pltpu.SemaphoreType.DMA((2,))] * 3,
        compiler_params=remote_params(6) if halves else params(1),
        cost_estimate=cost(36 * experts * slots * width * hidden, 40e6),
        name="expert_first",
    )(x_slots, d_slots, g_slots, weights, weights, weights, shares)


def expert_second_kernel(
    x_ref, d_ref, g_ref, wg_ref, wu_ref, wd_ref, yf_ref, dxf_ref, dgf_ref, sx_ref, sy_ref,
    y_ref, dx_home, dg_home, og_ref, share_ref,
    ag, au, ad, own_y, own_dx, ys, dxs, yp, dxp, dgs, out_x, out_y, in_x, in_y,
    core_send, core_recv, send, recv, local, share_send, share_recv, *, experts, halves,
):
    step = pl.program_id(0)
    block = experts - 1 - step
    sums = (ag, au, ad)
    me, core = lax.axis_index("dp"), lax.axis_index("tensor")
    mine = lax.rem(me, experts)
    other = device(me, 1 - core)
    slots = x_ref.shape[1]
    x, y, x_rank, y_rank = sides(me)

    def rank_at(k):
        total, bit = me - mine, 1
        while bit < experts:
            total += bit * lax.rem(lax.div(mine, bit) + lax.div(k, bit), 2)
            bit *= 2
        return total

    def core_copy(k, part):
        src, dst = ((ys, yp), (dxs, dxp))[part]
        return remote(
            src.at[lax.rem(k, 2)], dst.at[k], core_send.at[part, k], core_recv.at[part, k], other
        )

    def home_copy(k, part):
        src, dst = ((dxp, dx_home), (dgs, dg_home))[part]
        return remote(
            src.at[k], dst.at[mine], send.at[part, k], recv.at[part, k],
            device(rank_at(k), core),
        )

    def own_copy(part):
        src, dst = ((dxp, dx_home), (dgs, dg_home))[part]
        return pltpu.make_async_copy(src.at[0], dst.at[mine], local.at[part])

    def go_home(k, part):
        @pl.when(k == 0)
        def _():
            own_copy(part).start()

        @pl.when(k > 0)
        def _():
            home_copy(k, part).start()

    def share_copies():
        return (
            remote(out_x, in_x, share_send.at[0], share_recv.at[0], device(y_rank, core)),
            remote(out_y, in_y, share_send.at[1], share_recv.at[1], device(x_rank, core)),
        )

    @pl.when(step == 0)
    def _():
        greet(cluster_and_core(experts))
        for total in sums:
            total[...] = jnp.zeros_like(total)
        if halves:
            out_x[...] = sx_ref[:, pl.ds(1 - y, 1)]
            out_y[...] = sy_ref[:, pl.ds(1 - x, 1)]
            for copy in share_copies():
                copy.start()

    def settle(k):
        for part in (1, 0):
            core_copy(k, part).wait_recv()
            own, shared = ((own_y, yp), (own_dx, dxp))[part]
            total = (own[...] + shared[k].astype(F32)).astype(BF16)
            if part:
                dxp[k] = total
                go_home(k, 0)
            else:
                y_ref[...] = total

    @pl.when(step < experts)
    def _():
        out, row_grad, gate_grad = block_of(x_ref, d_ref, g_ref, (wg_ref, wu_ref, wd_ref), sums)
        out += yf_ref[...]
        row_grad += dxf_ref[...]

        @pl.when(step >= 1)
        def _():
            settle(block + 1)

        for part in (1, 0):

            @pl.when(step >= 2)
            def _():
                core_copy(block + 2, part).wait_send()

            own, half = ((own_y, ys), (own_dx, dxs))[part]
            value = (out, row_grad)[part]
            own[...] = value[:slots]
            half[lax.rem(block, 2)] = value[slots:].astype(BF16)
            core_copy(block, part).start()
        dgs[block] = jnp.broadcast_to(row_of(gate_grad), dgs.shape[1:]) + dgf_ref[...]
        go_home(block, 1)

    @pl.when(step == experts)
    def _():
        settle(block + 1)
        put_sums(og_ref, sums)
        if halves:
            cut = out_x.shape[-1]
            for copy in share_copies():
                copy.wait()
            kept_x, kept_y = sx_ref[:, pl.ds(y, 1)], sy_ref[:, pl.ds(x, 1)]
            total_x = kept_x.astype(F32) + in_x[...].astype(F32)
            total_y = kept_y.astype(F32) + in_y[...].astype(F32)
            share_ref[:, :, :cut] = total_x.astype(BF16).reshape(share_ref.shape[0], -1, cut)
            share_ref[:, :, cut:] = total_y.astype(BF16).reshape(share_ref.shape[0], -1, cut)
        for part in (0, 1):
            for k in (0, 1):
                core_copy(k, part).wait_send()
            own_copy(part).wait()
            for k in range(1, experts):
                home_copy(k, part).wait()


def expert_second(x_slots, d_slots, g_slots, weights, first, halves):
    experts, _, slots, width = x_slots.shape
    hidden = weights.shape[-1]
    y_first, dx_first, dg_first, sx, sy = first
    far = pl.BlockSpec(memory_space=pl.ANY)
    group, matrices, sums = expert_specs(
        experts, slots, width, weights, lambda i: jnp.maximum(experts - 1 - i, 0)
    )
    rows = group((2, slots, width))
    long, _, shard, cut = sx.shape
    share = (long, shard, 2 * cut)
    return pl.pallas_call(
        functools.partial(expert_second_kernel, experts=experts, halves=halves),
        grid=(experts + 1,),
        in_specs=[rows, rows, group((2, 8, slots))]
        + matrices
        + [group((2 * slots, width))] * 2
        + [group((8, 2 * slots)), whole(sx.shape), whole(sy.shape)],
        out_specs=[
            pl.BlockSpec((None, slots, width), lambda i: (jnp.minimum(experts - i, experts - 1), 0, 0)),
            far,
            far,
            whole(weights.shape),
            whole(share),
        ],
        out_shape=[
            jax.ShapeDtypeStruct((experts, slots, width), BF16),
            jax.ShapeDtypeStruct((experts, slots, width), BF16),
            jax.ShapeDtypeStruct((experts, 8, 2 * slots), F32),
            jax.ShapeDtypeStruct(weights.shape, BF16),
            jax.ShapeDtypeStruct(share, BF16),
        ],
        scratch_shapes=sums
        + [pltpu.VMEM((slots, width), F32)] * 2
        + [pltpu.VMEM((2, slots, width), BF16)] * 2
        + [pltpu.VMEM((experts, slots, width), BF16)] * 2
        + [pltpu.VMEM((experts, 8, 2 * slots), F32)]
        + [pltpu.VMEM((long, 1, shard, cut), BF16)] * 4
        + [pltpu.SemaphoreType.DMA((2, experts))] * 4
        + [pltpu.SemaphoreType.DMA((2,))] * 3,
        compiler_params=remote_params(3),
        cost_estimate=cost(36 * experts * slots * width * hidden, 40e6),
        name="expert_second",
    )(x_slots, d_slots, g_slots, weights, weights, weights, y_first, dx_first, dg_first, sx, sy)


def to_all(values, groups=None):
    count = lax.axis_size("dp") if groups is None else len(groups[0])
    copies = jnp.broadcast_to(values[None], (count,) + values.shape)
    return lax.all_to_all(copies, "dp", 0, 0, axis_index_groups=groups, tiled=True)


def after(values, *earlier):
    return lax.optimization_barrier((values,) + earlier)[0]


def per_device(
    layer_input, seq_lengths, expert_routes, w_query, w_key, w_value, w_output,
    gain_attn, gain_ffn, router_weight, expert_gate, expert_up, expert_down,
    shared_gate, shared_up, shared_down, out_cotangent,
):
    ranks = lax.axis_size("dp")
    _, own_len, width = layer_input.shape
    span = 2 * own_len
    shard = w_query.shape[0]
    pairs = w_query.shape[1] // LANES
    experts, hidden = expert_gate.shape[1:]
    capacity = 4 * span // experts
    slots = capacity // 2
    groups = [list(range(s, s + experts)) for s in range(0, ranks, experts)]

    qkv_own = jnp.stack([w_query, w_key, w_value], axis=1).reshape(shard, 3, pairs, LANES)
    qkv_own = qkv_own.transpose(0, 2, 1, 3).reshape(shard, pairs * 3 * LANES)
    small_own = jnp.concatenate(
        [gain_attn[:, None], gain_ffn[:, None], router_weight], axis=1
    )
    small_own = jnp.pad(small_own, ((0, 0), (0, LANES - small_own.shape[1])))
    first_own = jnp.concatenate([qkv_own, w_output, small_own], axis=1).astype(BF16)
    half = HD // 2
    inverse = np.exp(np.arange(half, dtype=np.float32) * np.float32(-math.log(10000.0) / half))
    angles = np.arange(span, dtype=np.float32)[:, None] * inverse[None, :]
    cos_half, sin_half = np.cos(angles), np.sin(angles)
    cosine = np.concatenate([cos_half] * 4, axis=1)
    sine = np.concatenate([-sin_half, sin_half] * 2, axis=1)

    direct = shard % 16 == 0
    halves = ranks == 16
    first_all = gather_all(first_own).reshape(width, first_own.shape[1])

    def to_experts(columns, *earlier):
        stack = jnp.stack(
            [w[:, :, columns] for w in (expert_gate, expert_up, expert_down)], axis=0
        ).astype(BF16)
        part = stack.shape[-1]
        stack = stack.transpose(2, 0, 1, 3).reshape(1, experts, 3 * shard, part)
        stack = jnp.broadcast_to(stack, (ranks // experts, experts, 3 * shard, part))
        stack = after(stack.reshape(ranks, 3 * shard, part), *earlier)
        gathered = lax.all_to_all(stack, "dp", 0, 0, tiled=True).reshape(ranks, 3, shard, part)
        if not direct:
            gathered = gathered.transpose(1, 0, 2, 3).reshape(1, 3, width, part)
        return gathered

    def from_experts(grads):
        if not direct:
            grads = grads.reshape(3, ranks, shard, grads.shape[-1]).transpose(1, 0, 2, 3)
        return lax.all_to_all(grads, "dp", 0, 0, tiled=True)

    def to_outputs(grads):
        grads = grads.reshape(ranks // experts, experts, 3, shard, grads.shape[-1])
        return jnp.sum(grads.astype(F32), axis=0)

    early = to_experts(slice(0, hidden // 2), first_all)

    shared_own = jnp.concatenate([shared_gate, shared_up, shared_down], axis=1).astype(BF16)
    (
        attn_in, qkv_rot, context, hidden_rows, ffn_in, grad_ffn, places, small, gates, shared_y,
        shared_dx, d_slots, x_slots, g_slots, shared_grads, _,
    ) = attn_forward(
        seq_lengths, layer_input[0], out_cotangent[0], expert_routes.reshape(span, 2).T,
        first_all, shared_own, cosine, sine, experts, slots,
    )
    late = to_experts(slice(hidden // 2, hidden), early, places)

    if halves:
        shares = shared_grads.reshape(4, 2, 2, shard, 3 * hidden)
    else:
        shares = shared_grads[0, :16, :LANES]
        shared_grads = lax.all_to_all(
            shared_grads.reshape(ranks, shard, 3 * hidden), "dp", 0, 0, tiled=True
        )

    y_first, dx_first, dg_first, early_grads, sx, sy = expert_first(
        x_slots, d_slots, g_slots, early, shares, halves
    )
    early_grads = from_experts(early_grads)
    y_near, dx_home, gate_grads, late_grads, shares = expert_second(
        x_slots, d_slots, g_slots, late, (y_first, dx_first, dg_first, sx, sy), halves
    )

    grad_input, layer_output, *grads = attn_backward(
        seq_lengths, places, gates, small, dx_home, gate_grads, y_near, shared_y, shares,
        late_grads, early_grads, shared_dx, ffn_in, hidden_rows, grad_ffn, layer_input[0], attn_in,
        first_all, qkv_rot, context, cosine, sine, ranks, halves,
    )
    if halves:
        attn_grads, expert_grads, shared_grads, small_grads = (
            grads[:4], grads[4:7], grads[7:10], grads[10]
        )
    else:
        attn_grads = grads[0].reshape(pairs, ranks, shard, 4 * LANES).transpose(1, 0, 2, 3)
        attn_grads = lax.all_to_all(attn_grads, "dp", 0, 0, tiled=True)
        attn_grads = jnp.sum(attn_grads.astype(F32), axis=0).reshape(pairs, shard, 4, LANES)
        attn_grads = [
            attn_grads[:, :, k].transpose(1, 0, 2).reshape(shard, pairs * LANES) for k in range(4)
        ]
        small_grads = lax.all_to_all(grads[1].reshape(ranks, shard, LANES), "dp", 0, 0, tiled=True)
        small_grads = jnp.sum(small_grads, axis=0)
        shared_grads = jnp.sum(shared_grads.astype(F32), axis=0)
        shared_grads = [shared_grads[:, k * hidden : (k + 1) * hidden] for k in range(3)]
        late_grads = from_experts(late_grads)
        expert_grads = jnp.concatenate([to_outputs(early_grads), to_outputs(late_grads)], axis=-1)
        expert_grads = [expert_grads[:, k].transpose(1, 0, 2) for k in range(3)]
    return (
        layer_output[None], grad_input[None],
        attn_grads[0], attn_grads[1], attn_grads[2], attn_grads[3],
        small_grads[:, 0], small_grads[:, 1], small_grads[:, 2 : 2 + experts],
        expert_grads[0], expert_grads[1], expert_grads[2],
        shared_grads[0], shared_grads[1], shared_grads[2],
    )


def solution(mesh):
    tokens = P("dp", "tensor", None)
    matrix = P("dp", "tensor")
    expert = P("dp", None, "tensor")
    in_specs = (
        (tokens, P("dp"), P("dp", None, None))
        + (matrix,) * 4
        + (P("dp"), P("dp"), P("dp", None))
        + (expert,) * 3
        + (matrix,) * 3
        + (tokens,)
    )
    out_specs = (
        (tokens, tokens)
        + (matrix,) * 4
        + (P("dp"), P("dp"), P("dp", None))
        + (expert,) * 3
        + (matrix,) * 3
    )
    return jax.shard_map(
        per_device, mesh=mesh, in_specs=in_specs, out_specs=out_specs, check_vma=False
    )
```

time: 654 us -> 594 us (0.908)
  Pallas kernels: 393 us -> 530 us
  waiting for transfers between devices: 83.7 us -> 0.01 us
  other arithmetic: 59.8 us -> 7.23 us
  starting transfers between devices: 55.3 us -> 19.4 us
  between operations: 15.9 us -> 1.78 us
  local copies, waits for them, and re-layouts: 32.3 us -> 25.6 us
    pallas_call x7 -> x5, Pallas kernels: 393 us -> 530 us  [the longest x1 191 us: attn_forward(): pl.pallas_call(functools.partial(attn_fwd_kernel, block=256, gathers=gath...]
    all_gather x1 -> x0, waiting for transfers between devices: 41.2 us -> none  [per_device(): shared_all = lax.all_gather(shared_own, 'dp', axis=0, tiled=True)]
    all_to_all x5 -> x3, waiting for transfers between devices: 40.4 us -> 0.01 us  [the longest x2 0.01 us: to_experts(): lax.all_to_all(stack, 'dp', 0, 0, tiled=True).reshape(ranks, 3, shard, part)]
    all_to_all x5 -> x3, starting transfers between devices: 53.3 us -> 19.4 us  [the longest x2 13.8 us: to_experts(): lax.all_to_all(stack, 'dp', 0, 0, tiled=True).reshape(ranks, 3, shard, part)]
    reduce_sum x9 -> x0, other arithmetic: 14.2 us -> none  [the longest x1 4.24 us: per_device(): expert_grads = jnp.sum(expert_grads.astype(F32), axis=0)]
    concatenate x6 -> x0, other arithmetic: 12.2 us -> none  [the longest x4 6.37 us: both_halves(): jnp.concatenate([jnp.where(first, own, other), jnp.where(first, other, ow...]
    convert_element_type x8 -> x0, other arithmetic: 8.12 us -> none  [the longest x1 2.19 us: per_device(): grad_attn = both_halves(grad_hidden.astype(BF16))]
    unnamed x71 -> x51, local copies, waits for them, and re-layouts: 13 us -> 18.7 us
  transfers between devices with their start and end apart: 15 -> 3, of which waited for: 6 -> 0; matrix products, arithmetic and copies ran while one was open for 13% -> 0% of each run, Pallas kernels for 61% -> 57%
where the time goes in v3:
time: 594 us; the launch traced here: 584 us
  Pallas kernels  530 us (89%)
  local copies, waits for them, and re-layouts  25.6 us (4%)
  starting transfers between devices  19.4 us (3%)
  other arithmetic  7.23 us (1%)
    pallas_call x1, Pallas kernels, attn_forward(): pl.pallas_call(functools.partial(attn_fwd_kernel, block=256, gathers=gath...  191 us
    pallas_call x1, Pallas kernels, attn_backward(): pl.pallas_call(functools.partial(attn_bwd_kernel, block=256, ranks=ranks,...  165 us
    pallas_call x1, Pallas kernels, expert_second(): pl.pallas_call(functools.partial(expert_second_kernel, experts=experts, h...  85.5 us
    pallas_call x1, Pallas kernels, expert_first(): pl.pallas_call(functools.partial(expert_first_kernel, halves=halves), gri...  57.1 us
    pallas_call x1, Pallas kernels, gather_all(): pl.pallas_call(gather_kernel, in_specs=[pl.BlockSpec(memory_space=pl.ANY)...  30.8 us
    unnamed x51, local copies, waits for them, and re-layouts  18.7 us
    all_to_all x2, starting transfers between devices, to_experts(): lax.all_to_all(stack, 'dp', 0, 0, tiled=True).reshape(ranks, 3, shard, part)  13.8 us
  transfers between devices with their start and end apart: 3, of which 0 were waited for; matrix products, arithmetic and copies ran while one was open for 0% of the time, Pallas kernels for 57%

profile of v3, /device:TPU:0, one launch (start us, length us, event | category | flops | bytes accessed | tf_op | source)
XLA Modules:
  0.0 583.7 jit_solution(15863353727526818926)
XLA Ops:
  0.7 0.8 convert.71
  1.5 0.7 convert_bitcast_fusion
  2.2 0.1 copy.51
  2.3 0.9 convert.65
  3.2 0.9 convert.66
  4.1 0.9 convert.67
  5.0 0.1 maximum_bitcast_fusion
  5.1 0.1 copy.50
  5.3 0.9 convert.68
  6.3 0.1 convert.75
  6.4 1.2 copy-done.3
  7.7 0.1 convert.76
  7.8 1.2 copy-done.4
  9.1 0.1 convert.77
  9.2 0.3 pad_maximum_fusion
  9.5 0.4 copy.53
  9.9 0.7 fusion.1.own_ref
  10.6 30.8 %gather_attn.1 = bf16[16,48,1664]{2,1,0:T(8,128)(2,1)} custom-call(bf16[48,1664]{1,0:T(8,128)(2,1)} %fusion.1.own_ref), custom_call_target="tpu_custom_call" | custom-call | flops 1000000 | bytes 60000000 | tf_op jit(solution)/shard_map/gather_attn/pallas_call | solution.py:205
  41.4 1.7 broadcast_in_dim.33
  43.1 5.1 all-to-all-start
  49.0 0.4 copy.52
  49.3 0.7 pad_maximum_fusion.2.shared_ref
  50.1 191.1 %attn_fwd.1 = (bf16[1024,768]{1,0:T(8,128)(2,1)}, bf16[1024,1152]{1,0:T(8,128)(2,1)}, bf16[1024,384]{1,0:T(8,128)(2,1)}, f32[512,768]{1,0:T(8,128)}, bf16[1024,7...) custom-call(s32[1]{0:T(128)S(6)} %copy.67.len_ref, ...), custom_call_target="tpu_custom_call" | custom-call | flops 20000000000 | bytes 60000000 | tf_op jit(solution)/shard_map/attn_fwd/pallas_call | solution.py:494
  241.2 1.6 broadcast_in_dim.31
  242.9 8.7 %all-to-all-start.1 = ((bf16[16,144,512]{2,1,0:T(8,128)(2,1)}), bf16[16,144,512]{2,1,0:T(8,128)(2,1)S(1)}, u32[]{:S(2)}, u32[]{:S(2)}) async-start(bf16[16,144,512]{2,1,0:T(8,128)(2,1)} %bitcast.13), calls=%async_computation.1 | async-start | bytes 4718592 | tf_op jit(solution)/shard_map/all_to_all | solution.py:1338
  251.5 57.1 %expert_first.1 = (f32[8,512,768]{2,1,0:T(8,128)}, f32[8,512,768]{2,1,0:T(8,128)}, f32[8,8,512]{2,1,0:T(8,128)}, bf16[16,3,48,512]{3,2,1,0:T(8,128)(2,1)}, bf16[...) custom-call(bf16[8,2,256,768]{3,2,1,0:T(8,128)(2,1)} %get-tuple-element.59.x_ref, ...), custom_call_target="tpu_custom_call" | custom-call | flops 28991029248 | bytes 40000000 | tf_op jit(solution)/shard_map/expert_first/pallas_call | solution.py:1096
  308.6 1.4 copy-done.1
  310.0 5.6 all-to-all-start.2
  315.6 85.5 %expert_second.1 = (bf16[8,256,768]{2,1,0:T(8,128)(2,1)}, bf16[8,256,768]{2,1,0:T(8,128)(2,1)}, f32[8,8,512]{2,1,0:T(8,128)}, bf16[16,3,48,512]{3,2,1,0:T(8,128)(2,1)}, bf16[4,48,3072]{2,1,0:T(8,128)(2,1)}) custom-call(bf16[8,2,256,768]{3,2,1,0:T(8,128)(2,1)} %get-tuple-element.59.x_ref, bf16[8,2,256,768]{3,2,1,0:T(8,128)(2,1)} %get-tuple-element.60.d_ref, ...), custom_call_target="tpu_custom_call" | custom-call | flops 28991029248 | bytes 40000000 | tf_op jit(solution)/shard_map/expert_second/pallas_call | solution.py:1252
  401.1 1.4 copy-done
  402.5 165.2 %attn_bwd.1 = (bf16[512,768]{1,0:T(8,128)(2,1)}, bf16[512,768]{1,0:T(8,128)(2,1)}, f32[48,384]{1,0:T(8,128)}, f32[48,384]{1,0:T(8,128)}, f32[48,384]{1,0:T(8,128...) custom-call(s32[1]{0:T(128)S(6)} %copy.67.len_ref, ...), custom_call_target="tpu_custom_call" | custom-call | flops 40000000000 | bytes 40000000 | tf_op jit(solution)/shard_map/attn_bwd/pallas_call | solution.py:898
  567.7 1.5 slice_reduce_fusion
  569.2 0.8 slice.41
  570.1 0.7 copy.54
  570.7 2.2 copy.68
  572.9 0.9 copy.69
  573.8 0.6 copy.70
  574.5 0.6 copy.71
  575.1 0.6 copy.72
  575.7 0.6 copy.73
  576.4 1.1 copy.74
  577.5 0.8 copy-done.6
  578.4 1.1 copy.75
  579.5 0.8 copy-done.5
  580.3 1.1 copy.76
  581.5 0.7 copy.77
  582.2 0.7 copy.78
  582.8 0.7 copy.79
  (46 shorter events, 0.4 us)
Async XLA Ops:
  0.6 5.6 copy-start.2
  6.2 1.4 copy-start.3
  7.7 1.4 copy-start.4
  43.1 5.8 copy-start.9
  43.1 5.8 %copy-start.10 = (f32[48,1024]{1,0:T(8,128)S(1)}, f32[48,1024]{1,0:T(8,128)}, u32[]{:S(2)}) copy-start(f32[48,1024]{1,0:T(8,128)} %param.33) | copy-start | bytes 589828
  43.1 5.9 %copy-start.11 = (f32[48,1024]{1,0:T(8,128)S(1)}, f32[48,1024]{1,0:T(8,128)}, u32[]{:S(2)}) copy-start(f32[48,1024]{1,0:T(8,128)} %param.34) | copy-start | bytes 589828
  43.1 198.2 %all-to-all-start = ((bf16[16,144,512]{2,1,0:T(8,128)(2,1)}), bf16[16,144,512]{2,1,0:T(8,128)(2,1)}, u32[]{:S(2)}, u32[]{:S(2)}) async-start(bf16[16,144,512]{2,1,0:T(8,128)(2,1)} %bitcast.19), calls=%async_computation | async-start | bytes 4718592 | tf_op jit(solution)/shard_map/all_to_all | solution.py:1338
  242.9 65.8 %all-to-all-start.1 = ((bf16[16,144,512]{2,1,0:T(8,128)(2,1)}), bf16[16,144,512]{2,1,0:T(8,128)(2,1)S(1)}, u32[]{:S(2)}, u32[]{:S(2)}) async-start(bf16[16,144,512]{2,1,0:T(8,128)(2,1)} %bitcast.13), calls=%async_computation.1 | async-start | bytes 4718592 | tf_op jit(solution)/shard_map/all_to_all | solution.py:1338
  308.6 1.4 copy-start.1
  310.0 91.0 %all-to-all-start.2 = ((bf16[16,3,48,512]{3,2,1,0:T(8,128)(2,1)}), bf16[16,3,48,512]{3,2,1,0:T(8,128)(2,1)S(1)}, u32[]{:S(2)}, u32[]{:S(2)}) async-start(bf16[16,3,48,512]{3,2,1,0:T(8,128)(2,1)} %get-tuple-element.83), calls=%async_computation.2 | async-start | bytes 4718592 | tf_op jit(solution)/shard_map/all_to_all | solution.py:1346
  401.1 1.4 copy-start
  567.7 5.2 copy-start.8
  570.7 3.1 copy-start.18
  570.7 3.7 copy-start.17
  570.7 4.4 copy-start.16
  570.7 5.0 copy-start.15
  570.7 5.6 copy-start.7
  576.4 2.0 copy-start.6
  578.3 2.0 copy-start.5
  580.3 1.2 copy-start.14
  580.3 1.8 copy-start.13
  580.3 2.5 copy-start.12

commit v4 on v3

--- a/solution.py
+++ b/solution.py
@@ -177,9 +177,24 @@
         self.own_copy().wait()
 
 
-def gather_kernel(own_ref, out_ref, *sems):
-    gather = Gather(own_ref, out_ref, sems, 0)
-    z, core = gather.z, gather.core
+def gather_kernel(
+    wq_ref, wk_ref, wv_ref, wo_ref, small_ref, sg_ref, su_ref, sd_ref, first_out, shared_out,
+    first_s, shared_s, *sems,
+):
+    pairs = wq_ref.shape[1] // LANES
+    for pair in range(pairs):
+        columns = slice(pair * LANES, (pair + 1) * LANES)
+        for kind, ref in enumerate((wq_ref, wk_ref, wv_ref)):
+            start = (3 * pair + kind) * LANES
+            first_s[:, start : start + LANES] = ref[:, columns].astype(BF16)
+    first_s[:, 3 * pairs * LANES : 4 * pairs * LANES] = wo_ref[...].astype(BF16)
+    first_s[:, 4 * pairs * LANES :] = small_ref[...].astype(BF16)
+    hidden = sg_ref.shape[1]
+    for kind, ref in enumerate((sg_ref, su_ref, sd_ref)):
+        shared_s[:, kind * hidden : (kind + 1) * hidden] = ref[...].astype(BF16)
+
+    gathers = Gather(first_s, first_out, sems, 0), Gather(shared_s, shared_out, sems, 1)
+    z, core = gathers[0].z, gathers[0].core
     barrier = pltpu.get_barrier_semaphore()
 
     def hello(rank):
@@ -187,31 +202,51 @@
             barrier, inc=1, device_id=device(rank, core), device_id_type=pl.DeviceIdType.MESH
         )
 
-    for rank in gather.sides_of:
+    for rank in gathers[0].sides_of:
         hello(rank)
-    pl.when(z < 3)(lambda: hello(gather.up))
-    pl.when(z > 0)(lambda: hello(gather.down))
+    pl.when(z < 3)(lambda: hello(gathers[0].up))
+    pl.when(z > 0)(lambda: hello(gathers[0].down))
     pl.semaphore_wait(barrier, 2 + lax.min(z, 1) + lax.min(3 - z, 1))
-    gather.begin()
-    for turn in range(1, gather.turns):
-        gather.turn(turn)
-    gather.end()
-
-
-def gather_all(own):
+    for gather in gathers:
+        gather.begin()
+    for turn in range(1, Gather.turns):
+        for gather in gathers:
+            gather.turn(turn)
+    for gather in gathers:
+        gather.end()
+
+
+def gather_weights(attention, small, shared):
     ranks = lax.axis_size("dp")
+    rows, heads_width = attention[0].shape
+    columns = 4 * heads_width + LANES
+    hidden = shared[0].shape[1]
     if ranks != 16:
-        return to_all(own)
+        pairs = heads_width // LANES
+        qkv = jnp.stack(attention[:3], axis=1).reshape(rows, 3, pairs, LANES)
+        qkv = qkv.transpose(0, 2, 1, 3).reshape(rows, 3 * heads_width)
+        first = jnp.concatenate([qkv, attention[3], small], axis=1).astype(BF16)
+        return to_all(first), to_all(jnp.concatenate(shared, axis=1).astype(BF16))
+    vmem = pl.BlockSpec(memory_space=pltpu.VMEM)
     return pl.pallas_call(
         gather_kernel,
-        in_specs=[pl.BlockSpec(memory_space=pl.ANY)],
-        out_specs=pl.BlockSpec(memory_space=pl.ANY),
-        out_shape=jax.ShapeDtypeStruct((ranks,) + own.shape, own.dtype),
-        scratch_shapes=Gather.semaphores(1),
-        compiler_params=pltpu.CompilerParams(collective_id=1, has_side_effects=True),
-        cost_estimate=cost(1e6, 60e6),
-        name="gather_attn",
-    )(own)
+        in_specs=[vmem] * 8,
+        out_specs=[pl.BlockSpec(memory_space=pl.ANY)] * 2,
+        out_shape=[
+            jax.ShapeDtypeStruct((ranks, rows, columns), BF16),
+            jax.ShapeDtypeStruct((ranks, rows, 3 * hidden), BF16),
+        ],
+        scratch_shapes=[
+            pltpu.VMEM((rows, columns), BF16),
+            pltpu.VMEM((rows, 3 * hidden), BF16),
+        ]
+        + Gather.semaphores(2),
+        compiler_params=pltpu.CompilerParams(
+            collective_id=1, has_side_effects=True, vmem_limit_bytes=VMEM_LIMIT
+        ),
+        cost_estimate=cost(1e6, 100e6),
+        name="gather_weights",
+    )(*attention, small, *shared)
 
 
 def partner(values):
@@ -292,10 +327,9 @@
 
 def attn_fwd_kernel(
     len_ref, x_ref, c_ref, routes_ref, w_ref, wo_ref, small_ref, shared_ref, cos_ref, sin_ref,
-    a_ref, qkv_ref, ctx_ref, h_ref, b_ref, d_ref, places_ref, rows_ref, gates_ref, y_ref, dx_ref, dr, xr, gr, og_ref, shared_all,
+    a_ref, qkv_ref, ctx_ref, h_ref, b_ref, d_ref, places_ref, rows_ref, gates_ref, y_ref, dx_ref, dr, xr, gr, og_ref,
     ds, xs, gs, ag, au, ad, shared_w, part, x_in, h_in, b_out, b_in, c_out, c_in,
-    send, recv, core_send, core_recv, local, pair_send, pair_recv, load, *gather_sems,
-    block, gathers,
+    send, recv, core_send, core_recv, local, pair_send, pair_recv, load, *, block,
 ):
     step = pl.program_id(0)
     me, core = lax.axis_index("dp"), lax.axis_index("tensor")
@@ -314,30 +348,14 @@
     own = pl.ds(pl.multiple_of(core * half, half), half)
     away = pl.ds(pl.multiple_of((1 - core) * half, half), half)
     pairs = pl.num_programs(0)
-    if gathers:
-        shared = Gather(shared_ref, shared_all, gather_sems, 0)
 
     def to_other(src, dst, index):
         return remote(src, dst, pair_send.at[index], pair_recv.at[index], other)
 
     @pl.when(step == 0)
     def _():
-        if gathers:
-            z = lax.div(me, 4)
-            barrier = pltpu.get_barrier_semaphore()
-
-            def hello(target):
-                pl.semaphore_signal(
-                    barrier, inc=1, device_id=target, device_id_type=pl.DeviceIdType.MESH
-                )
-
-            for target in cluster_and_core(experts):
-                hello(target)
-            pl.when(z == 1)(lambda: hello(device(shared.up, core)))
-            pl.when(z == 2)(lambda: hello(device(shared.down, core)))
-            pl.semaphore_wait(barrier, experts + lax.min(z, 1) * lax.min(3 - z, 1))
-        else:
-            greet(cluster_and_core(experts))
+        greet(cluster_and_core(experts))
+        pltpu.make_async_copy(shared_ref, shared_w, load).start()
         token = core * half + lax.broadcasted_iota(jnp.int32, c_ref.shape, 0)
         valid = jnp.where(token < length, c_ref[...].astype(F32), 0.0).astype(BF16)
         c_out[...] = valid
@@ -364,8 +382,6 @@
             hot = jnp.where(slot == place, 1.0, 0.0).astype(BF16)
             ds[k] = mm(hot, d_ref[...], NN).astype(BF16)
             trips[0].go(k)
-        if gathers:
-            shared.begin()
         rows_ref[...] = small_ref[...].astype(F32).T[: rows_ref.shape[0], :]
         swap_x.wait_recv()
         gain = rows_ref[0:1, :]
@@ -403,10 +419,6 @@
         context = jnp.where(head_lanes(parts[0].shape, 0), parts[0], parts[1]).astype(BF16)
         ctx_ref[index * block : keys, :] = context
         part[index * block : keys, :] += mm(context, wo_ref[...], NT)
-
-    if gathers:
-        for turn in range(1, 3):
-            pl.when(step == turn - 1)(functools.partial(shared.turn, turn))
 
     @pl.when(step == pairs - 1)
     def _():
@@ -440,13 +452,7 @@
         swap_b.wait_send()
         for total in (ag, au, ad):
             total[...] = jnp.zeros_like(total)
-        if gathers:
-            for turn in range(3, shared.turns):
-                shared.turn(turn)
-            shared.end()
-        read = pltpu.make_async_copy(shared_all if gathers else shared_ref, shared_w, load)
-        read.start()
-        read.wait()
+        pltpu.make_async_copy(shared_ref, shared_w, load).wait()
         for k in offsets(experts):
             trips[0].pass_on(k)
         hidden = ag.shape[1]
@@ -478,21 +484,14 @@
         write.wait()
 
 
-def attn_forward(length, rows, cotangent, routes, first_all, shared_own, cosine, sine, experts, slots):
+def attn_forward(length, rows, cotangent, routes, first_all, shared_all, cosine, sine, experts, slots):
     half, width = rows.shape
     span = 2 * half
-    ranks = lax.axis_size("dp")
     pairs = (first_all.shape[1] - LANES) // (4 * LANES)
-    gathers = ranks == 16
     far = pl.BlockSpec(memory_space=pl.ANY)
-    hidden = shared_own.shape[1] // 3
-    if gathers:
-        shared, parts = shared_own, (ranks,) + shared_own.shape
-    else:
-        parts = (1, width, shared_own.shape[1])
-        shared = to_all(shared_own).reshape(parts)
+    hidden = shared_all.shape[-1] // 3
     return pl.pallas_call(
-        functools.partial(attn_fwd_kernel, block=256, gathers=gathers),
+        functools.partial(attn_fwd_kernel, block=256),
         grid=(pairs,),
         in_specs=[
             pl.BlockSpec(memory_space=pltpu.SMEM),
@@ -519,7 +518,7 @@
             whole((span, width)),
             whole((span, width)),
         ]
-        + [far] * 5,
+        + [far] * 4,
         out_shape=[
             jax.ShapeDtypeStruct((span, width), BF16),
             jax.ShapeDtypeStruct((span, pairs * 3 * LANES), BF16),
@@ -535,8 +534,7 @@
             jax.ShapeDtypeStruct((experts, 2, slots, width), BF16),
             jax.ShapeDtypeStruct((experts, 2, slots, width), BF16),
             jax.ShapeDtypeStruct((experts, 2, 8, slots), F32),
-            jax.ShapeDtypeStruct(parts, BF16),
-            jax.ShapeDtypeStruct(parts if gathers else (1, 16, LANES), BF16),
+            jax.ShapeDtypeStruct(shared_all.shape, BF16),
         ],
         scratch_shapes=[
             pltpu.VMEM((experts, slots, width), BF16),
@@ -545,7 +543,7 @@
             pltpu.VMEM((width, hidden), F32),
             pltpu.VMEM((width, hidden), F32),
             pltpu.VMEM((width, hidden), F32),
-            pltpu.VMEM(parts, BF16),
+            pltpu.VMEM(shared_all.shape, BF16),
             pltpu.VMEM((span, width), F32),
             pltpu.VMEM((half, width), BF16),
             pltpu.VMEM((half, width), F32),
@@ -554,12 +552,11 @@
         + [pltpu.SemaphoreType.DMA((3, experts))] * 4
         + [pltpu.SemaphoreType.DMA((3,))]
         + [pltpu.SemaphoreType.DMA((4,))] * 2
-        + [pltpu.SemaphoreType.DMA]
-        + Gather.semaphores(1),
+        + [pltpu.SemaphoreType.DMA],
         compiler_params=remote_params(4),
         cost_estimate=cost(20e9, 60e6, 6e6),
         name="attn_fwd",
-    )(length, rows, cotangent, routes, first_all, first_all, first_all, shared, cosine, sine)
+    )(length, rows, cotangent, routes, first_all, first_all, first_all, shared_all, cosine, sine)
 
 
 def norm_back(grad, values, gain):
@@ -586,8 +583,9 @@
 ):
     if sends:
         go_refs, gx_refs, gsh_refs, gs_ref = rest[:4], rest[4:7], rest[7:10], rest[10]
-        gw_ref, total_ref, late_in, early_in, small_in = rest[11:16]
-        rest = rest[16:]
+        sum_x, sum_y, in_x, in_y, sums, in_z, total_ref, late_in, early_in, small_in = rest[11:21]
+        step_send, step_recv = rest[21:23]
+        rest = rest[23:]
     else:
         gw_ref, gs_ref = rest[:2]
         rest = rest[2:]
@@ -612,18 +610,14 @@
     def to_other(src, dst, index):
         return remote(src, dst, pair_send.at[index], pair_recv.at[index], other)
 
-    small, late = pairs, pairs + 1
+    small, late = 0, 1
 
     def part_of(index, rank):
         rows = pl.ds(pl.multiple_of(rank * shard, shard), shard)
-        if index is late:
-            return late_ref.at[rank]
-        return turned_s.at[rows] if index is small else gw_s.at[index, rows]
+        return late_ref.at[rank] if index == late else turned_s.at[rows]
 
     def place_of(index, rank):
-        if index is late:
-            return late_in.at[rank]
-        return small_in.at[rank] if index is small else gw_ref.at[rank, index]
+        return late_in.at[rank] if index == late else small_in.at[rank]
 
     def share(index, offset):
         rank = lax.rem(me + offset, ranks)
@@ -658,6 +652,74 @@
         for rank in range(1, ref.shape[0]):
             total += ref[(rank,) + index].astype(F32)
         return total
+
+    x, y, x_rank, y_rank = sides(me)
+    z = lax.div(me, 4)
+    cut = gw_s.shape[-1] // 2
+    low, high = slice(0, cut), slice(cut, 2 * cut)
+
+    def step_copy(src, dst, index, pair, rank):
+        return remote(
+            src, dst, step_send.at[index, pair], step_recv.at[index, pair], device(rank, core)
+        )
+
+    def sides_first(pair):
+        return (
+            step_copy(gw_s.at[pair, :, :, 1 - x, :, low], sum_x.at[pair], 0, pair, x_rank),
+            step_copy(gw_s.at[pair, :, 1 - y, :, :, high], sum_y.at[pair], 1, pair, y_rank),
+        )
+
+    def sides_second(pair):
+        return (
+            step_copy(sum_x.at[pair, :, 1 - y], in_x.at[pair], 2, pair, y_rank),
+            step_copy(sum_y.at[pair, :, 1 - x], in_y.at[pair], 3, pair, x_rank),
+        )
+
+    def along_z(pair):
+        copies = []
+        for offset in range(1, 4):
+            rank = flip(me, 4 * offset)
+            copies.append(
+                step_copy(
+                    sums.at[pair, lax.div(rank, 4)], in_z.at[pair, offset - 1], 3 + offset, pair, rank
+                )
+            )
+        return copies
+
+    def begin_sum(pair):
+        for copy in sides_first(pair):
+            copy.start()
+
+    def go_on(pair):
+        for copy in sides_first(pair):
+            copy.wait()
+        own_x = gw_s[pair, :, :, pl.ds(x, 1), :, low].reshape(sum_x.shape[1:])
+        own_y = gw_s[pair, :, pl.ds(y, 1), :, :, high].reshape(sum_y.shape[1:])
+        sum_x[pair] = (sum_x[pair].astype(F32) + own_x.astype(F32)).astype(BF16)
+        sum_y[pair] = (sum_y[pair].astype(F32) + own_y.astype(F32)).astype(BF16)
+        for copy in sides_second(pair):
+            copy.start()
+
+    def go_along(pair):
+        for copy in sides_second(pair):
+            copy.wait()
+        own_x = sum_x[pair, :, pl.ds(y, 1)].reshape(in_x.shape[1:])
+        own_y = sum_y[pair, :, pl.ds(x, 1)].reshape(in_y.shape[1:])
+        sums[pair, :, :, low] = (in_x[pair].astype(F32) + own_x.astype(F32)).astype(BF16)
+        sums[pair, :, :, high] = (in_y[pair].astype(F32) + own_y.astype(F32)).astype(BF16)
+        for copy in along_z(pair):
+            copy.start()
+
+    def end_sum(pair):
+        for copy in along_z(pair):
+            copy.wait()
+        total = sums[pair, pl.ds(z, 1)].reshape(shard, 2 * cut).astype(F32)
+        for offset in range(3):
+            total += in_z[pair, offset].astype(F32)
+        for kind in range(4):
+            go_refs[kind][:, pair * LANES : (pair + 1) * LANES] = total[
+                :, kind * LANES : (kind + 1) * LANES
+            ]
 
     def put_experts(ref, columns):
         for kind in range(3):
@@ -756,7 +818,7 @@
 
     grad_rows = grad_s[...]
     dctx_s[...] = mm(grad_rows, wo_ref[...], NN).astype(BF16)
-    gw_s[step, :, 3 * LANES :] = mm(grad_rows, ctx_ref[...], TN).astype(BF16)
+    out_grads = mm(grad_rows, ctx_ref[...], TN).astype(BF16)
     dk_s[...] = jnp.zeros_like(dk_s)
     dv_s[...] = jnp.zeros_like(dv_s)
     scale = jnp.asarray(HD**-0.5, BF16)
@@ -793,9 +855,15 @@
     dq = (dq * cosine - partner(dq) * sine).astype(BF16)
     dk = (dk * cosine - partner(dk) * sine).astype(BF16)
     grads = jnp.concatenate([dq, dk, dv_s[...].astype(BF16)], axis=1)
-    gw_s[step, :, : 3 * LANES] = mm(a_ref[...], grads, TN).astype(BF16)
+    in_grads = mm(a_ref[...], grads, TN).astype(BF16)
+    shape = gw_s.shape[1:-1]
+    gw_s[step, ..., : 3 * LANES] = in_grads.reshape(*shape, 3 * LANES)
+    gw_s[step, ..., 3 * LANES :] = out_grads.reshape(*shape, LANES)
     if sends:
-        give(step)
+        for pair in range(pairs):
+            pl.when(step == pair)(functools.partial(begin_sum, pair))
+            pl.when(step == pair + 1)(functools.partial(go_on, pair))
+            pl.when(step == pair + 2)(functools.partial(go_along, pair))
     else:
         gw_ref[step] = gw_s[step]
     da_s[...] += mm(grads, w_ref[...], NT)
@@ -810,6 +878,9 @@
         back, sums_s[0:1, :] = norm_back(da, x_ref[...].astype(F32), rows_ref[0:1, :])
         swap_s = to_other(sums_s, sums_in, 3)
         swap_s.start()
+        if sends:
+            go_on(pairs - 1)
+            go_along(pairs - 2)
         gi_ref[...] = (dh_s[...] + back).astype(BF16)
         swap_s.wait()
         turned = (sums_s[...] + sums_in[...]).T
@@ -818,6 +889,7 @@
             turned_s[:, : turned.shape[1]] = turned
             give(small)
             pltpu.make_async_copy(early_ref, early_in, y_local.at[2]).wait()
+            go_along(pairs - 1)
             put_experts(early_in, pl.ds(0, early_in.shape[-1]))
         for copy in own_rows():
             copy.wait()
@@ -851,12 +923,7 @@
             for kind in range(3):
                 gsh_refs[kind][...] = total[:, kind * hidden : (kind + 1) * hidden]
             for pair in range(pairs):
-                take(pair)
-                total = all_ranks(gw_ref, pair)
-                for kind in range(4):
-                    go_refs[kind][:, pair * LANES : (pair + 1) * LANES] = total[
-                        :, kind * LANES : (kind + 1) * LANES
-                    ]
+                end_sum(pair)
             take(small)
             gs_ref[...] = all_ranks(small_in)
         else:
@@ -885,15 +952,24 @@
         )
         outs = [(form, F32) for form in forms]
         extra = [
-            pltpu.VMEM((ranks, pairs, shard, 4 * LANES), BF16),
+            pltpu.VMEM((pairs, 4, 2, shard, 2 * LANES), BF16),
+            pltpu.VMEM((pairs, 4, 2, shard, 2 * LANES), BF16),
+            pltpu.VMEM((pairs, 4, shard, 2 * LANES), BF16),
+            pltpu.VMEM((pairs, 4, shard, 2 * LANES), BF16),
+            pltpu.VMEM((pairs, 4, shard, 4 * LANES), BF16),
+            pltpu.VMEM((pairs, 3, shard, 4 * LANES), BF16),
             pltpu.VMEM(shares.shape, BF16),
             pltpu.VMEM(late.shape, BF16),
             pltpu.VMEM(early.shape, BF16),
             pltpu.VMEM((ranks, shard, LANES), F32),
+            pltpu.SemaphoreType.DMA((7, pairs)),
+            pltpu.SemaphoreType.DMA((7, pairs)),
         ]
+        blocks = (4, 2, 2, shard)
     else:
         outs = [((pairs, width, 4 * LANES), BF16), ((width, LANES), F32)]
         extra = []
+        blocks = (width,)
     outs = [((half, width), BF16)] * 2 + outs
     return pl.pallas_call(
         functools.partial(attn_bwd_kernel, block=256, ranks=ranks, halves=halves, sends=sends),
@@ -931,14 +1007,14 @@
             pltpu.VMEM((16, width), F32),
             pltpu.VMEM((width, LANES), F32),
             pltpu.VMEM(y_near.shape, BF16),
-            pltpu.VMEM((pairs, width, 4 * LANES), BF16),
+            pltpu.VMEM((pairs,) + blocks + (4 * LANES,), BF16),
             pltpu.VMEM((span, LANES), BF16),
             pltpu.VMEM((span, LANES), F32),
             pltpu.VMEM((span, LANES), F32),
             pltpu.VMEM((span, LANES), F32),
-            pltpu.SemaphoreType.DMA((pairs + 2, ranks)),
-            pltpu.SemaphoreType.DMA((pairs + 2, ranks)),
-            pltpu.SemaphoreType.DMA((pairs + 2,)),
+            pltpu.SemaphoreType.DMA((2, ranks)),
+            pltpu.SemaphoreType.DMA((2, ranks)),
+            pltpu.SemaphoreType.DMA((2,)),
             pltpu.SemaphoreType.DMA((5,)),
             pltpu.SemaphoreType.DMA((5,)),
             pltpu.SemaphoreType.DMA((experts,)),
@@ -1309,13 +1385,15 @@
     slots = capacity // 2
     groups = [list(range(s, s + experts)) for s in range(0, ranks, experts)]
 
-    qkv_own = jnp.stack([w_query, w_key, w_value], axis=1).reshape(shard, 3, pairs, LANES)
-    qkv_own = qkv_own.transpose(0, 2, 1, 3).reshape(shard, pairs * 3 * LANES)
     small_own = jnp.concatenate(
         [gain_attn[:, None], gain_ffn[:, None], router_weight], axis=1
     )
     small_own = jnp.pad(small_own, ((0, 0), (0, LANES - small_own.shape[1])))
-    first_own = jnp.concatenate([qkv_own, w_output, small_own], axis=1).astype(BF16)
+    first_all, shared_all = gather_weights(
+        (w_query, w_key, w_value, w_output), small_own, (shared_gate, shared_up, shared_down)
+    )
+    first_all = first_all.reshape(width, first_all.shape[-1])
+
     half = HD // 2
     inverse = np.exp(np.arange(half, dtype=np.float32) * np.float32(-math.log(10000.0) / half))
     angles = np.arange(span, dtype=np.float32)[:, None] * inverse[None, :]
@@ -1325,7 +1403,6 @@
 
     direct = shard % 16 == 0
     halves = ranks == 16
-    first_all = gather_all(first_own).reshape(width, first_own.shape[1])
 
     def to_experts(columns, *earlier):
         stack = jnp.stack(
@@ -1351,13 +1428,13 @@
 
     early = to_experts(slice(0, hidden // 2), first_all)
 
-    shared_own = jnp.concatenate([shared_gate, shared_up, shared_down], axis=1).astype(BF16)
     (
         attn_in, qkv_rot, context, hidden_rows, ffn_in, grad_ffn, places, small, gates, shared_y,
-        shared_dx, d_slots, x_slots, g_slots, shared_grads, _,
+        shared_dx, d_slots, x_slots, g_slots, shared_grads,
     ) = attn_forward(
         seq_lengths, layer_input[0], out_cotangent[0], expert_routes.reshape(span, 2).T,
-        first_all, shared_own, cosine, sine, experts, slots,
+        first_all, shared_all if direct else shared_all.reshape(1, width, 3 * hidden), cosine, sine,
+        experts, slots,
     )
     late = to_experts(slice(hidden // 2, hidden), early, places)
 

time: 594 us -> 532 us (0.90)
  Pallas kernels: 530 us -> 473 us
    pallas_call x2, Pallas kernels: 222 us -> 192 us  [the longest x1 125 us: attn_forward(): pl.pallas_call(functools.partial(attn_fwd_kernel, block=256), grid=(pairs...]
    pallas_call x1, Pallas kernels: 165 us -> 139 us  [attn_backward(): pl.pallas_call(functools.partial(attn_bwd_kernel, block=256, ranks=ranks,...]
    unnamed x51 -> x43, local copies, waits for them, and re-layouts: 18.7 us -> 17.6 us
  transfers between devices with their start and end apart: 3 -> 3, of which waited for: 0 -> 0; matrix products, arithmetic and copies ran while one was open for 0% -> 0% of each run, Pallas kernels for 57% -> 51%
where the time goes in v4:
time: 532 us; the launch traced here: 523 us
  Pallas kernels  473 us (89%)
  local copies, waits for them, and re-layouts  24.9 us (5%)
  starting transfers between devices  21 us (4%)
    pallas_call x1, Pallas kernels, attn_backward(): pl.pallas_call(functools.partial(attn_bwd_kernel, block=256, ranks=ranks,...  139 us
    pallas_call x1, Pallas kernels, attn_forward(): pl.pallas_call(functools.partial(attn_fwd_kernel, block=256), grid=(pairs...  125 us
    pallas_call x1, Pallas kernels, expert_second(): pl.pallas_call(functools.partial(expert_second_kernel, experts=experts, h...  85.5 us
    pallas_call x1, Pallas kernels, gather_weights(): pl.pallas_call(gather_kernel, in_specs=[vmem] * 8, out_specs=[pl.BlockSpe...  66.6 us
    pallas_call x1, Pallas kernels, expert_first(): pl.pallas_call(functools.partial(expert_first_kernel, halves=halves), gri...  57 us
    unnamed x43, local copies, waits for them, and re-layouts  17.6 us
    all_to_all x2, starting transfers between devices, to_experts(): lax.all_to_all(stack, 'dp', 0, 0, tiled=True).reshape(ranks, 3, shard, part)  15.4 us
  transfers between devices with their start and end apart: 3, of which 0 were waited for; matrix products, arithmetic and copies ran while one was open for 0% of the time, Pallas kernels for 51%

profile of v4, /device:TPU:0, one launch (start us, length us, event | category | flops | bytes accessed | tf_op | source)
XLA Modules:
  0.0 523.4 jit_solution(7940761866403492015)
XLA Ops:
  0.6 0.7 pad_maximum_fusion.2
  1.4 0.1 copy.46
  1.5 1.6 convert.24
  3.1 0.1 slice_bitcast_fusion.2
  3.2 0.2 copy-done.2
  3.3 0.1 convert.25
  3.5 0.1 slice_bitcast_fusion.1
  3.5 1.2 copy-done.3
  4.7 0.1 convert.26
  4.9 0.1 slice_bitcast_fusion
  4.9 0.3 pad_maximum_fusion
  5.2 0.4 copy.48
  5.6 0.6 pad.4.small_ref
  6.2 66.6 %gather_weights.1 = (bf16[16,48,1664]{2,1,0:T(8,128)(2,1)}, bf16[16,48,3072]{2,1,0:T(8,128)(2,1)}) custom-call(f32[48,384]{1,0:T(8,128)} %wq_ref.1, f32[48,384]{1,0:T(8,128)} %wk_ref.1, f32[48,384]{1,0:T(8,128)} %wv_ref.1, f32[48,384]{1,0:T(8,128)} %wo_ref.1, f32[48,128]{1,0:T(8,128)} %pad.4.small_ref, f32[48,1024]{1,0:T(8,128)} %sg_ref.1, ...), custom_call_target="tpu_custom_call" | custom-call | flops 1000000 | bytes 100000000 | tf_op jit(solution)/shard_map/gather_weights/pallas_call | solution.py:231
  72.8 1.7 broadcast_in_dim.31
  74.4 5.9 %all-to-all-start = ((bf16[16,144,512]{2,1,0:T(8,128)(2,1)}), bf16[16,144,512]{2,1,0:T(8,128)(2,1)}, u32[]{:S(2)}, u32[]{:S(2)}) async-start(bf16[16,144,512]{2,1,0:T(8,128)(2,1)} %bitcast.18), calls=%async_computation | async-start | bytes 4718592 | tf_op jit(solution)/shard_map/all_to_all | solution.py:1415
  81.0 0.4 copy.47
  81.3 124.9 %attn_fwd.1 = (bf16[1024,768]{1,0:T(8,128)(2,1)}, bf16[1024,1152]{1,0:T(8,128)(2,1)}, bf16[1024,384]{1,0:T(8,128)(2,1)}, f32[512,768]{1,0:T(8,128)}, bf16[1024,7...) custom-call(s32[1]{0:T(128)S(6)} %copy.62.len_ref, ...), custom_call_target="tpu_custom_call" | custom-call | flops 20000000000 | bytes 60000000 | tf_op jit(solution)/shard_map/attn_fwd/pallas_call | solution.py:493
  206.2 0.0 all-to-all-done
  206.3 1.6 broadcast_in_dim.29
  207.9 9.6 %all-to-all-start.1 = ((bf16[16,144,512]{2,1,0:T(8,128)(2,1)}), bf16[16,144,512]{2,1,0:T(8,128)(2,1)S(1)}, u32[]{:S(2)}, u32[]{:S(2)}) async-start(bf16[16,144,512]{2,1,0:T(8,128)(2,1)} %bitcast.12), calls=%async_computation.1 | async-start | bytes 4718592 | tf_op jit(solution)/shard_map/all_to_all | solution.py:1415
  217.5 57.0 %expert_first.1 = (f32[8,512,768]{2,1,0:T(8,128)}, f32[8,512,768]{2,1,0:T(8,128)}, f32[8,8,512]{2,1,0:T(8,128)}, bf16[16,3,48,512]{3,2,1,0:T(8,128)(2,1)}, bf16[...) custom-call(bf16[8,2,256,768]{3,2,1,0:T(8,128)(2,1)} %get-tuple-element.63.x_ref, ...), custom_call_target="tpu_custom_call" | custom-call | flops 28991029248 | bytes 40000000 | tf_op jit(solution)/shard_map/expert_first/pallas_call | solution.py:1172
  274.5 0.0 all-to-all-done.1
  274.5 1.4 copy-done.1
  275.9 5.6 %all-to-all-start.2 = ((bf16[16,3,48,512]{3,2,1,0:T(8,128)(2,1)}), bf16[16,3,48,512]{3,2,1,0:T(8,128)(2,1)S(1)}, u32[]{:S(2)}, u32[]{:S(2)}) async-start(bf16[16,3,48,512]{3,2,1,0:T(8,128)(2,1)} %get-tuple-element.87), calls=%async_computation.2 | async-start | bytes 4718592 | tf_op jit(solution)/shard_map/all_to_all | solution.py:1423
  281.5 85.5 %expert_second.1 = (bf16[8,256,768]{2,1,0:T(8,128)(2,1)}, bf16[8,256,768]{2,1,0:T(8,128)(2,1)}, f32[8,8,512]{2,1,0:T(8,128)}, bf16[16,3,48,512]{3,2,1,0:T(8,128)(2,1)}, bf16[4,48,3072]{2,1,0:T(8,128)(2,1)}) custom-call(bf16[8,2,256,768]{3,2,1,0:T(8,128)(2,1)} %get-tuple-element.63.x_ref, bf16[8,2,256,768]{3,2,1,0:T(8,128)(2,1)} %get-tuple-element.64.d_ref, ...), custom_call_target="tpu_custom_call" | custom-call | flops 28991029248 | bytes 40000000 | tf_op jit(solution)/shard_map/expert_second/pallas_call | solution.py:1328
  366.9 0.0 all-to-all-done.2.early_ref
  367.0 1.4 copy-done
  368.4 139.0 %attn_bwd.1 = (bf16[512,768]{1,0:T(8,128)(2,1)}, bf16[512,768]{1,0:T(8,128)(2,1)}, f32[48,384]{1,0:T(8,128)}, f32[48,384]{1,0:T(8,128)}, f32[48,384]{1,0:T(8,128...) custom-call(s32[1]{0:T(128)S(6)} %copy.62.len_ref, ...), custom_call_target="tpu_custom_call" | custom-call | flops 40000000000 | bytes 40000000 | tf_op jit(solution)/shard_map/attn_bwd/pallas_call | solution.py:974
  507.4 1.5 slice_reduce_fusion
  509.0 0.8 slice.41
  509.8 0.7 copy.49
  510.4 2.2 copy.63
  512.6 0.9 copy.64
  513.5 0.0 copy-done.14
  513.5 0.6 copy.65
  514.2 0.6 copy.66
  514.8 0.0 copy-done.12
  514.8 0.6 copy.67
  515.4 0.6 copy.68
  516.1 1.1 copy.69
  517.2 0.8 copy-done.5
  518.1 1.1 copy.70
  519.2 0.8 copy-done.4
  520.0 1.1 copy.71
  521.2 0.7 copy.72
  521.9 0.7 copy.73
  522.5 0.7 copy.74
  (22 shorter events, 0.0 us)
Async XLA Ops:
  1.5 1.9 copy-start.2
  3.3 1.4 copy-start.3
  74.4 131.8 %all-to-all-start = ((bf16[16,144,512]{2,1,0:T(8,128)(2,1)}), bf16[16,144,512]{2,1,0:T(8,128)(2,1)}, u32[]{:S(2)}, u32[]{:S(2)}) async-start(bf16[16,144,512]{2,1,0:T(8,128)(2,1)} %bitcast.18), calls=%async_computation | async-start | bytes 4718592 | tf_op jit(solution)/shard_map/all_to_all | solution.py:1415
  207.9 66.6 %all-to-all-start.1 = ((bf16[16,144,512]{2,1,0:T(8,128)(2,1)}), bf16[16,144,512]{2,1,0:T(8,128)(2,1)S(1)}, u32[]{:S(2)}, u32[]{:S(2)}) async-start(bf16[16,144,512]{2,1,0:T(8,128)(2,1)} %bitcast.12), calls=%async_computation.1 | async-start | bytes 4718592 | tf_op jit(solution)/shard_map/all_to_all | solution.py:1415
  274.5 1.4 copy-start.1
  275.9 91.0 %all-to-all-start.2 = ((bf16[16,3,48,512]{3,2,1,0:T(8,128)(2,1)}), bf16[16,3,48,512]{3,2,1,0:T(8,128)(2,1)S(1)}, u32[]{:S(2)}, u32[]{:S(2)}) async-start(bf16[16,3,48,512]{3,2,1,0:T(8,128)(2,1)} %get-tuple-element.87), calls=%async_computation.2 | async-start | bytes 4718592 | tf_op jit(solution)/shard_map/all_to_all | solution.py:1423
  367.0 1.4 copy-start
  507.4 5.2 copy-start.7
  510.4 3.1 copy-start.14
  510.4 3.7 copy-start.13
  510.4 4.4 copy-start.12
  510.4 5.0 copy-start.11
  510.4 5.6 %copy-start.6 = (f32[48,8,1024]{2,1,0:T(8,128)S(1)}, f32[48,8,1024]{2,1,0:T(8,128)}, u32[]{:S(2)}) copy-start(f32[48,8,1024]{2,1,0:T(8,128)} %get-tuple-element.180) | copy-start | bytes 4718596
  516.1 2.0 copy-start.5
  518.0 2.0 copy-start.4
  520.0 1.2 copy-start.10
  520.0 1.8 copy-start.9
  520.0 2.5 copy-start.8

commit v5 on v4

--- a/solution.py
+++ b/solution.py
@@ -68,6 +68,56 @@
         src_ref=src, dst_ref=dst, send_sem=send, recv_sem=recv,
         device_id=target, device_id_type=pl.DeviceIdType.MESH,
     )
+
+
+class Deal:
+    def __init__(self, source, place, send, recv, local, ranks):
+        self.source, self.place, self.ranks = source, place, ranks
+        self.send, self.recv, self.local = send, recv, local
+        self.me, self.core = lax.axis_index("dp"), lax.axis_index("tensor")
+
+    @staticmethod
+    def semaphores(ranks):
+        dma = pltpu.SemaphoreType.DMA
+        return [dma((ranks,)), dma((ranks,)), dma]
+
+    def own(self):
+        return pltpu.make_async_copy(self.source(self.me), self.place(self.me), self.local)
+
+    order = (12, 1, 8, 2, 13, 4, 9, 3, 14, 5, 10, 6, 15, 7, 11)
+
+    def share(self, offset):
+        rank = flip(self.me, offset)
+        return remote(
+            self.source(rank), self.place(self.me), self.send.at[offset], self.recv.at[offset],
+            device(rank, self.core),
+        )
+
+    def each(self, body):
+        for offset in self.order:
+            body(self.share(offset))
+
+    def start(self, pieces=1):
+        self.own().start()
+        for piece in range(pieces):
+            for offset in self.order:
+                rank = flip(self.me, offset)
+                source, place = self.source(rank), self.place(self.me)
+                rows = source.shape[0] // pieces
+                here = pl.ds(piece * rows, rows)
+                remote(
+                    source.at[here], place.at[here], self.send.at[offset], self.recv.at[offset],
+                    device(rank, self.core),
+                ).start()
+
+    def wait(self):
+        self.own().wait()
+        self.each(lambda copy: copy.wait())
+
+
+def all_and_core(ranks):
+    me, core = lax.axis_index("dp"), lax.axis_index("tensor")
+    return [device(lax.rem(me + k, ranks), core) for k in range(1, ranks)] + [device(me, 1 - core)]
 
 
 class Gather:
@@ -326,10 +376,11 @@
 
 
 def attn_fwd_kernel(
-    len_ref, x_ref, c_ref, routes_ref, w_ref, wo_ref, small_ref, shared_ref, cos_ref, sin_ref,
-    a_ref, qkv_ref, ctx_ref, h_ref, b_ref, d_ref, places_ref, rows_ref, gates_ref, y_ref, dx_ref, dr, xr, gr, og_ref,
+    len_ref, x_ref, c_ref, routes_ref, w_ref, wo_ref, small_ref, cos_ref, sin_ref, shared_ref, own_ref,
+    a_ref, qkv_ref, ctx_ref, h_ref, b_ref, d_ref, places_ref, rows_ref, gates_ref, y_ref, dx_ref, dr, xr, gr, og_ref, early_ref,
     ds, xs, gs, ag, au, ad, shared_w, part, x_in, h_in, b_out, b_in, c_out, c_in,
-    send, recv, core_send, core_recv, local, pair_send, pair_recv, load, *, block,
+    send, recv, core_send, core_recv, local, pair_send, pair_recv, load, *sems,
+    block, ranks, deals,
 ):
     step = pl.program_id(0)
     me, core = lax.axis_index("dp"), lax.axis_index("tensor")
@@ -339,6 +390,11 @@
         Trip(ins, outs, send, recv, core_send, core_recv, local, index)
         for index, (ins, outs) in enumerate(((ds, dr), (xs, xr), (gs, gr)))
     ]
+    if deals:
+        deal = Deal(
+            lambda rank: own_ref.at[lax.rem(rank, experts)], lambda rank: early_ref.at[rank],
+            *sems, ranks,
+        )
     slot = core * slots + lax.broadcasted_iota(jnp.int32, (slots, a_ref.shape[0]), 0)
     slot = slot.astype(F32)
     mine = lax.rem(me, experts)
@@ -354,7 +410,9 @@
 
     @pl.when(step == 0)
     def _():
-        greet(cluster_and_core(experts))
+        greet(all_and_core(ranks) if deals else cluster_and_core(experts))
+        if deals:
+            deal.start(3)
         pltpu.make_async_copy(shared_ref, shared_w, load).start()
         token = core * half + lax.broadcasted_iota(jnp.int32, c_ref.shape, 0)
         valid = jnp.where(token < length, c_ref[...].astype(F32), 0.0).astype(BF16)
@@ -453,8 +511,6 @@
         for total in (ag, au, ad):
             total[...] = jnp.zeros_like(total)
         pltpu.make_async_copy(shared_ref, shared_w, load).wait()
-        for k in offsets(experts):
-            trips[0].pass_on(k)
         hidden = ag.shape[1]
 
         def matrix(index):
@@ -476,22 +532,27 @@
             )
         write = pltpu.make_async_copy(shared_w, og_ref, load)
         write.start()
-        for k in offsets(experts):
-            trips[1].pass_on(k)
-            trips[2].pass_on(k)
+        for trip in trips:
+            for k in offsets(experts):
+                trip.pass_on(k)
         for trip in trips:
             trip.end()
         write.wait()
-
-
-def attn_forward(length, rows, cotangent, routes, first_all, shared_all, cosine, sine, experts, slots):
+        if deals:
+            deal.wait()
+
+
+def attn_forward(length, rows, cotangent, routes, first_all, shared_all, own, cosine, sine, slots):
     half, width = rows.shape
     span = 2 * half
     pairs = (first_all.shape[1] - LANES) // (4 * LANES)
     far = pl.BlockSpec(memory_space=pl.ANY)
+    ranks = lax.axis_size("dp")
+    experts, own_rows, part = own.shape
+    deals = ranks == 16
     hidden = shared_all.shape[-1] // 3
     return pl.pallas_call(
-        functools.partial(attn_fwd_kernel, block=256),
+        functools.partial(attn_fwd_kernel, block=256, ranks=ranks, deals=deals),
         grid=(pairs,),
         in_specs=[
             pl.BlockSpec(memory_space=pltpu.SMEM),
@@ -501,10 +562,10 @@
             pl.BlockSpec((width, 3 * LANES), lambda i: (0, i)),
             pl.BlockSpec((width, LANES), lambda i: (0, 3 * pairs + i)),
             pl.BlockSpec((width, LANES), lambda i: (0, 4 * pairs)),
-            far,
             whole((span, LANES)),
             whole((span, LANES)),
-        ],
+        ]
+        + [far] * 2,
         out_specs=[
             whole((span, width)),
             pl.BlockSpec((span, 3 * LANES), lambda i: (0, i)),
@@ -518,7 +579,7 @@
             whole((span, width)),
             whole((span, width)),
         ]
-        + [far] * 4,
+        + [far] * 5,
         out_shape=[
             jax.ShapeDtypeStruct((span, width), BF16),
             jax.ShapeDtypeStruct((span, pairs * 3 * LANES), BF16),
@@ -535,6 +596,7 @@
             jax.ShapeDtypeStruct((experts, 2, slots, width), BF16),
             jax.ShapeDtypeStruct((experts, 2, 8, slots), F32),
             jax.ShapeDtypeStruct(shared_all.shape, BF16),
+            jax.ShapeDtypeStruct((ranks, own_rows, part) if deals else (1, 16, LANES), BF16),
         ],
         scratch_shapes=[
             pltpu.VMEM((experts, slots, width), BF16),
@@ -552,11 +614,12 @@
         + [pltpu.SemaphoreType.DMA((3, experts))] * 4
         + [pltpu.SemaphoreType.DMA((3,))]
         + [pltpu.SemaphoreType.DMA((4,))] * 2
-        + [pltpu.SemaphoreType.DMA],
+        + [pltpu.SemaphoreType.DMA]
+        + Deal.semaphores(ranks),
         compiler_params=remote_params(4),
         cost_estimate=cost(20e9, 60e6, 6e6),
         name="attn_fwd",
-    )(length, rows, cotangent, routes, first_all, first_all, first_all, shared_all, cosine, sine)
+    )(length, rows, cotangent, routes, first_all, first_all, first_all, cosine, sine, shared_all, own)
 
 
 def norm_back(grad, values, gain):
@@ -578,19 +641,18 @@
 
 def attn_bwd_kernel(
     len_ref, places_ref, gates_ref, rows_ref, dx_ref, dg_ref, base_ref, b_ref, h_ref, d_ref,
-    x_ref, a_ref, w_ref, wo_ref, qkv_ref, ctx_ref, cos_ref, sin_ref, sy_ref, y_ref, share_ref, late_ref, early_ref,
+    x_ref, a_ref, w_ref, wo_ref, qkv_ref, ctx_ref, cos_ref, sin_ref, sy_ref, y_ref, share_ref, late_ref,
     gi_ref, lo_ref, *rest, block, ranks, halves, sends,
 ):
     if sends:
-        go_refs, gx_refs, gsh_refs, gs_ref = rest[:4], rest[4:7], rest[7:10], rest[10]
-        sum_x, sum_y, in_x, in_y, sums, in_z, total_ref, late_in, early_in, small_in = rest[11:21]
-        step_send, step_recv = rest[21:23]
-        rest = rest[23:]
+        go_ref, late_in, total_ref, small_in = rest[:4]
+        sum_x, sum_y, in_x, in_y, sums, in_z, step_send, step_recv = rest[4:12]
+        rest = rest[12:]
     else:
         gw_ref, gs_ref = rest[:2]
         rest = rest[2:]
     (
-        db_s, dl_s, db_out, db_in, dh_s, grad_s, da_s, sums_s, sums_in, turned_s,
+        db_s, dl_s, db_out, y_out, db_in, dh_s, grad_s, da_s, sums_s, sums_in, turned_s,
         yh_s, gw_s, dctx_s, dq_s, dk_s, dv_s, send, recv, local, pair_send, pair_recv,
         y_send, y_recv, y_local, z_send, z_recv,
     ) = rest
@@ -610,48 +672,16 @@
     def to_other(src, dst, index):
         return remote(src, dst, pair_send.at[index], pair_recv.at[index], other)
 
-    small, late = 0, 1
-
-    def part_of(index, rank):
-        rows = pl.ds(pl.multiple_of(rank * shard, shard), shard)
-        return late_ref.at[rank] if index == late else turned_s.at[rows]
-
-    def place_of(index, rank):
-        return late_in.at[rank] if index == late else small_in.at[rank]
-
-    def share(index, offset):
-        rank = lax.rem(me + offset, ranks)
-        return remote(
-            part_of(index, rank), place_of(index, me), send.at[index, offset],
-            recv.at[index, offset], device(rank, core),
-        )
-
-    def own_share(index):
-        return pltpu.make_async_copy(part_of(index, me), place_of(index, me), local.at[index])
-
-    def give(index):
-        own_share(index).start()
-
-        def one(offset, carry):
-            share(index, offset).start()
-            return carry
-
-        lax.fori_loop(1, ranks, one, 0)
-
-    def take(index):
-        own_share(index).wait()
-
-        def done(offset, carry):
-            share(index, offset).wait()
-            return carry
-
-        lax.fori_loop(1, ranks, done, 0)
-
-    def all_ranks(ref, *index):
-        total = ref[(0,) + index].astype(F32)
-        for rank in range(1, ref.shape[0]):
-            total += ref[(rank,) + index].astype(F32)
-        return total
+    if sends:
+        rows_at = lambda rank: pl.ds(pl.multiple_of(rank * shard, shard), shard)
+        small = Deal(
+            lambda rank: turned_s.at[rows_at(rank)], lambda rank: small_in.at[rank],
+            send.at[0], recv.at[0], local.at[0], ranks,
+        )
+        late = Deal(
+            lambda rank: late_ref.at[rank], lambda rank: late_in.at[rank],
+            send.at[1], recv.at[1], local.at[1], ranks,
+        )
 
     x, y, x_rank, y_rank = sides(me)
     z = lax.div(me, 4)
@@ -716,18 +746,7 @@
         total = sums[pair, pl.ds(z, 1)].reshape(shard, 2 * cut).astype(F32)
         for offset in range(3):
             total += in_z[pair, offset].astype(F32)
-        for kind in range(4):
-            go_refs[kind][:, pair * LANES : (pair + 1) * LANES] = total[
-                :, kind * LANES : (kind + 1) * LANES
-            ]
-
-    def put_experts(ref, columns):
-        for kind in range(3):
-            for expert in range(experts):
-                total = ref[expert, kind].astype(F32)
-                for cluster in range(1, ranks // experts):
-                    total += ref[cluster * experts + expert, kind].astype(F32)
-                gx_refs[kind][:, expert, columns] = total
+        go_ref[pair] = total
 
     def y_copy(k):
         return remote(
@@ -765,12 +784,10 @@
             copy.start()
         for k in range(1, experts):
             y_copy(k).start()
-        if halves:
+        if sends:
             for k in range(1, 4):
                 z_copy(k).start()
-        if sends:
-            give(late)
-            pltpu.make_async_copy(early_ref, early_in, y_local.at[2]).start()
+            late.start(3)
         router = rows_ref[2 : 2 + experts, :]
         tokens = 256
 
@@ -873,6 +890,27 @@
         db_out[...] = da_s[away, :].astype(BF16)
         swap_d = to_other(db_out, db_in.at[0], 2)
         swap_d.start()
+
+        for copy in own_rows():
+            copy.wait()
+        for k in range(1, experts):
+            y_copy(k).wait()
+        mine = lax.rem(me, experts)
+
+        def near(rows):
+            table = [places_ref[pl.ds(flip(mine, k), 1), rows] for k in range(experts)]
+            return jnp.concatenate(table, axis=0).T
+
+        def add(index, carry):
+            here, _, total = put_together(near, yh_s, index, 256)
+            db_s[here, :] = total + sy_ref[here, :].astype(F32)
+            return carry
+
+        lax.fori_loop(0, span // 256, add, 0)
+        y_out[...] = db_s[away, :].astype(BF16)
+        swap_y = to_other(y_out, db_in.at[2], 4)
+        swap_y.start()
+
         swap_d.wait()
         da = da_s[own, :] + db_in[0].astype(F32)
         back, sums_s[0:1, :] = norm_back(da, x_ref[...].astype(F32), rows_ref[0:1, :])
@@ -887,51 +925,24 @@
         if sends:
             turned_s[...] = jnp.zeros_like(turned_s)
             turned_s[:, : turned.shape[1]] = turned
-            give(small)
-            pltpu.make_async_copy(early_ref, early_in, y_local.at[2]).wait()
+            small.start()
             go_along(pairs - 1)
-            put_experts(early_in, pl.ds(0, early_in.shape[-1]))
-        for copy in own_rows():
-            copy.wait()
-        for k in range(1, experts):
-            y_copy(k).wait()
-        mine = lax.rem(me, experts)
-
-        def near(rows):
-            table = [places_ref[pl.ds(flip(mine, k), 1), rows] for k in range(experts)]
-            return jnp.concatenate(table, axis=0).T
-
-        def add(index, carry):
-            here, _, total = put_together(near, yh_s, index, 256)
-            db_s[here, :] = total + sy_ref[here, :].astype(F32)
-            return carry
-
-        lax.fori_loop(0, span // 256, add, 0)
-        db_out[...] = db_s[away, :].astype(BF16)
-        swap_y = to_other(db_out, db_in.at[1], 4)
-        swap_y.start()
+        else:
+            gs_ref[:, : turned.shape[1]] = turned
         swap_y.wait()
-        out = db_s[own, :] + db_in[1].astype(F32)
+        out = db_s[own, :] + db_in[2].astype(F32)
         lo_ref[...] = (h_ref[...] + out).astype(BF16)
         if sends:
-            take(late)
-            put_experts(late_in, pl.ds(early_in.shape[-1], late_in.shape[-1]))
+            late.wait()
             for k in range(1, 4):
                 z_copy(k).wait()
-            total = all_ranks(total_ref)
-            hidden = total.shape[1] // 3
-            for kind in range(3):
-                gsh_refs[kind][...] = total[:, kind * hidden : (kind + 1) * hidden]
             for pair in range(pairs):
                 end_sum(pair)
-            take(small)
-            gs_ref[...] = all_ranks(small_in)
-        else:
-            gs_ref[:, : turned.shape[1]] = turned
+            small.wait()
 
 
 def attn_backward(
-    length, places, gates, rows, dx_home, gate_grads, y_near, shared_y, shares, late, early,
+    length, places, gates, rows, dx_home, gate_grads, y_near, shared_y, shares, late,
     shared_dx, ffn_in, hidden_rows, grad_ffn, layer_rows, attn_in, first_all, qkv_rot, context,
     cosine, sine, ranks, halves,
 ):
@@ -943,14 +954,12 @@
     sends = halves
     far = pl.BlockSpec(memory_space=pl.ANY)
     if sends:
-        hidden = shares.shape[-1] // 3
-        forms = (
-            [(shard, pairs * LANES)] * 4
-            + [(shard, experts, hidden)] * 3
-            + [(shard, hidden)] * 3
-            + [(shard, LANES)]
-        )
-        outs = [(form, F32) for form in forms]
+        outs = [
+            (whole((pairs, shard, 4 * LANES)), (pairs, shard, 4 * LANES), F32),
+            (far, late.shape, BF16),
+            (far, shares.shape, BF16),
+            (far, (ranks, shard, LANES), F32),
+        ]
         extra = [
             pltpu.VMEM((pairs, 4, 2, shard, 2 * LANES), BF16),
             pltpu.VMEM((pairs, 4, 2, shard, 2 * LANES), BF16),
@@ -958,19 +967,16 @@
             pltpu.VMEM((pairs, 4, shard, 2 * LANES), BF16),
             pltpu.VMEM((pairs, 4, shard, 4 * LANES), BF16),
             pltpu.VMEM((pairs, 3, shard, 4 * LANES), BF16),
-            pltpu.VMEM(shares.shape, BF16),
-            pltpu.VMEM(late.shape, BF16),
-            pltpu.VMEM(early.shape, BF16),
-            pltpu.VMEM((ranks, shard, LANES), F32),
             pltpu.SemaphoreType.DMA((7, pairs)),
             pltpu.SemaphoreType.DMA((7, pairs)),
         ]
         blocks = (4, 2, 2, shard)
     else:
-        outs = [((pairs, width, 4 * LANES), BF16), ((width, LANES), F32)]
+        forms = (pairs, width, 4 * LANES), (width, LANES)
+        outs = [(whole(forms[0]), forms[0], BF16), (whole(forms[1]), forms[1], F32)]
         extra = []
         blocks = (width,)
-    outs = [((half, width), BF16)] * 2 + outs
+    outs = [(whole((half, width)), (half, width), BF16)] * 2 + outs
     return pl.pallas_call(
         functools.partial(attn_bwd_kernel, block=256, ranks=ranks, halves=halves, sends=sends),
         grid=(pairs,),
@@ -991,15 +997,16 @@
             whole((span, LANES)),
             whole((span, width)),
         ]
-        + [far] * 4,
-        out_specs=[whole(form) for form, _ in outs],
-        out_shape=[jax.ShapeDtypeStruct(form, kind) for form, kind in outs],
+        + [far] * 3,
+        out_specs=[spec for spec, _, _ in outs],
+        out_shape=[jax.ShapeDtypeStruct(form, kind) for _, form, kind in outs],
         scratch_shapes=extra
         + [
             pltpu.VMEM((span, width), F32),
             pltpu.VMEM((span, experts), F32),
             pltpu.VMEM((half, width), BF16),
-            pltpu.VMEM((2, half, width), BF16),
+            pltpu.VMEM((half, width), BF16),
+            pltpu.VMEM((3, half, width), BF16),
             pltpu.VMEM((half, width), F32),
             pltpu.VMEM((span, width), BF16),
             pltpu.VMEM((span, width), F32),
@@ -1029,8 +1036,63 @@
     )(
         length, places, gates, rows, dx_home, gate_grads, shared_dx, ffn_in, hidden_rows, grad_ffn,
         layer_rows, attn_in, first_all, first_all, qkv_rot, context, cosine, sine, shared_y,
-        y_near, shares, late, early,
-    )
+        y_near, shares, late,
+    )
+
+
+def finish_kernel(
+    gi_in, lo_in, proj_ref, early_ref, late_ref, total_ref, small_ref, gi_ref, lo_ref, *refs
+):
+    gi_ref[...] = gi_in[...]
+    lo_ref[...] = lo_in[...]
+    for pair in range(proj_ref.shape[0]):
+        for kind in range(4):
+            refs[kind][:, pair * LANES : (pair + 1) * LANES] = proj_ref[
+                pair, :, kind * LANES : (kind + 1) * LANES
+            ]
+    experts = refs[4].shape[1]
+    part = early_ref.shape[-1]
+    for kind in range(3):
+        for index, ref in enumerate((early_ref, late_ref)):
+            for expert in range(experts):
+                total = ref[expert, kind].astype(F32)
+                for rank in range(expert + experts, ref.shape[0], experts):
+                    total += ref[rank, kind].astype(F32)
+                refs[4 + kind][:, expert, index * part : (index + 1) * part] = total
+    hidden = total_ref.shape[-1] // 3
+    for kind in range(3):
+        columns = slice(kind * hidden, (kind + 1) * hidden)
+        total = total_ref[0, :, columns].astype(F32)
+        for place in range(1, total_ref.shape[0]):
+            total += total_ref[place, :, columns].astype(F32)
+        refs[7 + kind][...] = total
+    total = small_ref[0]
+    for rank in range(1, small_ref.shape[0]):
+        total += small_ref[rank]
+    refs[10][...] = total
+
+
+def finish(rows, outputs, proj, early, late, total, small, experts):
+    pairs, shard, _ = proj.shape
+    hidden = total.shape[-1] // 3
+    forms = (
+        [(rows.shape, BF16)] * 2
+        + [((shard, pairs * LANES), F32)] * 4
+        + [((shard, experts, hidden), F32)] * 3
+        + [((shard, hidden), F32)] * 3
+        + [((shard, LANES), F32)]
+    )
+    args = (rows, outputs, proj, early, late, total, small)
+    return pl.pallas_call(
+        finish_kernel,
+        grid=(1,),
+        in_specs=[whole(v.shape) for v in args],
+        out_specs=[whole(form) for form, _ in forms],
+        out_shape=[jax.ShapeDtypeStruct(form, kind) for form, kind in forms],
+        compiler_params=params(1),
+        cost_estimate=cost(1e7, 2e7),
+        name="finish",
+    )(*args)
 
 
 def column_of(row):
@@ -1091,9 +1153,10 @@
 
 
 def expert_first_kernel(
-    x_ref, d_ref, g_ref, wg_ref, wu_ref, wd_ref, share_ref,
-    y_ref, dx_ref, dg_ref, og_ref, sx_ref, sy_ref,
-    ag, au, ad, own_x, own_y, in_x, in_y, send, recv, local, *, halves,
+    x_ref, d_ref, g_ref, wg_ref, wu_ref, wd_ref, share_ref, late_ref,
+    y_ref, dx_ref, dg_ref, og_ref, sx_ref, sy_ref, late_out,
+    ag, au, ad, own_x, own_y, in_x, in_y, send, recv, local, *sems,
+    experts, ranks, halves,
 ):
     step = pl.program_id(0)
     sums = (ag, au, ad)
@@ -1108,6 +1171,10 @@
     def over_y(place):
         return share_ref.at[:, place, :, :, high]
 
+    deal = Deal(
+        lambda rank: late_ref.at[lax.rem(rank, experts)], lambda rank: late_out.at[rank], *sems, ranks
+    )
+
     def copies():
         return (
             remote(over_x(1 - x), in_x, send.at[0], recv.at[0], device(x_rank, core)),
@@ -1125,9 +1192,10 @@
         for total in sums:
             total[...] = jnp.zeros_like(total)
         if halves:
-            greet([device(x_rank, core), device(y_rank, core)])
+            greet(all_and_core(ranks))
             for copy in copies() + loads():
                 copy.start()
+            deal.start(3)
 
     out, row_grad, gate_grad = block_of(x_ref, d_ref, g_ref, (wg_ref, wu_ref, wd_ref), sums)
     y_ref[...] = out
@@ -1142,6 +1210,7 @@
                 copy.wait()
             sx_ref[...] = (own_x[...].astype(F32) + in_x[...].astype(F32)).astype(BF16)
             sy_ref[...] = (own_y[...].astype(F32) + in_y[...].astype(F32)).astype(BF16)
+            deal.wait()
 
 
 def expert_specs(experts, slots, width, weights, order):
@@ -1159,9 +1228,10 @@
     return group, matrices, [pltpu.VMEM((width, hidden), F32)] * 3
 
 
-def expert_first(x_slots, d_slots, g_slots, weights, shares, halves):
+def expert_first(x_slots, d_slots, g_slots, weights, shares, late, halves):
     experts, _, slots, width = x_slots.shape
     hidden = weights.shape[-1]
+    ranks = lax.axis_size("dp")
     group, matrices, sums = expert_specs(experts, slots, width, weights, lambda i: i)
     rows = group((2, slots, width))
     if halves:
@@ -1170,27 +1240,30 @@
     else:
         part = (1, 1, 16, LANES)
     return pl.pallas_call(
-        functools.partial(expert_first_kernel, halves=halves),
+        functools.partial(expert_first_kernel, experts=experts, ranks=ranks, halves=halves),
         grid=(experts,),
         in_specs=[rows, rows, group((2, 8, slots))]
         + matrices
+        + [pl.BlockSpec(memory_space=pl.ANY)] * 2,
+        out_specs=[group((2 * slots, width))] * 2
+        + [group((8, 2 * slots)), whole(weights.shape), whole(part), whole(part)]
         + [pl.BlockSpec(memory_space=pl.ANY)],
-        out_specs=[group((2 * slots, width))] * 2
-        + [group((8, 2 * slots)), whole(weights.shape), whole(part), whole(part)],
         out_shape=[jax.ShapeDtypeStruct((experts, 2 * slots, width), F32)] * 2
         + [
             jax.ShapeDtypeStruct((experts, 8, 2 * slots), F32),
             jax.ShapeDtypeStruct(weights.shape, BF16),
             jax.ShapeDtypeStruct(part, BF16),
             jax.ShapeDtypeStruct(part, BF16),
+            jax.ShapeDtypeStruct((ranks,) + late.shape[1:] if halves else (1, 16, LANES), BF16),
         ],
         scratch_shapes=sums
         + [pltpu.VMEM(part, BF16)] * 4
-        + [pltpu.SemaphoreType.DMA((2,))] * 3,
+        + [pltpu.SemaphoreType.DMA((2,))] * 3
+        + Deal.semaphores(ranks),
         compiler_params=remote_params(6) if halves else params(1),
         cost_estimate=cost(36 * experts * slots * width * hidden, 40e6),
         name="expert_first",
-    )(x_slots, d_slots, g_slots, weights, weights, weights, shares)
+    )(x_slots, d_slots, g_slots, weights, weights, weights, shares, late)
 
 
 def expert_second_kernel(
@@ -1393,6 +1466,8 @@
         (w_query, w_key, w_value, w_output), small_own, (shared_gate, shared_up, shared_down)
     )
     first_all = first_all.reshape(width, first_all.shape[-1])
+    if shard % 16:
+        shared_all = shared_all.reshape(1, width, shared_all.shape[-1])
 
     half = HD // 2
     inverse = np.exp(np.arange(half, dtype=np.float32) * np.float32(-math.log(10000.0) / half))
@@ -1404,18 +1479,22 @@
     direct = shard % 16 == 0
     halves = ranks == 16
 
-    def to_experts(columns, *earlier):
+    def by_expert(columns):
         stack = jnp.stack(
             [w[:, :, columns] for w in (expert_gate, expert_up, expert_down)], axis=0
         ).astype(BF16)
-        part = stack.shape[-1]
-        stack = stack.transpose(2, 0, 1, 3).reshape(1, experts, 3 * shard, part)
-        stack = jnp.broadcast_to(stack, (ranks // experts, experts, 3 * shard, part))
-        stack = after(stack.reshape(ranks, 3 * shard, part), *earlier)
-        gathered = lax.all_to_all(stack, "dp", 0, 0, tiled=True).reshape(ranks, 3, shard, part)
-        if not direct:
-            gathered = gathered.transpose(1, 0, 2, 3).reshape(1, 3, width, part)
-        return gathered
+        return stack.transpose(2, 0, 1, 3).reshape(experts, 3 * shard, stack.shape[-1])
+
+    def to_experts(own):
+        part = own.shape[-1]
+        copies = jnp.broadcast_to(own[None], (ranks // experts,) + own.shape)
+        return lax.all_to_all(copies.reshape(ranks, 3 * shard, part), "dp", 0, 0, tiled=True)
+
+    def matrices(gathered):
+        gathered = gathered.reshape(ranks, 3, shard, gathered.shape[-1])
+        if direct:
+            return gathered
+        return gathered.transpose(1, 0, 2, 3).reshape(1, 3, width, gathered.shape[-1])
 
     def from_experts(grads):
         if not direct:
@@ -1426,17 +1505,18 @@
         grads = grads.reshape(ranks // experts, experts, 3, shard, grads.shape[-1])
         return jnp.sum(grads.astype(F32), axis=0)
 
-    early = to_experts(slice(0, hidden // 2), first_all)
+    early_own = by_expert(slice(0, hidden // 2))
+    late_own = by_expert(slice(hidden // 2, hidden))
 
     (
         attn_in, qkv_rot, context, hidden_rows, ffn_in, grad_ffn, places, small, gates, shared_y,
-        shared_dx, d_slots, x_slots, g_slots, shared_grads,
+        shared_dx, d_slots, x_slots, g_slots, shared_grads, early,
     ) = attn_forward(
         seq_lengths, layer_input[0], out_cotangent[0], expert_routes.reshape(span, 2).T,
-        first_all, shared_all if direct else shared_all.reshape(1, width, 3 * hidden), cosine, sine,
-        experts, slots,
-    )
-    late = to_experts(slice(hidden // 2, hidden), early, places)
+        first_all, shared_all, early_own, cosine, sine, slots,
+    )
+    if not halves:
+        early = to_experts(early_own)
 
     if halves:
         shares = shared_grads.reshape(4, 2, 2, shard, 3 * hidden)
@@ -1446,20 +1526,27 @@
             shared_grads.reshape(ranks, shard, 3 * hidden), "dp", 0, 0, tiled=True
         )
 
-    y_first, dx_first, dg_first, early_grads, sx, sy = expert_first(
-        x_slots, d_slots, g_slots, early, shares, halves
-    )
+    y_first, dx_first, dg_first, early_grads, sx, sy, late = expert_first(
+        x_slots, d_slots, g_slots, matrices(early), shares, late_own, halves
+    )
+    if not halves:
+        late = to_experts(late_own)
     early_grads = from_experts(early_grads)
     y_near, dx_home, gate_grads, late_grads, shares = expert_second(
-        x_slots, d_slots, g_slots, late, (y_first, dx_first, dg_first, sx, sy), halves
-    )
+        x_slots, d_slots, g_slots, matrices(late), (y_first, dx_first, dg_first, sx, sy), halves
+    )
+    late_grads = after(late_grads, early_grads)
 
     grad_input, layer_output, *grads = attn_backward(
         seq_lengths, places, gates, small, dx_home, gate_grads, y_near, shared_y, shares,
-        late_grads, early_grads, shared_dx, ffn_in, hidden_rows, grad_ffn, layer_input[0], attn_in,
+        late_grads, shared_dx, ffn_in, hidden_rows, grad_ffn, layer_input[0], attn_in,
         first_all, qkv_rot, context, cosine, sine, ranks, halves,
     )
     if halves:
+        proj, late_in, total, small_in = grads
+        grad_input, layer_output, *grads = finish(
+            grad_input, layer_output, proj, early_grads, late_in, total, small_in, experts
+        )
         attn_grads, expert_grads, shared_grads, small_grads = (
             grads[:4], grads[4:7], grads[7:10], grads[10]
         )

time: 532 us -> 517 us (0.972); the launches traced: 523 us -> 514 us
  Pallas kernels: 473 us -> 498 us
  starting transfers between devices: 21 us -> 4.04 us
  local copies, waits for them, and re-layouts: 24.9 us -> 8 us
    pallas_call x2 -> x3, Pallas kernels: 182 us -> 208 us  [the longest x1 138 us: attn_forward(): pl.pallas_call(functools.partial(attn_fwd_kernel, block=256, ranks=ranks,...]
    unnamed x43 -> x7, local copies, waits for them, and re-layouts: 17.6 us -> 2.06 us
    all_to_all x2 -> x0, starting transfers between devices: 15.4 us -> none  [to_experts(): lax.all_to_all(stack, 'dp', 0, 0, tiled=True).reshape(ranks, 3, shard, part)]
  transfers between devices with their start and end apart: 3 -> 1, of which waited for: 0 -> 0; matrix products, arithmetic and copies ran while one was open for 0% -> 0% of each run, Pallas kernels for 51% -> 17%
where the time goes in v5:
time: 517 us; the launch traced here: 514 us
  Pallas kernels  498 us (96%)
  local copies, waits for them, and re-layouts  8 us (2%)
    pallas_call x1, Pallas kernels, attn_forward(): pl.pallas_call(functools.partial(attn_fwd_kernel, block=256, ranks=ranks,...  138 us
    pallas_call x1, Pallas kernels, attn_backward(): pl.pallas_call(functools.partial(attn_bwd_kernel, block=256, ranks=ranks,...  137 us
    pallas_call x1, Pallas kernels, expert_second(): pl.pallas_call(functools.partial(expert_second_kernel, experts=experts, h...  85.5 us
    pallas_call x1, Pallas kernels, gather_weights(): pl.pallas_call(gather_kernel, in_specs=[vmem] * 8, out_specs=[pl.BlockSpe...  66.6 us
    pallas_call x1, Pallas kernels, expert_first(): pl.pallas_call(functools.partial(expert_first_kernel, experts=experts, ra...  63.9 us
  transfers between devices with their start and end apart: 1, of which 0 were waited for; matrix products, arithmetic and copies ran while one was open for 0% of the time, Pallas kernels for 17%

profile of v5, /device:TPU:0, one launch (start us, length us, event | category | flops | bytes accessed | tf_op | source)
XLA Modules:
  0.0 514.4 jit_solution(12781759806619843013)
XLA Ops:
  1.3 0.7 pad_maximum_fusion
  2.0 0.1 copy.46
  2.1 0.0 copy-start.1
  2.1 1.6 convert.24
  3.7 0.1 slice_bitcast_fusion.2
  3.8 0.2 copy-done.1
  4.0 0.0 copy-start.2
  4.0 0.1 convert.25
  4.1 0.1 slice_bitcast_fusion.1
  4.2 1.2 copy-done.2
  5.4 0.1 convert.26
  5.5 0.1 slice_bitcast_fusion
  5.6 0.3 maximum_bitcast_fusion
  5.8 1.4 copy.47
  7.2 1.4 copy.48
  8.6 0.6 pad.4.small_ref
  9.2 66.6 %gather_weights.1 = (bf16[16,48,1664]{2,1,0:T(8,128)(2,1)}, bf16[16,48,3072]{2,1,0:T(8,128)(2,1)}) custom-call(f32[48,384]{1,0:T(8,128)} %wq_ref.1, f32[48,384]{1,0:T(8,128)} %wk_ref.1, f32[48,384]{1,0:T(8,128)} %wv_ref.1, f32[48,384]{1,0:T(8,128)} %wo_ref.1, f32[48,128]{1,0:T(8,128)} %pad.4.small_ref, f32[48,1024]{1,0:T(8,128)} %sg_ref.1, ...), custom_call_target="tpu_custom_call" | custom-call | flops 1000000 | bytes 100000000 | tf_op jit(solution)/shard_map/gather_weights/pallas_call | solution.py:281
  75.8 138.1 %attn_fwd.1 = (bf16[1024,768]{1,0:T(8,128)(2,1)}, bf16[1024,1152]{1,0:T(8,128)(2,1)}, bf16[1024,384]{1,0:T(8,128)(2,1)}, f32[512,768]{1,0:T(8,128)}, bf16[1024,7...) custom-call(s32[1]{0:T(128)S(6)} %copy.50.len_ref, ...), custom_call_target="tpu_custom_call" | custom-call | flops 20000000000 | bytes 60000000 | tf_op jit(solution)/shard_map/attn_fwd/pallas_call | solution.py:554
  213.9 63.9 %expert_first.1 = (f32[8,512,768]{2,1,0:T(8,128)}, f32[8,512,768]{2,1,0:T(8,128)}, f32[8,8,512]{2,1,0:T(8,128)}, bf16[16,3,48,512]{3,2,1,0:T(8,128)(2,1)}, bf16[...) custom-call(bf16[8,2,256,768]{3,2,1,0:T(8,128)(2,1)} %get-tuple-element.70.x_ref, ...), custom_call_target="tpu_custom_call" | custom-call | flops 28991029248 | bytes 40000000 | tf_op jit(solution)/shard_map/expert_first/pallas_call | solution.py:1242
  277.8 4.0 all-to-all-start
  281.8 85.5 %expert_second.1 = (bf16[8,256,768]{2,1,0:T(8,128)(2,1)}, bf16[8,256,768]{2,1,0:T(8,128)(2,1)}, f32[8,8,512]{2,1,0:T(8,128)}, bf16[16,3,48,512]{3,2,1,0:T(8,128)(2,1)}, bf16[4,48,3072]{2,1,0:T(8,128)(2,1)}) custom-call(bf16[8,2,256,768]{3,2,1,0:T(8,128)(2,1)} %get-tuple-element.70.x_ref, bf16[8,2,256,768]{3,2,1,0:T(8,128)(2,1)} %get-tuple-element.71.d_ref, ...), custom_call_target="tpu_custom_call" | custom-call | flops 28991029248 | bytes 40000000 | tf_op jit(solution)/shard_map/expert_second/pallas_call | solution.py:1401
  367.3 0.0 all-to-all-done.early_ref
  367.3 0.0 copy-start
  367.4 137.3 %attn_bwd.1 = (bf16[512,768]{1,0:T(8,128)(2,1)}, bf16[512,768]{1,0:T(8,128)(2,1)}, f32[3,48,512]{2,1,0:T(8,128)}, bf16[16,3,48,512]{3,2,1,0:T(8,128)(2,1)}, bf16...) custom-call(s32[1]{0:T(128)S(6)} %copy.50.len_ref, f32[8,1024]{1,0:T(8,128)} %get-tuple-element.67.places_ref, ...), custom_call_target="tpu_custom_call" | custom-call | flops 40000000000 | bytes 40000000 | tf_op jit(solution)/shard_map/attn_bwd/pallas_call | solution.py:980
  504.7 0.0 copy-done
  504.7 6.5 %finish.1 = (bf16[512,768]{1,0:T(8,128)(2,1)}, bf16[512,768]{1,0:T(8,128)(2,1)}, f32[48,384]{1,0:T(8,128)}, f32[48,384]{1,0:T(8,128)}, f32[48,384]{1,0:T(8,128)}...) custom-call(bf16[512,768]{1,0:T(8,128)(2,1)} %get-tuple-element.96.g, ...), custom_call_target="tpu_custom_call" | custom-call | flops 10000000 | bytes 20000000 | tf_op jit(solution)/shard_map/finish/pallas_call | solution.py:1086
  511.2 1.5 slice_reduce_fusion
  512.7 0.8 slice.41
  513.5 0.7 copy.49
Async XLA Ops:
  2.1 1.9 copy-start.1
  4.0 1.4 copy-start.2
  277.8 89.6 %all-to-all-start = ((bf16[16,3,48,512]{3,2,1,0:T(8,128)(2,1)}), bf16[16,3,48,512]{3,2,1,0:T(8,128)(2,1)S(1)}, u32[]{:S(2)}, u32[]{:S(2)}) async-start(bf16[16,3,48,512]{3,2,1,0:T(8,128)(2,1)} %get-tuple-element.94), calls=%async_computation | async-start | bytes 4718592 | tf_op jit(solution)/shard_map/all_to_all | solution.py:1502
  367.3 137.3 %copy-start = (bf16[16,3,48,512]{3,2,1,0:T(8,128)(2,1)}, bf16[16,3,48,512]{3,2,1,0:T(8,128)(2,1)S(1)}, u32[]{:S(2)}) copy-start(bf16[16,3,48,512]{3,2,1,0:T(8,128)(2,1)S(1)} %all-to-all-done.early_ref) | copy-start | bytes 7077892

commit v6 on v5

--- a/solution.py
+++ b/solution.py
@@ -228,9 +228,16 @@
 
 
 def gather_kernel(
-    wq_ref, wk_ref, wv_ref, wo_ref, small_ref, sg_ref, su_ref, sd_ref, first_out, shared_out,
-    first_s, shared_s, *sems,
+    wq_ref, wk_ref, wv_ref, wo_ref, small_ref, sg_ref, su_ref, sd_ref, eg_ref, eu_ref, ed_ref,
+    first_out, shared_out, early_out, late_out,
+    first_s, shared_s, raw_s, packed_s, load, store, *sems,
 ):
+    loads = [
+        pltpu.make_async_copy(ref, raw_s.at[kind], load.at[kind])
+        for kind, ref in enumerate((eg_ref, eu_ref, ed_ref))
+    ]
+    for copy in loads:
+        copy.start()
     pairs = wq_ref.shape[1] // LANES
     for pair in range(pairs):
         columns = slice(pair * LANES, (pair + 1) * LANES)
@@ -259,14 +266,35 @@
     pl.semaphore_wait(barrier, 2 + lax.min(z, 1) + lax.min(3 - z, 1))
     for gather in gathers:
         gather.begin()
+    _, rows, experts, _ = raw_s.shape
+    part = packed_s.shape[-1]
+    for copy in loads:
+        copy.wait()
     for turn in range(1, Gather.turns):
         for gather in gathers:
             gather.turn(turn)
+        for expert in range(turn - 1, experts, Gather.turns - 1):
+            for kind in range(3):
+                for half in range(2):
+                    packed_s[half, expert, kind * rows : (kind + 1) * rows, :] = raw_s[
+                        kind, :, expert, half * part : (half + 1) * part
+                    ].astype(BF16)
+    count = early_out.shape[0] // experts
+    stores = [
+        pltpu.make_async_copy(
+            packed_s.at[0], early_out.at[pl.ds(index * experts, experts)], store.at[index]
+        )
+        for index in range(count)
+    ] + [pltpu.make_async_copy(packed_s.at[1], late_out, store.at[count])]
+    for copy in stores:
+        copy.start()
+    for copy in stores:
+        copy.wait()
     for gather in gathers:
         gather.end()
 
 
-def gather_weights(attention, small, shared):
+def gather_weights(attention, small, shared, expert):
     ranks = lax.axis_size("dp")
     rows, heads_width = attention[0].shape
     columns = 4 * heads_width + LANES
@@ -276,19 +304,33 @@
         qkv = jnp.stack(attention[:3], axis=1).reshape(rows, 3, pairs, LANES)
         qkv = qkv.transpose(0, 2, 1, 3).reshape(rows, 3 * heads_width)
         first = jnp.concatenate([qkv, attention[3], small], axis=1).astype(BF16)
-        return to_all(first), to_all(jnp.concatenate(shared, axis=1).astype(BF16))
+        stack = jnp.stack(expert, axis=0).astype(BF16).transpose(2, 0, 1, 3)
+        stack = stack.reshape(stack.shape[0], 3 * rows, hidden)
+        early, late = stack[:, :, : hidden // 2], stack[:, :, hidden // 2 :]
+        early = jnp.concatenate([early] * (ranks // early.shape[0]), axis=0)
+        return (
+            to_all(first), to_all(jnp.concatenate(shared, axis=1).astype(BF16)), early, late
+        )
     vmem = pl.BlockSpec(memory_space=pltpu.VMEM)
+    far = pl.BlockSpec(memory_space=pl.ANY)
+    experts = expert[0].shape[1]
     return pl.pallas_call(
         gather_kernel,
-        in_specs=[vmem] * 8,
-        out_specs=[pl.BlockSpec(memory_space=pl.ANY)] * 2,
+        in_specs=[vmem] * 8 + [far] * 3,
+        out_specs=[far] * 4,
         out_shape=[
             jax.ShapeDtypeStruct((ranks, rows, columns), BF16),
             jax.ShapeDtypeStruct((ranks, rows, 3 * hidden), BF16),
+            jax.ShapeDtypeStruct((ranks, 3 * rows, hidden // 2), BF16),
+            jax.ShapeDtypeStruct((experts, 3 * rows, hidden // 2), BF16),
         ],
         scratch_shapes=[
             pltpu.VMEM((rows, columns), BF16),
             pltpu.VMEM((rows, 3 * hidden), BF16),
+            pltpu.VMEM((3, rows, experts, hidden), F32),
+            pltpu.VMEM((2, experts, 3 * rows, hidden // 2), BF16),
+            pltpu.SemaphoreType.DMA((3,)),
+            pltpu.SemaphoreType.DMA((ranks // experts + 1,)),
         ]
         + Gather.semaphores(2),
         compiler_params=pltpu.CompilerParams(
@@ -296,7 +338,7 @@
         ),
         cost_estimate=cost(1e6, 100e6),
         name="gather_weights",
-    )(*attention, small, *shared)
+    )(*attention, small, *shared, *expert)
 
 
 def partner(values):
@@ -376,11 +418,10 @@
 
 
 def attn_fwd_kernel(
-    len_ref, x_ref, c_ref, routes_ref, w_ref, wo_ref, small_ref, cos_ref, sin_ref, shared_ref, own_ref,
-    a_ref, qkv_ref, ctx_ref, h_ref, b_ref, d_ref, places_ref, rows_ref, gates_ref, y_ref, dx_ref, dr, xr, gr, og_ref, early_ref,
+    len_ref, x_ref, c_ref, routes_ref, w_ref, wo_ref, small_ref, cos_ref, sin_ref, shared_ref,
+    a_ref, qkv_ref, ctx_ref, h_ref, b_ref, d_ref, places_ref, rows_ref, gates_ref, y_ref, dx_ref, dr, xr, gr, og_ref,
     ds, xs, gs, ag, au, ad, shared_w, part, x_in, h_in, b_out, b_in, c_out, c_in,
-    send, recv, core_send, core_recv, local, pair_send, pair_recv, load, *sems,
-    block, ranks, deals,
+    send, recv, core_send, core_recv, local, pair_send, pair_recv, load, *, block,
 ):
     step = pl.program_id(0)
     me, core = lax.axis_index("dp"), lax.axis_index("tensor")
@@ -390,11 +431,6 @@
         Trip(ins, outs, send, recv, core_send, core_recv, local, index)
         for index, (ins, outs) in enumerate(((ds, dr), (xs, xr), (gs, gr)))
     ]
-    if deals:
-        deal = Deal(
-            lambda rank: own_ref.at[lax.rem(rank, experts)], lambda rank: early_ref.at[rank],
-            *sems, ranks,
-        )
     slot = core * slots + lax.broadcasted_iota(jnp.int32, (slots, a_ref.shape[0]), 0)
     slot = slot.astype(F32)
     mine = lax.rem(me, experts)
@@ -410,9 +446,7 @@
 
     @pl.when(step == 0)
     def _():
-        greet(all_and_core(ranks) if deals else cluster_and_core(experts))
-        if deals:
-            deal.start(3)
+        greet(cluster_and_core(experts))
         pltpu.make_async_copy(shared_ref, shared_w, load).start()
         token = core * half + lax.broadcasted_iota(jnp.int32, c_ref.shape, 0)
         valid = jnp.where(token < length, c_ref[...].astype(F32), 0.0).astype(BF16)
@@ -538,21 +572,16 @@
         for trip in trips:
             trip.end()
         write.wait()
-        if deals:
-            deal.wait()
-
-
-def attn_forward(length, rows, cotangent, routes, first_all, shared_all, own, cosine, sine, slots):
+
+
+def attn_forward(length, rows, cotangent, routes, first_all, shared_all, cosine, sine, experts, slots):
     half, width = rows.shape
     span = 2 * half
     pairs = (first_all.shape[1] - LANES) // (4 * LANES)
     far = pl.BlockSpec(memory_space=pl.ANY)
-    ranks = lax.axis_size("dp")
-    experts, own_rows, part = own.shape
-    deals = ranks == 16
     hidden = shared_all.shape[-1] // 3
     return pl.pallas_call(
-        functools.partial(attn_fwd_kernel, block=256, ranks=ranks, deals=deals),
+        functools.partial(attn_fwd_kernel, block=256),
         grid=(pairs,),
         in_specs=[
             pl.BlockSpec(memory_space=pltpu.SMEM),
@@ -565,7 +594,7 @@
             whole((span, LANES)),
             whole((span, LANES)),
         ]
-        + [far] * 2,
+        + [far],
         out_specs=[
             whole((span, width)),
             pl.BlockSpec((span, 3 * LANES), lambda i: (0, i)),
@@ -579,7 +608,7 @@
             whole((span, width)),
             whole((span, width)),
         ]
-        + [far] * 5,
+        + [far] * 4,
         out_shape=[
             jax.ShapeDtypeStruct((span, width), BF16),
             jax.ShapeDtypeStruct((span, pairs * 3 * LANES), BF16),
@@ -596,7 +625,6 @@
             jax.ShapeDtypeStruct((experts, 2, slots, width), BF16),
             jax.ShapeDtypeStruct((experts, 2, 8, slots), F32),
             jax.ShapeDtypeStruct(shared_all.shape, BF16),
-            jax.ShapeDtypeStruct((ranks, own_rows, part) if deals else (1, 16, LANES), BF16),
         ],
         scratch_shapes=[
             pltpu.VMEM((experts, slots, width), BF16),
@@ -614,12 +642,11 @@
         + [pltpu.SemaphoreType.DMA((3, experts))] * 4
         + [pltpu.SemaphoreType.DMA((3,))]
         + [pltpu.SemaphoreType.DMA((4,))] * 2
-        + [pltpu.SemaphoreType.DMA]
-        + Deal.semaphores(ranks),
+        + [pltpu.SemaphoreType.DMA],
         compiler_params=remote_params(4),
         cost_estimate=cost(20e9, 60e6, 6e6),
         name="attn_fwd",
-    )(length, rows, cotangent, routes, first_all, first_all, first_all, cosine, sine, shared_all, own)
+    )(length, rows, cotangent, routes, first_all, first_all, first_all, cosine, sine, shared_all)
 
 
 def norm_back(grad, values, gain):
@@ -1462,8 +1489,9 @@
         [gain_attn[:, None], gain_ffn[:, None], router_weight], axis=1
     )
     small_own = jnp.pad(small_own, ((0, 0), (0, LANES - small_own.shape[1])))
-    first_all, shared_all = gather_weights(
-        (w_query, w_key, w_value, w_output), small_own, (shared_gate, shared_up, shared_down)
+    first_all, shared_all, early_own, late_own = gather_weights(
+        (w_query, w_key, w_value, w_output), small_own, (shared_gate, shared_up, shared_down),
+        (expert_gate, expert_up, expert_down),
     )
     first_all = first_all.reshape(width, first_all.shape[-1])
     if shard % 16:
@@ -1479,17 +1507,6 @@
     direct = shard % 16 == 0
     halves = ranks == 16
 
-    def by_expert(columns):
-        stack = jnp.stack(
-            [w[:, :, columns] for w in (expert_gate, expert_up, expert_down)], axis=0
-        ).astype(BF16)
-        return stack.transpose(2, 0, 1, 3).reshape(experts, 3 * shard, stack.shape[-1])
-
-    def to_experts(own):
-        part = own.shape[-1]
-        copies = jnp.broadcast_to(own[None], (ranks // experts,) + own.shape)
-        return lax.all_to_all(copies.reshape(ranks, 3 * shard, part), "dp", 0, 0, tiled=True)
-
     def matrices(gathered):
         gathered = gathered.reshape(ranks, 3, shard, gathered.shape[-1])
         if direct:
@@ -1505,18 +1522,14 @@
         grads = grads.reshape(ranks // experts, experts, 3, shard, grads.shape[-1])
         return jnp.sum(grads.astype(F32), axis=0)
 
-    early_own = by_expert(slice(0, hidden // 2))
-    late_own = by_expert(slice(hidden // 2, hidden))
-
+    early = lax.all_to_all(early_own, "dp", 0, 0, tiled=True)
     (
         attn_in, qkv_rot, context, hidden_rows, ffn_in, grad_ffn, places, small, gates, shared_y,
-        shared_dx, d_slots, x_slots, g_slots, shared_grads, early,
+        shared_dx, d_slots, x_slots, g_slots, shared_grads,
     ) = attn_forward(
         seq_lengths, layer_input[0], out_cotangent[0], expert_routes.reshape(span, 2).T,
-        first_all, shared_all, early_own, cosine, sine, slots,
-    )
-    if not halves:
-        early = to_experts(early_own)
+        first_all, shared_all, cosine, sine, experts, slots,
+    )
 
     if halves:
         shares = shared_grads.reshape(4, 2, 2, shard, 3 * hidden)
@@ -1530,7 +1543,8 @@
         x_slots, d_slots, g_slots, matrices(early), shares, late_own, halves
     )
     if not halves:
-        late = to_experts(late_own)
+        late = jnp.concatenate([late_own] * (ranks // experts), axis=0)
+        late = lax.all_to_all(late, "dp", 0, 0, tiled=True)
     early_grads = from_experts(early_grads)
     y_near, dx_home, gate_grads, late_grads, shares = expert_second(
         x_slots, d_slots, g_slots, matrices(late), (y_first, dx_first, dg_first, sx, sy), halves

time: 517 us -> 508 us (0.983)
  Pallas kernels: 498 us -> 485 us
  starting transfers between devices: 4.04 us -> 10 us
    pallas_call x2, Pallas kernels: 205 us -> 192 us  [the longest x1 125 us: attn_forward(): pl.pallas_call(functools.partial(attn_fwd_kernel, block=256), grid=(pairs...]
    all_to_all x0 -> x1, starting transfers between devices: none -> 5.83 us  [per_device(): early = lax.all_to_all(early_own, 'dp', 0, 0, tiled=True)]
  transfers between devices with their start and end apart: 1 -> 2, of which waited for: 0 -> 0; matrix products, arithmetic and copies ran while one was open for 0% -> 0% of each run, Pallas kernels for 17% -> 42%
where the time goes in v6:
time: 508 us; the launch traced here: 502 us
  Pallas kernels  485 us (95%)
  starting transfers between devices  10 us (2%)
  local copies, waits for them, and re-layouts  5.09 us (1%)
    pallas_call x1, Pallas kernels, attn_backward(): pl.pallas_call(functools.partial(attn_bwd_kernel, block=256, ranks=ranks,...  137 us
    pallas_call x1, Pallas kernels, attn_forward(): pl.pallas_call(functools.partial(attn_fwd_kernel, block=256), grid=(pairs...  125 us
    pallas_call x1, Pallas kernels, expert_second(): pl.pallas_call(functools.partial(expert_second_kernel, experts=experts, h...  85.4 us
    pallas_call x1, Pallas kernels, gather_weights(): pl.pallas_call(gather_kernel, in_specs=[vmem] * 8 + [far] * 3, out_specs=...  66.6 us
    pallas_call x1, Pallas kernels, expert_first(): pl.pallas_call(functools.partial(expert_first_kernel, experts=experts, ra...  64.1 us
  transfers between devices with their start and end apart: 2, of which 0 were waited for; matrix products, arithmetic and copies ran while one was open for 0% of the time, Pallas kernels for 42%

profile of v6, /device:TPU:0, one launch (start us, length us, event | category | flops | bytes accessed | tf_op | source)
XLA Modules:
  0.0 502.4 jit_solution(153449954167548966)
XLA Ops:
  0.6 0.7 pad_maximum_fusion
  1.4 0.1 copy.42
  1.5 0.6 pad.4.small_ref
  2.1 66.6 %gather_weights.1 = (bf16[16,48,1664]{2,1,0:T(8,128)(2,1)}, bf16[16,48,3072]{2,1,0:T(8,128)(2,1)}, bf16[16,144,512]{2,1,0:T(8,128)(2,1)}, bf16[8,144,512]{2,1,0:T(8,128)(2,1)}) custom-call(f32[48,384]{1,0:T(8,128)} %wq_ref.1, f32[48,384]{1,0:T(8,128)} %wk_ref.1, f32[48,384]{1,0:T(8,128)} %wv_ref.1, f32[48,384]{1,0:T(8,128)} %wo_ref.1, ...), custom_call_target="tpu_custom_call" | custom-call | flops 1000000 | bytes 100000000 | tf_op jit(solution)/shard_map/gather_weights/pallas_call | solution.py:317
  68.7 5.8 %all-to-all-start = ((bf16[16,144,512]{2,1,0:T(8,128)(2,1)}), bf16[16,144,512]{2,1,0:T(8,128)(2,1)S(1)}, u32[]{:S(2)}, u32[]{:S(2)}) async-start(bf16[16,144,512]{2,1,0:T(8,128)(2,1)} %get-tuple-element.74), calls=%async_computation | async-start | bytes 4718592 | tf_op jit(solution)/shard_map/all_to_all | solution.py:1525
  75.2 124.9 %attn_fwd.1 = (bf16[1024,768]{1,0:T(8,128)(2,1)}, bf16[1024,1152]{1,0:T(8,128)(2,1)}, bf16[1024,384]{1,0:T(8,128)(2,1)}, f32[512,768]{1,0:T(8,128)}, bf16[1024,7...) custom-call(s32[1]{0:T(128)S(6)} %copy.44.len_ref, ...), custom_call_target="tpu_custom_call" | custom-call | flops 20000000000 | bytes 60000000 | tf_op jit(solution)/shard_map/attn_fwd/pallas_call | solution.py:583
  200.1 0.0 all-to-all-done
  200.1 0.0 copy-start.1
  200.1 1.4 copy-done.1
  201.5 64.1 %expert_first.1 = (f32[8,512,768]{2,1,0:T(8,128)}, f32[8,512,768]{2,1,0:T(8,128)}, f32[8,8,512]{2,1,0:T(8,128)}, bf16[16,3,48,512]{3,2,1,0:T(8,128)(2,1)}, bf16[...) custom-call(bf16[8,2,256,768]{3,2,1,0:T(8,128)(2,1)} %get-tuple-element.71.x_ref, ...), custom_call_target="tpu_custom_call" | custom-call | flops 28991029248 | bytes 40000000 | tf_op jit(solution)/shard_map/expert_first/pallas_call | solution.py:1269
  265.6 4.2 all-to-all-start.1
  269.8 85.4 %expert_second.1 = (bf16[8,256,768]{2,1,0:T(8,128)(2,1)}, bf16[8,256,768]{2,1,0:T(8,128)(2,1)}, f32[8,8,512]{2,1,0:T(8,128)}, bf16[16,3,48,512]{3,2,1,0:T(8,128)(2,1)}, bf16[4,48,3072]{2,1,0:T(8,128)(2,1)}) custom-call(bf16[8,2,256,768]{3,2,1,0:T(8,128)(2,1)} %get-tuple-element.71.x_ref, bf16[8,2,256,768]{3,2,1,0:T(8,128)(2,1)} %get-tuple-element.72.d_ref, ...), custom_call_target="tpu_custom_call" | custom-call | flops 28991029248 | bytes 40000000 | tf_op jit(solution)/shard_map/expert_second/pallas_call | solution.py:1428
  355.2 0.0 all-to-all-done.1.early_ref
  355.3 0.0 copy-start
  355.3 137.3 %attn_bwd.1 = (bf16[512,768]{1,0:T(8,128)(2,1)}, bf16[512,768]{1,0:T(8,128)(2,1)}, f32[3,48,512]{2,1,0:T(8,128)}, bf16[16,3,48,512]{3,2,1,0:T(8,128)(2,1)}, bf16...) custom-call(s32[1]{0:T(128)S(6)} %copy.44.len_ref, f32[8,1024]{1,0:T(8,128)} %get-tuple-element.68.places_ref, ...), custom_call_target="tpu_custom_call" | custom-call | flops 40000000000 | bytes 40000000 | tf_op jit(solution)/shard_map/attn_bwd/pallas_call | solution.py:1007
  492.6 0.0 copy-done
  492.6 6.5 %finish.1 = (bf16[512,768]{1,0:T(8,128)(2,1)}, bf16[512,768]{1,0:T(8,128)(2,1)}, f32[48,384]{1,0:T(8,128)}, f32[48,384]{1,0:T(8,128)}, f32[48,384]{1,0:T(8,128)}...) custom-call(bf16[512,768]{1,0:T(8,128)(2,1)} %get-tuple-element.98.g, ...), custom_call_target="tpu_custom_call" | custom-call | flops 10000000 | bytes 20000000 | tf_op jit(solution)/shard_map/finish/pallas_call | solution.py:1113
  499.1 1.5 slice_reduce_fusion
  500.6 0.8 slice.11
  501.4 0.7 copy.43
Async XLA Ops:
  68.7 131.4 %all-to-all-start = ((bf16[16,144,512]{2,1,0:T(8,128)(2,1)}), bf16[16,144,512]{2,1,0:T(8,128)(2,1)S(1)}, u32[]{:S(2)}, u32[]{:S(2)}) async-start(bf16[16,144,512]{2,1,0:T(8,128)(2,1)} %get-tuple-element.74), calls=%async_computation | async-start | bytes 4718592 | tf_op jit(solution)/shard_map/all_to_all | solution.py:1525
  200.1 1.4 copy-start.1
  265.6 89.6 %all-to-all-start.1 = ((bf16[16,3,48,512]{3,2,1,0:T(8,128)(2,1)}), bf16[16,3,48,512]{3,2,1,0:T(8,128)(2,1)S(1)}, u32[]{:S(2)}, u32[]{:S(2)}) async-start(bf16[16,3,48,512]{3,2,1,0:T(8,128)(2,1)} %get-tuple-element.96), calls=%async_computation.1 | async-start | bytes 4718592 | tf_op jit(solution)/shard_map/all_to_all | solution.py:1519
  355.3 137.3 %copy-start = (bf16[16,3,48,512]{3,2,1,0:T(8,128)(2,1)}, bf16[16,3,48,512]{3,2,1,0:T(8,128)(2,1)S(1)}, u32[]{:S(2)}) copy-start(bf16[16,3,48,512]{3,2,1,0:T(8,128)(2,1)S(1)} %all-to-all-done.1.early_ref) | copy-start | bytes 7077892

commit v7 on v6

--- a/solution.py
+++ b/solution.py
@@ -668,13 +668,13 @@
 
 def attn_bwd_kernel(
     len_ref, places_ref, gates_ref, rows_ref, dx_ref, dg_ref, base_ref, b_ref, h_ref, d_ref,
-    x_ref, a_ref, w_ref, wo_ref, qkv_ref, ctx_ref, cos_ref, sin_ref, sy_ref, y_ref, share_ref, late_ref,
+    x_ref, a_ref, w_ref, wo_ref, qkv_ref, ctx_ref, cos_ref, sin_ref, sy_ref, y_ref, share_ref,
     gi_ref, lo_ref, *rest, block, ranks, halves, sends,
 ):
     if sends:
-        go_ref, late_in, total_ref, small_in = rest[:4]
-        sum_x, sum_y, in_x, in_y, sums, in_z, step_send, step_recv = rest[4:12]
-        rest = rest[12:]
+        go_ref, total_ref, small_in = rest[:3]
+        sum_x, sum_y, in_x, in_y, sums, in_z, step_send, step_recv = rest[3:11]
+        rest = rest[11:]
     else:
         gw_ref, gs_ref = rest[:2]
         rest = rest[2:]
@@ -705,10 +705,6 @@
             lambda rank: turned_s.at[rows_at(rank)], lambda rank: small_in.at[rank],
             send.at[0], recv.at[0], local.at[0], ranks,
         )
-        late = Deal(
-            lambda rank: late_ref.at[rank], lambda rank: late_in.at[rank],
-            send.at[1], recv.at[1], local.at[1], ranks,
-        )
 
     x, y, x_rank, y_rank = sides(me)
     z = lax.div(me, 4)
@@ -814,7 +810,6 @@
         if sends:
             for k in range(1, 4):
                 z_copy(k).start()
-            late.start(3)
         router = rows_ref[2 : 2 + experts, :]
         tokens = 256
 
@@ -960,7 +955,6 @@
         out = db_s[own, :] + db_in[2].astype(F32)
         lo_ref[...] = (h_ref[...] + out).astype(BF16)
         if sends:
-            late.wait()
             for k in range(1, 4):
                 z_copy(k).wait()
             for pair in range(pairs):
@@ -969,7 +963,7 @@
 
 
 def attn_backward(
-    length, places, gates, rows, dx_home, gate_grads, y_near, shared_y, shares, late,
+    length, places, gates, rows, dx_home, gate_grads, y_near, shared_y, shares,
     shared_dx, ffn_in, hidden_rows, grad_ffn, layer_rows, attn_in, first_all, qkv_rot, context,
     cosine, sine, ranks, halves,
 ):
@@ -983,7 +977,6 @@
     if sends:
         outs = [
             (whole((pairs, shard, 4 * LANES)), (pairs, shard, 4 * LANES), F32),
-            (far, late.shape, BF16),
             (far, shares.shape, BF16),
             (far, (ranks, shard, LANES), F32),
         ]
@@ -1024,7 +1017,7 @@
             whole((span, LANES)),
             whole((span, width)),
         ]
-        + [far] * 3,
+        + [far] * 2,
         out_specs=[spec for spec, _, _ in outs],
         out_shape=[jax.ShapeDtypeStruct(form, kind) for _, form, kind in outs],
         scratch_shapes=extra
@@ -1046,9 +1039,9 @@
             pltpu.VMEM((span, LANES), F32),
             pltpu.VMEM((span, LANES), F32),
             pltpu.VMEM((span, LANES), F32),
-            pltpu.SemaphoreType.DMA((2, ranks)),
-            pltpu.SemaphoreType.DMA((2, ranks)),
-            pltpu.SemaphoreType.DMA((2,)),
+            pltpu.SemaphoreType.DMA((1, ranks)),
+            pltpu.SemaphoreType.DMA((1, ranks)),
+            pltpu.SemaphoreType.DMA((1,)),
             pltpu.SemaphoreType.DMA((5,)),
             pltpu.SemaphoreType.DMA((5,)),
             pltpu.SemaphoreType.DMA((experts,)),
@@ -1063,7 +1056,7 @@
     )(
         length, places, gates, rows, dx_home, gate_grads, shared_dx, ffn_in, hidden_rows, grad_ffn,
         layer_rows, attn_in, first_all, first_all, qkv_rot, context, cosine, sine, shared_y,
-        y_near, shares, late,
+        y_near, shares,
     )
 
 
@@ -1549,17 +1542,17 @@
     y_near, dx_home, gate_grads, late_grads, shares = expert_second(
         x_slots, d_slots, g_slots, matrices(late), (y_first, dx_first, dg_first, sx, sy), halves
     )
-    late_grads = after(late_grads, early_grads)
+    late_grads = from_experts(after(late_grads, early_grads))
 
     grad_input, layer_output, *grads = attn_backward(
         seq_lengths, places, gates, small, dx_home, gate_grads, y_near, shared_y, shares,
-        late_grads, shared_dx, ffn_in, hidden_rows, grad_ffn, layer_input[0], attn_in,
+        shared_dx, ffn_in, hidden_rows, grad_ffn, layer_input[0], attn_in,
         first_all, qkv_rot, context, cosine, sine, ranks, halves,
     )
     if halves:
-        proj, late_in, total, small_in = grads
+        proj, total, small_in = grads
         grad_input, layer_output, *grads = finish(
-            grad_input, layer_output, proj, early_grads, late_in, total, small_in, experts
+            grad_input, layer_output, proj, early_grads, late_grads, total, small_in, experts
         )
         attn_grads, expert_grads, shared_grads, small_grads = (
             grads[:4], grads[4:7], grads[7:10], grads[10]
@@ -1575,7 +1568,6 @@
         small_grads = jnp.sum(small_grads, axis=0)
         shared_grads = jnp.sum(shared_grads.astype(F32), axis=0)
         shared_grads = [shared_grads[:, k * hidden : (k + 1) * hidden] for k in range(3)]
-        late_grads = from_experts(late_grads)
         expert_grads = jnp.concatenate([to_outputs(early_grads), to_outputs(late_grads)], axis=-1)
         expert_grads = [expert_grads[:, k].transpose(1, 0, 2) for k in range(3)]
     return (

time: 508 us -> 500 us (0.984)
  Pallas kernels: 485 us -> 464 us
  starting transfers between devices: 10 us -> 20.6 us
    pallas_call x1, Pallas kernels: 137 us -> 117 us  [attn_backward(): pl.pallas_call(functools.partial(attn_bwd_kernel, block=256, ranks=ranks,...]
    all_to_all x1 -> x2, starting transfers between devices: 4.18 us -> 14.8 us  [from_experts(): return lax.all_to_all(grads, 'dp', 0, 0, tiled=True)]
  transfers between devices with their start and end apart: 2 -> 3, of which waited for: 0 -> 0; matrix products, arithmetic and copies ran while one was open for 0% -> 0% of each run, Pallas kernels for 42% -> 66%
where the time goes in v7:
time: 500 us; the launch traced here: 494 us
  Pallas kernels  464 us (93%)
  starting transfers between devices  20.6 us (4%)
  local copies, waits for them, and re-layouts  6.48 us (1%)
    pallas_call x1, Pallas kernels, attn_forward(): pl.pallas_call(functools.partial(attn_fwd_kernel, block=256), grid=(pairs...  125 us
    pallas_call x1, Pallas kernels, attn_backward(): pl.pallas_call(functools.partial(attn_bwd_kernel, block=256, ranks=ranks,...  117 us
    pallas_call x1, Pallas kernels, expert_second(): pl.pallas_call(functools.partial(expert_second_kernel, experts=experts, h...  85.5 us
    pallas_call x1, Pallas kernels, gather_weights(): pl.pallas_call(gather_kernel, in_specs=[vmem] * 8 + [far] * 3, out_specs=...  66.6 us
    pallas_call x1, Pallas kernels, expert_first(): pl.pallas_call(functools.partial(expert_first_kernel, experts=experts, ra...  64.1 us
    all_to_all x2, starting transfers between devices, from_experts(): return lax.all_to_all(grads, 'dp', 0, 0, tiled=True)  14.8 us
  transfers between devices with their start and end apart: 3, of which 0 were waited for; matrix products, arithmetic and copies ran while one was open for 0% of the time, Pallas kernels for 66%

profile of v7, /device:TPU:0, one launch (start us, length us, event | category | flops | bytes accessed | tf_op | source)
XLA Modules:
  0.0 494.0 jit_solution(2614021432791823465)
XLA Ops:
  0.6 0.7 pad_maximum_fusion
  1.4 0.1 copy.42
  1.5 0.6 pad.4.small_ref
  2.1 66.6 %gather_weights.1 = (bf16[16,48,1664]{2,1,0:T(8,128)(2,1)}, bf16[16,48,3072]{2,1,0:T(8,128)(2,1)}, bf16[16,144,512]{2,1,0:T(8,128)(2,1)}, bf16[8,144,512]{2,1,0:T(8,128)(2,1)}) custom-call(f32[48,384]{1,0:T(8,128)} %wq_ref.1, f32[48,384]{1,0:T(8,128)} %wk_ref.1, f32[48,384]{1,0:T(8,128)} %wv_ref.1, f32[48,384]{1,0:T(8,128)} %wo_ref.1, ...), custom_call_target="tpu_custom_call" | custom-call | flops 1000000 | bytes 100000000 | tf_op jit(solution)/shard_map/gather_weights/pallas_call | solution.py:317
  68.7 5.8 %all-to-all-start = ((bf16[16,144,512]{2,1,0:T(8,128)(2,1)}), bf16[16,144,512]{2,1,0:T(8,128)(2,1)S(1)}, u32[]{:S(2)}, u32[]{:S(2)}) async-start(bf16[16,144,512]{2,1,0:T(8,128)(2,1)} %get-tuple-element.73), calls=%async_computation | async-start | bytes 4718592 | tf_op jit(solution)/shard_map/all_to_all | solution.py:1518
  75.2 125.0 %attn_fwd.1 = (bf16[1024,768]{1,0:T(8,128)(2,1)}, bf16[1024,1152]{1,0:T(8,128)(2,1)}, bf16[1024,384]{1,0:T(8,128)(2,1)}, f32[512,768]{1,0:T(8,128)}, bf16[1024,7...) custom-call(s32[1]{0:T(128)S(6)} %copy.44.len_ref, ...), custom_call_target="tpu_custom_call" | custom-call | flops 20000000000 | bytes 60000000 | tf_op jit(solution)/shard_map/attn_fwd/pallas_call | solution.py:583
  200.2 0.0 all-to-all-done
  200.2 0.0 copy-start.1
  200.2 1.4 copy-done.1
  201.6 64.1 %expert_first.1 = (f32[8,512,768]{2,1,0:T(8,128)}, f32[8,512,768]{2,1,0:T(8,128)}, f32[8,8,512]{2,1,0:T(8,128)}, bf16[16,3,48,512]{3,2,1,0:T(8,128)(2,1)}, bf16[...) custom-call(bf16[8,2,256,768]{3,2,1,0:T(8,128)(2,1)} %get-tuple-element.70.x_ref, ...), custom_call_target="tpu_custom_call" | custom-call | flops 28991029248 | bytes 40000000 | tf_op jit(solution)/shard_map/expert_first/pallas_call | solution.py:1262
  265.8 4.2 all-to-all-start.1
  269.9 85.5 %expert_second.1 = (bf16[8,256,768]{2,1,0:T(8,128)(2,1)}, bf16[8,256,768]{2,1,0:T(8,128)(2,1)}, f32[8,8,512]{2,1,0:T(8,128)}, bf16[16,3,48,512]{3,2,1,0:T(8,128)(2,1)}, bf16[4,48,3072]{2,1,0:T(8,128)(2,1)}) custom-call(bf16[8,2,256,768]{3,2,1,0:T(8,128)(2,1)} %get-tuple-element.70.x_ref, bf16[8,2,256,768]{3,2,1,0:T(8,128)(2,1)} %get-tuple-element.71.d_ref, ...), custom_call_target="tpu_custom_call" | custom-call | flops 28991029248 | bytes 40000000 | tf_op jit(solution)/shard_map/expert_second/pallas_call | solution.py:1421
  355.4 0.0 all-to-all-done.1.early_ref
  355.4 0.0 copy-start
  355.4 1.4 copy-done
  356.8 10.6 %all-to-all-start.2 = ((bf16[16,3,48,512]{3,2,1,0:T(8,128)(2,1)}), bf16[16,3,48,512]{3,2,1,0:T(8,128)(2,1)}, u32[]{:S(2)}, u32[]{:S(2)}) async-start(bf16[16,3,48,512]{3,2,1,0:T(8,128)(2,1)} %get-tuple-element.99), calls=%async_computation.2 | async-start | bytes 4718592 | tf_op jit(solution)/shard_map/all_to_all | solution.py:1512
  367.5 116.6 %attn_bwd.1 = (bf16[512,768]{1,0:T(8,128)(2,1)}, bf16[512,768]{1,0:T(8,128)(2,1)}, f32[3,48,512]{2,1,0:T(8,128)}, bf16[4,48,3072]{2,1,0:T(8,128)(2,1)}, f32[16,48,128]{2,1,0:T(8,128)}) custom-call(s32[1]{0:T(128)S(6)} %copy.44.len_ref, f32[8,1024]{1,0:T(8,128)} %get-tuple-element.67.places_ref, f32[8,1024]{1,0:T(8,128)} %get-tuple-element.68.gates_ref, ...), custom_call_target="tpu_custom_call" | custom-call | flops 40000000000 | bytes 40000000 | tf_op jit(solution)/shard_map/attn_bwd/pallas_call | solution.py:1000
  484.1 0.0 all-to-all-done.2.late_ref
  484.1 6.5 %finish.1 = (bf16[512,768]{1,0:T(8,128)(2,1)}, bf16[512,768]{1,0:T(8,128)(2,1)}, f32[48,384]{1,0:T(8,128)}, f32[48,384]{1,0:T(8,128)}, f32[48,384]{1,0:T(8,128)}...) custom-call(bf16[512,768]{1,0:T(8,128)(2,1)} %get-tuple-element.94.g, ...), custom_call_target="tpu_custom_call" | custom-call | flops 10000000 | bytes 20000000 | tf_op jit(solution)/shard_map/finish/pallas_call | solution.py:1106
  490.7 1.5 slice_reduce_fusion
  492.2 0.8 slice.11
  493.0 0.7 copy.43
Async XLA Ops:
  68.7 131.5 %all-to-all-start = ((bf16[16,144,512]{2,1,0:T(8,128)(2,1)}), bf16[16,144,512]{2,1,0:T(8,128)(2,1)S(1)}, u32[]{:S(2)}, u32[]{:S(2)}) async-start(bf16[16,144,512]{2,1,0:T(8,128)(2,1)} %get-tuple-element.73), calls=%async_computation | async-start | bytes 4718592 | tf_op jit(solution)/shard_map/all_to_all | solution.py:1518
  200.2 1.4 copy-start.1
  265.8 89.7 %all-to-all-start.1 = ((bf16[16,3,48,512]{3,2,1,0:T(8,128)(2,1)}), bf16[16,3,48,512]{3,2,1,0:T(8,128)(2,1)S(1)}, u32[]{:S(2)}, u32[]{:S(2)}) async-start(bf16[16,3,48,512]{3,2,1,0:T(8,128)(2,1)} %get-tuple-element.97), calls=%async_computation.1 | async-start | bytes 4718592 | tf_op jit(solution)/shard_map/all_to_all | solution.py:1512
  355.4 1.4 copy-start
  356.8 127.3 %all-to-all-start.2 = ((bf16[16,3,48,512]{3,2,1,0:T(8,128)(2,1)}), bf16[16,3,48,512]{3,2,1,0:T(8,128)(2,1)}, u32[]{:S(2)}, u32[]{:S(2)}) async-start(bf16[16,3,48,512]{3,2,1,0:T(8,128)(2,1)} %get-tuple-element.99), calls=%async_computation.2 | async-start | bytes 4718592 | tf_op jit(solution)/shard_map/all_to_all | solution.py:1512
